TPU v7x, 32 devices: a whole 2x2x4 slice. The times are simulated.
32 devices in a mesh: span: 4 (over y, x), tok: 8 (over z, core).
Axes of the slice: x: 2, y: 2, z: 4, core: 2. Of those that a mesh axis runs over, the one named last changes fastest.
Arguments:
- latents: bfloat16 [4, 512, 3584], P('span', 'tok'), may hold values from -6 to 6
- levels: int32 [4], P('span'), may hold values from 0 to 14
- visible: int32 [4, 4], replicated, may hold values 0 or 1
- frame_counts: int32 [4], replicated, may hold values from 0 to 2
- modulation: float32 [16, 3, 3584], replicated, may hold values from -4 to 4
- w_qkv: bfloat16 [3584, 3, 4096], P(None, None, 'tok')
- qk_gain: float32 [2, 4096], P(None, 'tok'), may hold values from 0 to 5
- w_out: bfloat16 [4096, 3584], P('tok'), may hold values from -0.09375 to 0.09375
- w_head: bfloat16 [3584, 96], replicated, may hold values from -0.09375 to 0.09375
- conv_w: bfloat16 [3, 96, 384], replicated, may hold values from -0.375 to 0.375
Outputs:
- denoised: bfloat16 [4, 512, 3584], P('span', 'tok')
- decoded: bfloat16 [4, 512, 384], P('span', 'tok')
All inputs are finite; a program needn't handle non-finite values.
Results may differ from a plain program's by a relative error of at most 0.015.
Values may be sent and summed in bfloat16 or wider, within the bound.
No kernel may reach another device: no remote copies, remote signals or barrier semaphores. Data moves between devices by JAX's collectives and lax.ppermute only.
A program may use at most 128 MiB of HBM per device.

v0:
```python
import jax
import jax.numpy as jnp
from jax import lax
from jax.sharding import PartitionSpec as P

HD = 128
FRAMES = 8
KEEP = 2
SPOTS = 8
TOK_DEV = 64


EPS = 1e-06
NEG = -1e30


def from_behind(array, axis, by):
    devices = lax.axis_size(axis)
    pairs = [(i, i + by) for i in range(devices) if 0 <= i + by < devices]
    return lax.ppermute(array, axis, pairs)


def modulate(rows, shift, scale):
    values = rows.astype(jnp.float32)
    centre = values - jnp.mean(values, -1, keepdims=True)
    spread = jnp.mean(centre * centre, -1, keepdims=True)
    return (centre * lax.rsqrt(spread + EPS) * (1.0 + scale) + shift).astype(jnp.bfloat16)


def qk_scale(tensor, gain):
    square = jnp.mean(tensor * tensor, -1, keepdims=True)
    return (
        tensor * lax.rsqrt(square + EPS) * gain.reshape(tensor.shape[-2], tensor.shape[-1])
    ).astype(jnp.bfloat16)


def pick_level(table, level):
    matched = jnp.arange(table.shape[0]) == level
    picked = jnp.sum(jnp.where(matched[:, None, None], table, 0.0), 0)
    return (picked[0], picked[1], picked[2])


def lookup_one(table, index):
    matched = jnp.arange(table.shape[0], dtype=jnp.int32) == index
    return jnp.sum(jnp.where(matched, table, 0))


def fold_block(carry, query, block_keys, block_values, allow):
    best, total, acc = carry
    scores = jnp.einsum(
        "qhd,khd->hqk", query, block_keys, preferred_element_type=jnp.float32
    ) * HD ** (-0.5)
    scores = jnp.where(allow[None, None, :], scores, NEG)
    fresh = jnp.maximum(best, jnp.max(scores, -1))
    terms = jnp.where(allow[None, None, :], jnp.exp(scores - fresh[..., None]), 0.0)
    decay = jnp.exp(best - fresh)
    total = total * decay + jnp.sum(terms, -1)
    acc = acc * decay[..., None] + jnp.einsum(
        "hqk,khd->hqd", terms.astype(jnp.bfloat16), block_values, preferred_element_type=jnp.float32
    )
    return (fresh, total, acc)


def attention(proj, qk_gain, clip_id, visible_row, frame_counts):
    rows = proj.shape[0]
    cols = qk_gain.shape[1]
    heads = cols // HD
    tiles = rows // TOK_DEV
    lead = KEEP * SPOTS
    split = proj.reshape(rows, 3, heads, HD)
    query = qk_scale(split[:, 0], qk_gain[0])
    keys = qk_scale(split[:, 1], qk_gain[1])
    values = split[:, 2].astype(jnp.bfloat16)
    start_carry = (
        jnp.full((heads, rows), NEG, jnp.float32),
        jnp.zeros((heads, rows), jnp.float32),
        jnp.zeros((heads, rows, HD), jnp.float32),
    )
    everywhere = jnp.ones((rows,), jnp.bool_)
    own = fold_block(start_carry, query, keys, values, everywhere)
    lead_keys = keys.reshape(tiles, TOK_DEV, cols)[:, :lead].reshape(tiles * lead, cols)
    lead_values = values.reshape(tiles, TOK_DEV, cols)[:, :lead].reshape(tiles * lead, cols)
    packed = jnp.stack([lead_keys, lead_values], 0)[None]
    count = tiles * lead
    frame = jnp.arange(count, dtype=jnp.int32) % lead // SPOTS
    carry = own
    piece = lax.all_gather(packed, "span", axis=0, tiled=True)
    start = jnp.int32(0)
    for index in range(piece.shape[0]):
        source = start + index
        seen = lookup_one(visible_row, source)
        limit = lookup_one(frame_counts, source)
        allow = (frame < limit) & (source < clip_id) & (seen == 1)
        block_keys = piece[index, 0].reshape(count, heads, HD)
        block_values = piece[index, 1].reshape(count, heads, HD)
        carry = fold_block(carry, query, block_keys, block_values, allow)
    best, total, acc = carry
    return (acc / total[..., None]).transpose(1, 0, 2).reshape(rows, cols).astype(jnp.bfloat16)


def head_terms(attended, w_out):
    partial_term = jnp.dot(attended, w_out, preferred_element_type=jnp.float32).astype(jnp.bfloat16)
    return lax.optimization_barrier(partial_term).astype(jnp.float32)


def per_device(
    latents, levels, visible, frame_counts, modulation, w_qkv, qk_gain, w_out, w_head, conv_w
):
    current = latents[0]
    tok_rows = current.shape[0]
    width = current.shape[1]
    clip_id = lax.axis_index("span")
    level = levels[0]
    visible_row = lax.dynamic_index_in_dim(visible, clip_id, 0, keepdims=False)
    w_flat = w_qkv.reshape(width, -1)
    shift, scale, gate = pick_level(modulation, level)
    modulated = modulate(current, shift, scale)
    proj = jnp.dot(
        lax.all_gather(modulated, "tok", axis=0, tiled=True),
        w_flat,
        preferred_element_type=jnp.float32,
    )
    attended = attention(proj, qk_gain, clip_id, visible_row, frame_counts)
    summed = lax.psum_scatter(
        head_terms(attended, w_out).astype(jnp.bfloat16), "tok", scatter_dimension=0, tiled=True
    ).astype(jnp.float32)
    current = (current.astype(jnp.float32) + gate * summed).astype(jnp.bfloat16)
    channels = w_head.shape[1]
    feats = jnp.dot(current, w_head, preferred_element_type=jnp.float32).astype(jnp.bfloat16)
    feats = feats.reshape(FRAMES, tok_rows // FRAMES, channels)
    earlier = from_behind(feats[FRAMES - 2 :], "span", 1)
    sequence = jnp.concatenate([earlier, feats], 0)
    conv = jnp.zeros((tok_rows, conv_w.shape[2]), jnp.float32)
    for tap in range(3):
        window = sequence[2 - tap : 2 - tap + FRAMES].reshape(tok_rows, channels)
        conv = conv + jnp.dot(window, conv_w[tap], preferred_element_type=jnp.float32)
    decoded = jax.nn.silu(conv).astype(jnp.bfloat16)
    return (current[None], decoded[None])


def solution(mesh):
    placed = (
        P("span", "tok", None),
        P("span"),
        P(),
        P(),
        P(),
        P(None, None, "tok"),
        P(None, "tok"),
        P("tok", None),
        P(),
        P(),
    )
    return jax.shard_map(
        per_device,
        mesh=mesh,
        in_specs=placed,
        out_specs=(P("span", "tok", None), P("span", "tok", None)),
        check_vma=False,
    )
```

profile of v0, /device:TPU:4, one launch (start us, length us, event | category | flops | bytes accessed | tf_op | source)
XLA Modules:
  0.0 174.4 jit_solution(17494877010509784933)
XLA Ops:
  7.2 0.0 copy-start
  7.2 0.0 all-gather.4.cloned.1.call-start
  7.9 1.3 select_reduce_fusion
  9.2 0.1 slice_reduce_fusion.1
  9.4 1.2 convert_reduce_fusion
  10.6 1.3 fusion.45
  11.9 2.0 %fusion.48 = bf16[64,3584]{1,0:T(8,128)(2,1)} fusion(bf16[1,64,3584]{2,1,0:T(8,128)(2,1)} %param.10, f32[3584]{0:T(1024)S(1)} %get-tuple-element.5, f32[3584]{0:T(1024)S(1)} %get-tuple-element.6, f32[64]{0:T(128)S(1)} %add_rsqrt_fusion.2, f32[64]{0:T(128)S(1)} %broadcast_multiply_fusion), kind=kLoop, calls=%fused_computation.59 | loop fusion | flops 1376256 | bytes 946688 | tf_op jit(solution)/shard_map/convert_element_type | solution.py:27
  13.9 0.0 all-gather.4.cloned.1.call-update
  13.9 0.0 copy-start.7
  14.0 0.0 all-gather.6.cloned.1.call-start
  14.0 15.1 %copy.50 = bf16[3584,3,512]{0,2,1:T(8,128)(2,1)} copy(bf16[3584,3,512]{2,0,1:T(8,128)(2,1)} %param.15) | data formatting | bytes 22020096 | tf_op args[5]
  29.1 28.8 %all-gather.4.cloned.1.call-done = bf16[512,3584]{1,0:T(8,128)(2,1)} async-done(((bf16[64,3584]{1,0:T(8,128)(2,1)}), bf16[512,3584]{1,0:T(8,128)(2,1)}) %all-gather.4.cloned.1.call-update) | async-done | bytes 3670032 | tf_op jit(solution)/shard_map/all_gather | solution.py:119
  57.9 9.8 %fusion = f32[512,3,4,128]{0,3,2,1:T(8,128)S(1)} fusion(bf16[3,4,128,3584]{3,2,1,0:T(8,128)(2,1)} %bitcast.248, bf16[512,3584]{1,0:T(8,128)(2,1)} %all-gather.4.cloned.1.call-done), kind=kOutput, calls=%fused_computation.3 | convolution fusion | flops 5637144576 | bytes 17825792 | tf_op jit(solution)/shard_map/dot_general | solution.py:118
  67.7 0.1 slice.165
  67.8 0.3 multiply_reduce_fusion.1
  68.0 1.3 copy-done.2
  69.4 0.3 copy.56
  69.7 0.2 convert_element_type.76
  69.9 0.1 copy.86
  70.1 0.6 mul.195.clone
  70.7 0.0 copy-start.8
  70.7 1.4 mul.203
  72.1 0.4 copy.54
  72.5 0.4 squeeze.31
  72.9 1.0 fusion.80
  73.9 0.7 pad_maximum_fusion
  74.7 0.0 all-gather.6.cloned.1.call-update
  74.7 0.2 reduce-scatter.2.cloned.1.call-start
  74.9 1.4 fusion.113
  78.9 0.7 fusion.112
  79.6 1.3 and_and_fusion.2
  80.9 1.3 and_and_fusion
  82.2 1.4 multiply_convert_fusion
  83.6 4.1 %multiply_reduce_fusion = (f32[4,512]{1,0:T(4,128)S(1)}, f32[4,512,512]{1,2,0:T(8,128)}) fusion(bf16[512,4,128]{0,2,1:T(8,128)(2,1)S(1)} %multiply_convert_fusion, f32[4,128]{1,0:T(4,128)S(1)} %bitcast.264, f32[512,4]{0,1:T(4,128)S(1)} %get-tuple-element.46, f32[512,3,4,128]{0,3,2,1:T(8,128)} %copy-done.2), kind=kOutput, calls=%fused_computation.2 | convolution fusion | flops 271316992 | bytes 5785600 | tf_op jit(solution)/shard_map/qhd,khd->hqk/dot_general | solution.py:50
  87.6 12.7 %all-gather.6.cloned.1.call-done = bf16[8,128,512]{2,1,0:T(8,128)(2,1)} async-done(((bf16[2,128,512]{2,1,0:T(8,128)(2,1)}), bf16[8,128,512]{2,1,0:T(8,128)(2,1)}) %all-gather.6.cloned.1.call-update) | async-done | bytes 1048592 | tf_op jit(solution)/shard_map/all_gather | solution.py:87
  100.3 1.6 copy.57
  101.9 0.1 fusion.126
  102.0 0.4 fusion.130
  102.4 0.4 fusion.128
  102.8 0.4 fusion.129
  103.1 0.4 fusion.131
  103.5 0.2 fusion.52
  103.8 0.4 convolution_bitcast_fusion.2
  104.1 0.2 fusion.50
  104.4 0.4 convolution_bitcast_fusion.3
  104.7 0.2 fusion.56
  105.0 0.2 fusion.54
  105.2 0.5 copy-done.1
  105.7 0.7 fusion.2
  106.5 0.4 copy-done.3
  106.9 1.0 fusion.26
  107.9 0.4 fusion.32
  108.3 0.4 fusion.37
  108.7 1.3 copy-done.5
  110.0 3.9 %convolution_convert_fusion = bf16[512,3584]{1,0:T(8,128)(2,1)} fusion(bf16[512,512]{0,1:T(8,128)(2,1)S(1)} %bitcast.259, bf16[512,3584]{1,0:T(8,128)(2,1)S(1)} %copy-done.5), kind=kOutput, calls=%fused_computation | convolution fusion | flops 1880883200 | bytes 7864320 | tf_op jit(solution)/shard_map/dot_general | solution.py:102
  113.9 0.0 reduce-scatter.2.cloned.1.call-update
  113.9 45.2 %reduce-scatter.2.cloned.1.call-done = bf16[64,3584]{1,0:T(8,128)(2,1)} async-done(((bf16[512,3584]{1,0:T(8,128)(2,1)}), bf16[64,3584]{1,0:T(8,128)(2,1)}) %reduce-scatter.2.cloned.1.call-update) | async-done | bytes 458768 | tf_op jit(solution)/shard_map/reduce_scatter | solution.py:124
  159.1 1.4 convolution_convert_fusion.1
  160.5 3.4 %collective-permute-start = (bf16[2,8,96]{2,1,0:T(8,128)(2,1)S(1)}, bf16[2,8,96]{2,1,0:T(8,128)(2,1)S(1)}, u32[]{:S(2)}, u32[]{:S(2)}) collective-permute-start(bf16[2,8,96]{2,1,0:T(8,128)(2,1)S(1)} %slice_bitcast_fusion.1), channel_id=1, source_target_pairs={{0,8},{8,16},{16,24},{1,9},{9,17},{17,25},{2,10},{10,18},{18,26},{... | collective-permute-start | bytes 9224 | tf_op jit(solution)/shard_map/ppermute | solution.py:20
  163.9 1.9 %fusion.82 = bf16[1,64,3584]{2,1,0:T(8,128)(2,1)} fusion(bf16[64,3584]{1,0:T(8,128)(2,1)} %reduce-scatter.2.cloned.1.call-done, f32[3584]{0:T(1024)S(1)} %get-tuple-element.4, bf16[1,64,3584]{2,1,0:T(8,128)(2,1)S(1)} %copy-done.4), kind=kLoop, calls=%fused_computation.90 | loop fusion | flops 1146880 | bytes 1390592 | tf_op jit(solution)/shard_map/broadcast_in_dim | solution.py:138
  165.8 0.1 fusion.86
  166.0 0.9 collective-permute-done
  166.9 0.1 convolution_add_fusion.1
  167.1 0.8 fusion.83
  (22 shorter events, 0.1 us)
Async XLA Ops:
  7.2 152.0 %copy-start = (bf16[3584,96]{0,1:T(8,128)(2,1)S(1)}, bf16[3584,96]{0,1:T(8,128)(2,1)}, u32[]{:S(2)}) copy-start(bf16[3584,96]{0,1:T(8,128)(2,1)} %param.18) | copy-start | bytes 2064388
  7.2 50.7 %all-gather.4.cloned.1.call-start = ((), (), s32[]{:S(2)}) async-start(), calls=%async_computation.1 | async-start | bytes 4128768 | tf_op jit(solution)/shard_map/all_gather | solution.py:119
  13.9 15.1 %copy-start.7 = (f32[2,512]{1,0:T(2,128)S(1)}, f32[2,512]{1,0:T(2,128)}, u32[]{:S(2)}) copy-start(f32[2,512]{1,0:T(2,128)} %param.16) | copy-start | bytes 12292
  14.0 86.4 %all-gather.6.cloned.1.call-start = ((), (), s32[]{:S(2)}) async-start(), calls=%async_computation.3 | async-start | bytes 1310720 | tf_op jit(solution)/shard_map/all_gather | solution.py:87
  67.7 1.7 copy-start.2
  69.4 2.7 %slice-start = ((f32[512,3,4,128]{0,3,2,1:T(8,128)}), f32[512,1,4,128]{0,3,2,1:T(8,128)S(1)}, s32[]{:S(2)}) async-start(f32[512,3,4,128]{0,3,2,1:T(8,128)} %copy-done.2), calls=%async_computation.4 | async-start | bytes 2097152 | tf_op jit(solution)/shard_map/slice | solution.py:72
  70.7 8.2 %copy-start.8 = (s32[4]{0:T(128)S(1)}, s32[4]{0:T(128)}, u32[]{:S(2)}) copy-start(s32[4]{0:T(128)} %param.13) | copy-start | bytes 52
  74.7 84.4 %reduce-scatter.2.cloned.1.call-start = ((), (), s32[]{:S(2)}) async-start(), calls=%async_computation.2 | async-start | bytes 4128768 | tf_op jit(solution)/shard_map/reduce_scatter | solution.py:124
  103.5 2.2 %copy-start.1 = (f32[4,512,512]{1,2,0:T(8,128)S(1)}, f32[4,512,512]{1,2,0:T(8,128)}, u32[]{:S(2)}) copy-start(f32[4,512,512]{1,2,0:T(8,128)} %get-tuple-element.45) | copy-start | bytes 12582916
  104.4 2.5 %copy-start.3 = (f32[512,3,4,128]{0,3,2,1:T(8,128)S(1)}, f32[512,3,4,128]{0,3,2,1:T(8,128)}, u32[]{:S(2)}) copy-start(f32[512,3,4,128]{0,3,2,1:T(8,128)} %copy-done.2) | copy-start | bytes 9437188
  107.9 2.0 %copy-start.5 = (bf16[512,3584]{1,0:T(8,128)(2,1)S(1)}, bf16[512,3584]{1,0:T(8,128)(2,1)}, u32[]{:S(2)}) copy-start(bf16[512,3584]{1,0:T(8,128)(2,1)} %param.17) | copy-start | bytes 11010052
  110.0 49.2 %copy-start.4 = (bf16[1,64,3584]{2,1,0:T(8,128)(2,1)S(1)}, bf16[1,64,3584]{2,1,0:T(8,128)(2,1)}, u32[]{:S(2)}) copy-start(bf16[1,64,3584]{2,1,0:T(8,128)(2,1)} %param.10) | copy-start | bytes 1376260
  113.9 52.0 %copy-start.6 = (bf16[3,96,384]{2,1,0:T(8,128)(2,1)S(1)}, bf16[3,96,384]{2,1,0:T(8,128)(2,1)}, u32[]{:S(2)}) copy-start(bf16[3,96,384]{2,1,0:T(8,128)(2,1)} %param.19) | copy-start | bytes 663556
  160.5 6.4 %collective-permute-start = (bf16[2,8,96]{2,1,0:T(8,128)(2,1)S(1)}, bf16[2,8,96]{2,1,0:T(8,128)(2,1)S(1)}, u32[]{:S(2)}, u32[]{:S(2)}) collective-permute-start(bf16[2,8,96]{2,1,0:T(8,128)(2,1)S(1)} %slice_bitcast_fusion.1), channel_id=1, source_target_pairs={{0,8},{8,16},{16,24},{1,9},{9,17},{17,25},{2,10},{10,18},{18,26},{... | collective-permute-start | bytes 9224 | tf_op jit(solution)/shard_map/ppermute | solution.py:20
Sparse Core Ops, SparseCore 0:
  14.1 43.7 all-gather.3
  74.8 25.4 all-gather.5
  114.0 45.0 reduce-scatter.1
where the time goes:
time: 176 us; the launch traced here: 174 us
  waiting for transfers between devices  87.7 us (50%)
  matrix products  24.1 us (14%)
  local copies, waits for them, and re-layouts  23.9 us (14%)
  other arithmetic  17.6 us (10%)
  between operations  17.3 us (10%)
  starting transfers between devices  3.69 us (2%)
    reduce_scatter x1, waiting for transfers between devices, per_device(): lax.psum_scatter(head_terms(attended, w_out).astype(jnp.bfloat16), 'tok',...  45.2 us
    all_gather x1, waiting for transfers between devices, per_device(): lax.all_gather(modulated, 'tok', axis=0, tiled=True)  28.8 us
    unnamed x20, local copies, waits for them, and re-layouts  18.8 us
    all_gather x1, waiting for transfers between devices, attention(): piece = lax.all_gather(packed, 'span', axis=0, tiled=True)  12.7 us
    dot_general x1, matrix products, per_device(): jnp.dot(lax.all_gather(modulated, 'tok', axis=0, tiled=True), w_flat, pre...  9.77 us
    dot_general x5, matrix products, fold_block(): jnp.einsum('qhd,khd->hqk', query, block_keys, preferred_element_type=jnp....  5.52 us
    dot_general x1, matrix products, head_terms(): jnp.dot(attended, w_out, preferred_element_type=jnp.float32)  3.91 us
  transfers between devices with their start and end apart: 4, of which 4 were waited for; matrix products, arithmetic and copies ran while one was open for 16% of the time, Pallas kernels for 0%

commit v1 on v0

v1 whole, which is shorter than its diff:
```python
import functools

import jax
import jax.numpy as jnp
from jax import lax
from jax.experimental import pallas as pl
from jax.experimental.pallas import tpu as pltpu
from jax.sharding import PartitionSpec as P

HD = 128
FRAMES = 8
KEEP = 2
SPOTS = 8
TOK_DEV = 64
CORES = 2
LEAD = KEEP * SPOTS
HALO = 2 * SPOTS


EPS = 1e-06
NEG = -1e30
LOG2E = 1.4426950408889634
MIB = 1 << 20


def routes(line):
    if line == 4:
        return [
            [([(0, 2), (2, 3), (3, 1), (1, 0)], None)],
            [([(0, 1), (1, 3), (3, 2), (2, 0)], None)],
            [([(1, 2), (2, 1)], None), ([(2, 3), (1, 0)], 0)],
        ]
    return [[([(i, (i + by) % line) for i in range(line)], None)] for by in range(1, line)]


def lanes(pairs):
    return [(a * CORES + c, b * CORES + c) for a, b in pairs for c in range(CORES)]


def back(pairs):
    return [(b, a) for a, b in pairs]


def over_core(array):
    devices = lax.axis_size("tok")
    return lax.ppermute(array, "tok", [(i, i ^ 1) for i in range(devices)])


def from_behind(array, axis, by):
    devices = lax.axis_size(axis)
    pairs = [(i, i + by) for i in range(devices) if 0 <= i + by < devices]
    return lax.ppermute(array, axis, pairs)


def vmem():
    return pl.BlockSpec(memory_space=pltpu.VMEM)


def smem():
    return pl.BlockSpec(memory_space=pltpu.SMEM)


def cost(flops, moved, exps=0):
    return pl.CostEstimate(flops=int(flops), bytes_accessed=int(moved), transcendentals=int(exps))


def level_spec(table):
    return pl.BlockSpec((3, 8, table.shape[2]), lambda i, level: (0, level[0] // 8, 0))


def modulate_kernel(level, rows, table, out):
    at = pl.ds(level[0] % 8, 1)
    values = rows[...].astype(jnp.float32)
    centre = values - jnp.mean(values, -1, keepdims=True)
    spread = jnp.mean(centre * centre, -1, keepdims=True)
    out[...] = (
        centre * lax.rsqrt(spread + EPS) * (1.0 + table[1, at, :]) + table[0, at, :]
    ).astype(jnp.bfloat16)


def modulate(latents, levels, table, start, rows):
    width = latents.shape[1]
    unit = 16
    return pl.pallas_call(
        modulate_kernel,
        grid_spec=pltpu.PrefetchScalarGridSpec(
            num_scalar_prefetch=1,
            grid=(rows // unit,),
            in_specs=[
                pl.BlockSpec((unit, width), lambda i, level: (i + start // unit, 0)),
                level_spec(table),
            ],
            out_specs=pl.BlockSpec((unit, width), lambda i, level: (i, 0)),
        ),
        out_shape=jax.ShapeDtypeStruct((rows, width), jnp.bfloat16),
        compiler_params=pltpu.CompilerParams(vmem_limit_bytes=16 * MIB),
        cost_estimate=cost(10 * rows * width, 4 * rows * width + 24 * width * 4),
    )(levels, latents, table)


def project_kernel(count, *refs):
    tiles, (weight, gain, out, held, sems) = refs[:count], refs[count:]
    part = pl.program_id(0)
    first = (part == 0) & (pl.program_id(1) == 0)
    rows = tiles[0].shape[0]

    @pl.when(first)
    def _():
        copies = [
            pltpu.make_async_copy(tile, held.at[pl.ds(i * rows, rows)], sems.at[i])
            for i, tile in enumerate(tiles)
        ]
        for copy in copies:
            copy.start()
        for copy in copies:
            copy.wait()

    proj = jnp.dot(held[...], weight[0], preferred_element_type=jnp.float32)

    @pl.when(part == 2)
    def _():
        out[0] = proj.astype(jnp.bfloat16)

    @pl.when(part < 2)
    def _():
        for h in range(proj.shape[1] // HD):
            head = proj[:, h * HD : (h + 1) * HD]
            square = jnp.mean(head * head, -1, keepdims=True)
            cut = slice(h * HD, (h + 1) * HD)
            scale = jnp.where(part == 0, gain[0:1, cut], gain[1:2, cut])
            out[0, :, cut] = (
                head * lax.rsqrt(square + EPS) * scale
            ).astype(jnp.bfloat16)


def project(tiles, weight, gain):
    rows = tiles[0].shape[0] * len(tiles)
    width, cols = weight.shape[1:]
    unit = min(cols, 2 * HD)
    return pl.pallas_call(
        functools.partial(project_kernel, len(tiles)),
        grid=(3, cols // unit),
        in_specs=[pl.BlockSpec(memory_space=pl.ANY)] * len(tiles)
        + [
            pl.BlockSpec((1, width, unit), lambda p, i: (p, 0, i)),
            pl.BlockSpec((2, unit), lambda p, i: (0, i)),
        ],
        out_specs=pl.BlockSpec((1, rows, unit), lambda p, i: (p, 0, i)),
        out_shape=jax.ShapeDtypeStruct((3, rows, cols), jnp.bfloat16),
        scratch_shapes=[
            pltpu.VMEM((rows, width), jnp.bfloat16),
            pltpu.SemaphoreType.DMA((len(tiles),)),
        ],
        compiler_params=pltpu.CompilerParams(vmem_limit_bytes=32 * MIB),
        cost_estimate=cost(6 * rows * width * cols, 6 * width * cols + 2 * rows * width),
    )(*tiles, weight, gain)


def attend_kernel(pieces, behind, clip, visible, counts, *refs):
    queries = refs[:pieces]
    keys = refs[pieces : 2 * pieces]
    values = refs[2 * pieces : 3 * pieces]
    packed = refs[3 * pieces : 3 * pieces + behind]
    out = refs[-1]
    me = clip[0]
    scale = HD ** (-0.5) * LOG2E
    bias = []
    for by in range(1, behind + 1):
        source = me - by
        at = jnp.maximum(source, 0)
        limit = jnp.where((source >= 0) & (visible[me, at] == 1), counts[at], 0)
        row = lax.broadcasted_iota(jnp.int32, (1, packed[by - 1].shape[1]), 1)
        bias.append(jnp.where(row % LEAD // SPOTS < limit, 0.0, NEG))
    for h in range(out.shape[1] // HD):
        cut = slice(h * HD, (h + 1) * HD)
        key = [ref[0, :, cut] for ref in keys] + [ref[0, :, cut] for ref in packed]
        value = [ref[0, :, cut] for ref in values] + [ref[1, :, cut] for ref in packed]
        shift = [None] * pieces + bias
        begin = 0
        for query in queries:
            rows = query.shape[1]
            scores = []
            for block, add in zip(key, shift):
                score = lax.dot_general(
                    query[0, :, cut],
                    block,
                    (((1,), (1,)), ((), ())),
                    preferred_element_type=jnp.float32,
                )
                scores.append(score if add is None else score + add)
            best = functools.reduce(
                jnp.maximum, [jnp.max(score, -1, keepdims=True) for score in scores]
            )
            total = 0.0
            acc = 0.0
            for score, block in zip(scores, value):
                terms = jnp.exp2((score - best) * scale)
                total = total + jnp.sum(terms, -1, keepdims=True)
                acc = acc + jnp.dot(
                    terms.astype(jnp.bfloat16), block, preferred_element_type=jnp.float32
                )
            out[begin : begin + rows, cut] = (acc / total).astype(jnp.bfloat16)
            begin += rows


def attend(lane, parts, packed, clip, visible, counts):
    cols = parts[0].shape[2]
    own = sum(part.shape[1] for part in parts)
    seen = own + sum(block.shape[1] for block in packed)
    rows = own // CORES

    def half(part):
        return pl.BlockSpec((1, part.shape[1] // CORES, cols), lambda i: (0, lane, 0))

    def whole(part, which):
        return pl.BlockSpec((1,) + part.shape[1:], lambda i: (which, 0, 0))

    specs = [half(part) for part in parts]
    specs += [whole(part, 1) for part in parts] + [whole(part, 2) for part in parts]
    specs += [pl.BlockSpec(block.shape, lambda i: (0, 0, 0)) for block in packed]
    return pl.pallas_call(
        functools.partial(attend_kernel, len(parts), len(packed)),
        grid=(1,),
        in_specs=[smem()] * 3 + specs,
        out_specs=pl.BlockSpec((rows, cols), lambda i: (0, 0)),
        out_shape=jax.ShapeDtypeStruct((rows, cols), jnp.bfloat16),
        compiler_params=pltpu.CompilerParams(vmem_limit_bytes=32 * MIB),
        cost_estimate=cost(
            4 * rows * seen * cols, 2 * cols * (rows + 2 * seen), rows * seen * cols // HD
        ),
    )(clip, visible, counts, *parts, *parts, *parts, *packed)


def output_kernel(slots, sizes, mine, theirs, w_mine, w_theirs, *outs):
    term = jnp.dot(mine[...], w_mine[...], preferred_element_type=jnp.float32)
    term += jnp.dot(theirs[...], w_theirs[...], preferred_element_type=jnp.float32)
    term = term.astype(jnp.bfloat16)
    index = 0
    begin = 0
    for size in sizes:
        for _ in range(slots):
            outs[index][...] = term[begin : begin + size]
            begin += size
            index += 1


def output(mine, theirs, w_mine, w_theirs, slots, sizes):
    rows, cols = mine.shape
    width = w_mine.shape[1]
    unit = 512
    shapes = [size for size in sizes for _ in range(slots)]
    outs = pl.pallas_call(
        functools.partial(output_kernel, slots, sizes),
        grid=(width // unit,),
        in_specs=[pl.BlockSpec((rows, cols), lambda i: (0, 0))] * 2
        + [pl.BlockSpec((cols, unit), lambda i: (0, i))] * 2,
        out_specs=[pl.BlockSpec((size, unit), lambda i: (0, i)) for size in shapes],
        out_shape=[jax.ShapeDtypeStruct((size, width), jnp.bfloat16) for size in shapes],
        compiler_params=pltpu.CompilerParams(vmem_limit_bytes=32 * MIB),
        cost_estimate=cost(4 * rows * cols * width, 4 * cols * width + 2 * rows * width),
    )(mine, theirs, w_mine, w_theirs)
    return [outs[i * slots : (i + 1) * slots] for i in range(len(sizes))]


def residual_kernel(count, level, rows, table, head, *refs):
    terms, (denoised, feats) = refs[:count], refs[count:]
    at = pl.ds(level[0] % 8, 1)
    total = functools.reduce(lambda a, b: a + b, [term[...].astype(jnp.float32) for term in terms])
    new = (rows[...].astype(jnp.float32) + table[2, at, :] * total).astype(jnp.bfloat16)
    denoised[...] = new
    feats[...] = lax.dot_general(
        new, head[...], (((1,), (1,)), ((), ())), preferred_element_type=jnp.float32
    ).astype(jnp.bfloat16)


def residual(latents, levels, table, head, terms):
    rows, width = latents.shape
    channels = head.shape[0]
    whole = lambda i, level: (0, 0)
    return pl.pallas_call(
        functools.partial(residual_kernel, len(terms)),
        grid_spec=pltpu.PrefetchScalarGridSpec(
            num_scalar_prefetch=1,
            grid=(1,),
            in_specs=[
                pl.BlockSpec((rows, width), whole),
                level_spec(table),
                pl.BlockSpec(head.shape, whole),
            ]
            + [pl.BlockSpec((rows, width), whole)] * len(terms),
            out_specs=[
                pl.BlockSpec((rows, width), whole),
                pl.BlockSpec((rows, channels), whole),
            ],
        ),
        out_shape=[
            jax.ShapeDtypeStruct((rows, width), jnp.bfloat16),
            jax.ShapeDtypeStruct((rows, channels), jnp.bfloat16),
        ],
        compiler_params=pltpu.CompilerParams(vmem_limit_bytes=24 * MIB),
        cost_estimate=cost(
            2 * rows * width * channels, 2 * rows * width * (2 + len(terms)) + 2 * width * channels
        ),
    )(levels, latents, table, head, *terms)


def conv_kernel(earlier, feats, weight, out):
    rows = feats.shape[0]
    sequence = jnp.concatenate([earlier[...], feats[...]], 0)
    conv = jnp.zeros(out.shape, jnp.float32)
    for tap in range(3):
        begin = HALO - tap * SPOTS
        conv = conv + jnp.dot(
            sequence[begin : begin + rows], weight[tap], preferred_element_type=jnp.float32
        )
    out[...] = (conv / (1.0 + jnp.exp(-conv))).astype(jnp.bfloat16)


def conv(earlier, feats, weight):
    return pl.pallas_call(
        conv_kernel,
        in_specs=[vmem()] * 3,
        out_specs=vmem(),
        out_shape=jax.ShapeDtypeStruct((feats.shape[0], weight.shape[2]), jnp.bfloat16),
        compiler_params=pltpu.CompilerParams(vmem_limit_bytes=16 * MIB),
        cost_estimate=cost(6 * feats.shape[0] * weight.shape[1] * weight.shape[2], 400000),
    )(earlier, feats, weight)


def spread(tile, table, place):
    held = []
    for entries in table:
        got = None
        for pairs, source in entries:
            came = lax.ppermute(tile if source is None else held[source], "tok", lanes(pairs))
            if got is None:
                got = came
            else:
                takes = functools.reduce(lambda a, b: a | b, [place == b for _, b in pairs])
                got = jnp.where(takes, came, got)
        held.append(got)
    return [tile] + held


def gather_sums(terms, table):
    own, sent = terms[0], list(terms[1:])
    arrived = []
    for slot in reversed(range(len(table))):
        for pairs, source in table[slot]:
            came = lax.ppermute(sent[slot], "tok", lanes(back(pairs)))
            if source is None:
                arrived.append(came)
            else:
                sent[source] = (
                    sent[source].astype(jnp.float32) + came.astype(jnp.float32)
                ).astype(jnp.bfloat16)
    return [own] + arrived


def per_device(
    latents, levels, visible, frame_counts, modulation, w_qkv, qk_gain, w_out, w_head, conv_w
):
    current = latents[0]
    line = lax.axis_size("tok") // CORES
    place = lax.axis_index("tok") // CORES
    clip = lax.axis_index("span").astype(jnp.int32).reshape(1)
    table = routes(line)
    slots = line
    mods = modulation.transpose(1, 0, 2)
    weight = w_qkv.transpose(1, 0, 2)
    head = w_head.transpose(1, 0)
    w_theirs = over_core(w_out)

    modulated = modulate(current, levels, mods, 0, TOK_DEV)
    lane = spread(modulated, table, place)
    tiles = lane + [over_core(tile) for tile in lane]
    qkv = project(tiles, weight, qk_gain)

    cols = qkv.shape[2]
    lead = qkv.reshape(3, len(tiles), TOK_DEV, cols)[1:, :, :LEAD].reshape(2, -1, cols)
    packed = [from_behind(lead, "span", by) for by in range(1, lax.axis_size("span"))]

    theirs = attend(1, [qkv], packed, clip, visible, frame_counts)
    theirs = over_core(theirs)
    mine = attend(0, [qkv], packed, clip, visible, frame_counts)
    terms = output(mine, theirs, w_out, w_theirs, slots, [TOK_DEV])[0]
    sums = gather_sums(terms, table)
    denoised, feats = residual(current, levels, mods, head, sums)
    earlier = from_behind(feats[TOK_DEV - HALO :], "span", 1)
    decoded = conv(earlier, feats, conv_w)
    return (denoised[None], decoded[None])


def solution(mesh):
    placed = (
        P("span", "tok", None),
        P("span"),
        P(),
        P(),
        P(),
        P(None, None, "tok"),
        P(None, "tok"),
        P("tok", None),
        P(),
        P(),
    )
    return jax.shard_map(
        per_device,
        mesh=mesh,
        in_specs=placed,
        out_specs=(P("span", "tok", None), P("span", "tok", None)),
        check_vma=False,
    )
```

time: 176 us -> 135 us (0.77)
  Pallas kernels: 0 us -> 25.8 us
  matrix products: 24.1 us -> 0 us
  starting transfers between devices: 3.69 us -> 24.3 us
  other arithmetic: 17.6 us -> 0.16 us
  between operations: 17.3 us -> 1.57 us
  local copies, waits for them, and re-layouts: 23.9 us -> 8.77 us
  waiting for transfers between devices: 87.7 us -> 73.9 us
    ppermute x0 -> x14, waiting for transfers between devices: none -> 57.5 us  [the longest x4 28.4 us: spread(): lax.ppermute(tile if source is None else held[source], 'tok', lanes(pairs))]
    reduce_scatter x1 -> x0, waiting for transfers between devices: 45.2 us -> none  [per_device(): lax.psum_scatter(head_terms(attended, w_out).astype(jnp.bfloat16), 'tok',...]
    all_gather x2 -> x0, waiting for transfers between devices: 41.5 us -> none  [the longest x1 28.8 us: per_device(): lax.all_gather(modulated, 'tok', axis=0, tiled=True)]
    pallas_call x0 -> x7, Pallas kernels: none -> 25.8 us  [the longest x1 10.9 us: project(): pl.pallas_call(functools.partial(project_kernel, len(tiles)), grid=(3, co...]
    dot_general x16 -> x0, matrix products: 24.1 us -> none  [the longest x1 9.77 us: per_device(): jnp.dot(lax.all_gather(modulated, 'tok', axis=0, tiled=True), w_flat, pre...]
    ppermute x0 -> x14, starting transfers between devices: none -> 16.2 us  [the longest x4 8.01 us: spread(): lax.ppermute(tile if source is None else held[source], 'tok', lanes(pairs))]
    ppermute x1 -> x4, waiting for transfers between devices: 0.94 us -> 16.4 us  [from_behind(): return lax.ppermute(array, axis, pairs)]
    unnamed x20 -> x26, local copies, waits for them, and re-layouts: 18.8 us -> 8.75 us
  transfers between devices with their start and end apart: 4 -> 18, of which waited for: 4 -> 9; matrix products, arithmetic and copies ran while one was open for 16% -> 0% of each run, Pallas kernels for 0% -> 13%
where the time goes in v1:
time: 135 us
  waiting for transfers between devices  73.9 us (55%)
  Pallas kernels  25.8 us (19%)
  starting transfers between devices  24.3 us (18%)
  local copies, waits for them, and re-layouts  8.77 us (6%)
  between operations  1.57 us (1%)
    ppermute x4, waiting for transfers between devices, spread(): lax.ppermute(tile if source is None else held[source], 'tok', lanes(pairs))  28.4 us
    ppermute x4, waiting for transfers between devices, gather_sums(): came = lax.ppermute(sent[slot], 'tok', lanes(back(pairs)))  28.1 us
    ppermute x4, waiting for transfers between devices, from_behind(): return lax.ppermute(array, axis, pairs)  16.4 us
    pallas_call x1, Pallas kernels, project(): pl.pallas_call(functools.partial(project_kernel, len(tiles)), grid=(3, co...  10.9 us
    unnamed x26, local copies, waits for them, and re-layouts  8.75 us
    ppermute x4, starting transfers between devices, from_behind(): return lax.ppermute(array, axis, pairs)  8.03 us
    ppermute x4, starting transfers between devices, spread(): lax.ppermute(tile if source is None else held[source], 'tok', lanes(pairs))  8.01 us
    ppermute x4, starting transfers between devices, gather_sums(): came = lax.ppermute(sent[slot], 'tok', lanes(back(pairs)))  7.45 us
  transfers between devices with their start and end apart: 18, of which 9 were waited for; matrix products, arithmetic and copies ran while one was open for 0% of the time, Pallas kernels for 13%

profile of v1, /device:TPU:4, one launch (start us, length us, event | category | flops | bytes accessed | tf_op | source)
XLA Modules:
  0.0 134.5 jit_solution(700612974222434259)
XLA Ops:
  0.6 0.1 collective-permute-start.12
  1.4 0.0 copy-start.1
  1.4 1.1 copy-done.1
  2.5 1.0 copy-done.3
  3.5 1.1 shard_map.113.refs_0_
  4.6 2.6 %collective-permute-start = (bf16[64,3584]{1,0:T(8,128)(2,1)S(1)}, bf16[64,3584]{1,0:T(8,128)(2,1)S(1)}, u32[]{:S(2)}, u32[]{:S(2)}) collective-permute-start(bf16[64,3584]{1,0:T(8,128)(2,1)S(1)} %shard_map.113.refs_0_), channel_id=1, source_target_pairs={{0,4},{1,5},{4,6},{5,7},{6,2},{7,3},{2,0},{3,1},{8,12},{9,13},{12,... | collective-permute-start | bytes 1376264 | tf_op jit(solution)/shard_map/ppermute | solution.py:335
  7.3 0.7 collective-permute-start.3
  8.0 3.4 %collective-permute-start.1 = (bf16[64,3584]{1,0:T(8,128)(2,1)S(1)}, bf16[64,3584]{1,0:T(8,128)(2,1)S(1)}, u32[]{:S(2)}, u32[]{:S(2)}) collective-permute-start(bf16[64,3584]{1,0:T(8,128)(2,1)S(1)} %shard_map.113.refs_0_), channel_id=1, source_target_pairs={{0,2},{1,3},{2,6},{3,7},{6,4},{7,5},{4,0},{5,1},{8,10},{9,11},{10,... | collective-permute-start | bytes 1376264 | tf_op jit(solution)/shard_map/ppermute | solution.py:335
  11.4 6.8 %collective-permute-done.refs_1_ = bf16[64,3584]{1,0:T(8,128)(2,1)S(1)} collective-permute-done((bf16[64,3584]{1,0:T(8,128)(2,1)S(1)}, bf16[64,3584]{1,0:T(8,128)(2,1)S(1)}, u32[]{:S(2)}, u32[]{:S(2)}) %collective-permute-start) | collective-permute-done | bytes 458784 | tf_op jit(solution)/shard_map/ppermute | solution.py:335
  18.1 1.3 collective-permute-start.2
  19.4 0.1 collective-permute-start.4
  19.5 0.0 collective-permute-done.3
  19.5 0.5 collective-permute-start.5
  20.0 19.3 %collective-permute-done.1.refs_2_ = bf16[64,3584]{1,0:T(8,128)(2,1)S(1)} collective-permute-done((bf16[64,3584]{1,0:T(8,128)(2,1)S(1)}, bf16[64,3584]{1,0:T(8,128)(2,1)S(1)}, u32[]{:S(2)}, u32[]{:S(2)}) %collective-permute-start.1) | collective-permute-done | bytes 458784 | tf_op jit(solution)/shard_map/ppermute | solution.py:335
  39.3 0.0 collective-permute-start.6
  39.3 2.3 %collective-permute-done.2 = bf16[64,3584]{1,0:T(8,128)(2,1)S(1)} collective-permute-done((bf16[64,3584]{1,0:T(8,128)(2,1)S(1)}, bf16[64,3584]{1,0:T(8,128)(2,1)S(1)}, u32[]{:S(2)}, u32[]{:S(2)}) %collective-permute-start.2) | collective-permute-done | bytes 458784 | tf_op jit(solution)/shard_map/ppermute | solution.py:335
  41.7 0.1 collective-permute-start.7
  41.8 0.0 collective-permute-done.4.refs_4_
  41.8 0.0 copy-start.10
  41.8 0.8 copy-done.10
  42.5 0.0 collective-permute-done.6.refs_6_
  42.5 0.0 collective-permute-done.5.refs_5_
  42.5 1.0 collective-permute-done.7.refs_7_
  43.6 4.1 %copy-done.9 = bf16[3584,3,512]{2,0,1:T(8,128)(2,1)S(1)} copy-done((bf16[3584,3,512]{2,0,1:T(8,128)(2,1)S(1)}, bf16[3584,3,512]{2,0,1:T(8,128)(2,1)}, u32[]{:S(2)}) %copy-start.9) | copy-done | bytes 11010072
  47.7 1.0 copy-done.11
  48.7 0.7 copy-done.12
  49.4 10.9 %shard_map.114.refs_0_.refs_1_.refs_2_ = bf16[3,512,512]{2,1,0:T(8,128)(2,1)S(1)} custom-call(bf16[64,3584]{1,0:T(8,128)(2,1)S(1)} %shard_map.113.refs_0_, bf16[64,3584]{1,0:T(8,128)(2,1)S(1)} %collective-permute-done.refs_1_, bf16[64,3584]{1,0:T(8,128)(2,1)S(1)} %collective-permute-done.1.refs_2_, bf16[64,3584]{1,0:T(8,128)(2,1)S(1)} %broadcast_select_fusion.refs_3_, ...), custom_call_target="tpu_custom_call" | custom-call | flops 5637144576 | bytes 14680064 | tf_op jit(solution)/shard_map/pallas_call | solution.py:140
  60.3 0.7 collective-permute-start.10
  61.0 1.3 collective-permute-start.9
  62.3 4.0 %collective-permute-start.8 = (bf16[2,128,512]{2,1,0:T(8,128)(2,1)S(1)}, bf16[2,128,512]{2,1,0:T(8,128)(2,1)S(1)}, u32[]{:S(2)}, u32[]{:S(2)}) collective-permute-start(bf16[2,128,512]{2,1,0:T(8,128)(2,1)S(1)} %bitcast.18), channel_id=1, source_target_pairs={{0,8},{8,16},{16,24},{1,9},{9,17},{17,25},{2,10},{10,18},{18,26},{... | collective-permute-start | bytes 786440 | tf_op jit(solution)/shard_map/ppermute | solution.py:52
  66.4 0.0 collective-permute-done.10.refs_5_
  66.4 12.1 %collective-permute-done.9.refs_4_ = bf16[2,128,512]{2,1,0:T(8,128)(2,1)S(1)} collective-permute-done((bf16[2,128,512]{2,1,0:T(8,128)(2,1)S(1)}, bf16[2,128,512]{2,1,0:T(8,128)(2,1)S(1)}, u32[]{:S(2)}, u32[]{:S(2)}) %collective-permute-start.9) | collective-permute-done | bytes 262176 | tf_op jit(solution)/shard_map/ppermute | solution.py:52
  78.4 0.0 collective-permute-done.8.refs_3_
  78.4 0.0 copy-done.7
  78.4 0.0 copy-done.8
  78.5 2.8 %shard_map.116 = bf16[256,512]{1,0:T(8,128)(2,1)S(1)} custom-call(s32[1]{0:T(128)} %bitcast.3.clip, s32[4,4]{1,0:T(4,128)S(1)} %copy-done.7, s32[4]{0:T(128)S(1)} %copy-done.8, bf16[3,512,512]{2,1,0:T(8,128)(2,1)S(1)} %shard_map.114.refs_0_.refs_1_.refs_2_, bf16[3,512,512]{2,1,0:T(8,128)(2,1)S(1)} %shard_map.114.refs_0_.refs_1_.refs_2_, ...), custom_call_target="tpu_custom_call" | custom-call | flops 469762048 | bytes 2097152 | tf_op jit(solution)/shard_map/pallas_call | solution.py:221
  81.2 0.0 copy-start
  81.2 0.1 collective-permute-start.11
  81.3 2.8 %shard_map.115.mine = bf16[256,512]{1,0:T(8,128)(2,1)S(1)} custom-call(s32[1]{0:T(128)} %bitcast.3.clip, s32[4,4]{1,0:T(4,128)S(1)} %copy-done.7, s32[4]{0:T(128)S(1)} %copy-done.8, bf16[3,512,512]{2,1,0:T(8,128)(2,1)S(1)} %shard_map.114.refs_0_.refs_1_.refs_2_, bf16[3,512,512]{2,1,0:T(8,128)(2,1)S(1)} %shard_map.114.refs_0_.refs_1_.refs_2_, ...), custom_call_target="tpu_custom_call" | custom-call | flops 469762048 | bytes 2097152 | tf_op jit(solution)/shard_map/pallas_call | solution.py:221
  84.1 0.0 copy-start.2
  84.1 0.0 copy-start.4
  84.1 0.0 copy-start.5
  84.1 0.0 collective-permute-done.11.theirs
  84.1 0.0 collective-permute-done.12.w_theirs
  84.1 0.0 copy-done
  84.1 6.3 %shard_map.117 = (bf16[64,3584]{1,0:T(8,128)(2,1)S(1)}, bf16[64,3584]{1,0:T(8,128)(2,1)S(1)}, bf16[64,3584]{1,0:T(8,128)(2,1)S(1)}, bf16[64,3584]{1,0:T(8,128)(2,1)S(1)}) custom-call(bf16[256,512]{1,0:T(8,128)(2,1)S(1)} %shard_map.115.mine, bf16[256,512]{1,0:T(8,128)(2,1)S(1)} %collective-permute-done.11.theirs, bf16[512,3584]{1,0:T(8,128)(2,1)S(1)} %copy-done, ...), custom_call_target="tpu_custom_call" | custom-call | flops 1879048192 | bytes 9175040 | tf_op jit(solution)/shard_map/pallas_call | solution.py:252
  90.5 0.0 copy-start.6
  90.5 1.6 %collective-permute-start.15 = (bf16[64,3584]{1,0:T(8,128)(2,1)S(1)}, bf16[64,3584]{1,0:T(8,128)(2,1)S(1)}, u32[]{:S(2)}, u32[]{:S(2)}) collective-permute-start(bf16[64,3584]{1,0:T(8,128)(2,1)S(1)} %get-tuple-element.9), channel_id=1, source_target_pairs={{6,4},{7,5},{0,2},{1,3},{14,12},{15,13},{8,10},{9,11},{22,20},{23,... | collective-permute-start | bytes 1376264 | tf_op jit(solution)/shard_map/ppermute | solution.py:350
  92.1 0.7 collective-permute-start.13
  92.8 2.6 %collective-permute-start.14 = (bf16[64,3584]{1,0:T(8,128)(2,1)S(1)}, bf16[64,3584]{1,0:T(8,128)(2,1)S(1)}, u32[]{:S(2)}, u32[]{:S(2)}) collective-permute-start(bf16[64,3584]{1,0:T(8,128)(2,1)S(1)} %get-tuple-element.10), channel_id=1, source_target_pairs={{2,0},{3,1},{6,2},{7,3},{4,6},{5,7},{0,4},{1,5},{10,8},{11,9},{14,... | collective-permute-start | bytes 1376264 | tf_op jit(solution)/shard_map/ppermute | solution.py:350
  95.4 7.5 %collective-permute-done.15 = bf16[64,3584]{1,0:T(8,128)(2,1)S(1)} collective-permute-done((bf16[64,3584]{1,0:T(8,128)(2,1)S(1)}, bf16[64,3584]{1,0:T(8,128)(2,1)S(1)}, u32[]{:S(2)}, u32[]{:S(2)}) %collective-permute-start.15) | collective-permute-done | bytes 458784 | tf_op jit(solution)/shard_map/ppermute | solution.py:350
  102.9 0.1 add_convert_fusion
  103.0 2.5 %collective-permute-start.16 = (bf16[64,3584]{1,0:T(8,128)(2,1)S(1)}, bf16[64,3584]{1,0:T(8,128)(2,1)S(1)}, u32[]{:S(2)}, u32[]{:S(2)}) collective-permute-start(bf16[64,3584]{1,0:T(8,128)(2,1)S(1)} %add_convert_fusion), channel_id=1, source_target_pairs={{4,0},{5,1},{6,4},{7,5},{2,6},{3,7},{0,2},{1,3},{12,8},{13,9},{14,... | collective-permute-start | bytes 1376264 | tf_op jit(solution)/shard_map/ppermute | solution.py:350
  105.5 7.2 %collective-permute-done.14.refs_2_ = bf16[64,3584]{1,0:T(8,128)(2,1)S(1)} collective-permute-done((bf16[64,3584]{1,0:T(8,128)(2,1)S(1)}, bf16[64,3584]{1,0:T(8,128)(2,1)S(1)}, u32[]{:S(2)}, u32[]{:S(2)}) %collective-permute-start.14) | collective-permute-done | bytes 458784 | tf_op jit(solution)/shard_map/ppermute | solution.py:350
  112.7 0.0 collective-permute-done.13.refs_1_
  112.7 13.4 %collective-permute-done.16.refs_3_ = bf16[64,3584]{1,0:T(8,128)(2,1)S(1)} collective-permute-done((bf16[64,3584]{1,0:T(8,128)(2,1)S(1)}, bf16[64,3584]{1,0:T(8,128)(2,1)S(1)}, u32[]{:S(2)}, u32[]{:S(2)}) %collective-permute-start.16) | collective-permute-done | bytes 458784 | tf_op jit(solution)/shard_map/ppermute | solution.py:350
  126.2 0.0 copy-done.2
  126.2 0.0 copy-done.4
  126.2 0.0 copy-done.5
  126.2 1.1 shard_map.118
  127.3 2.0 %collective-permute-start.17 = (bf16[16,96]{1,0:T(8,128)(2,1)S(1)}, bf16[16,96]{1,0:T(8,128)(2,1)S(1)}, u32[]{:S(2)}, u32[]{:S(2)}) collective-permute-start(bf16[16,96]{1,0:T(8,128)(2,1)S(1)} %slice.7), channel_id=1, source_target_pairs={{0,8},{8,16},{16,24},{1,9},{9,17},{17,25},{2,10},{10,18},{18,26},{... | collective-permute-start | bytes 9224 | tf_op jit(solution)/shard_map/ppermute | solution.py:52
  129.4 4.3 %collective-permute-done.17.earlier = bf16[16,96]{1,0:T(8,128)(2,1)S(1)} collective-permute-done((bf16[16,96]{1,0:T(8,128)(2,1)S(1)}, bf16[16,96]{1,0:T(8,128)(2,1)S(1)}, u32[]{:S(2)}, u32[]{:S(2)}) %collective-permute-start.17) | collective-permute-done | bytes 3104 | tf_op jit(solution)/shard_map/ppermute | solution.py:52
  133.7 0.0 copy-done.6
  133.7 0.8 shard_map.119
  (9 shorter events, 0.1 us)
Async XLA Ops:
  0.6 83.5 %collective-permute-start.12 = (bf16[512,3584]{1,0:T(8,128)(2,1)}, bf16[512,3584]{1,0:T(8,128)(2,1)}, u32[]{:S(2)}, u32[]{:S(2)}) collective-permute-start(bf16[512,3584]{1,0:T(8,128)(2,1)} %w_mine.1), channel_id=1, source_target_pairs={{0,1},{1,0},{2,3},{3,2},{4,5},{5,4},{6,7},{7,6},{8,9},{9,8},{10,11... | collective-permute-start | bytes 11010056 | tf_op jit(solution)/shard_map/ppermute | solution.py:46
  1.4 1.1 copy-start.1
  2.5 1.0 copy-start.3
  4.6 13.5 %collective-permute-start = (bf16[64,3584]{1,0:T(8,128)(2,1)S(1)}, bf16[64,3584]{1,0:T(8,128)(2,1)S(1)}, u32[]{:S(2)}, u32[]{:S(2)}) collective-permute-start(bf16[64,3584]{1,0:T(8,128)(2,1)S(1)} %shard_map.113.refs_0_), channel_id=1, source_target_pairs={{0,4},{1,5},{4,6},{5,7},{6,2},{7,3},{2,0},{3,1},{8,12},{9,13},{12,... | collective-permute-start | bytes 1376264 | tf_op jit(solution)/shard_map/ppermute | solution.py:335
  7.3 12.3 %collective-permute-start.3 = (bf16[64,3584]{1,0:T(8,128)(2,1)S(1)}, bf16[64,3584]{1,0:T(8,128)(2,1)S(1)}, u32[]{:S(2)}, u32[]{:S(2)}) collective-permute-start(bf16[64,3584]{1,0:T(8,128)(2,1)S(1)} %shard_map.113.refs_0_), channel_id=1, source_target_pairs={{2,4},{3,5},{4,2},{5,3},{10,12},{11,13},{12,10},{13,11},{18,20},{1... | collective-permute-start | bytes 1376264 | tf_op jit(solution)/shard_map/ppermute | solution.py:335
  8.0 31.3 %collective-permute-start.1 = (bf16[64,3584]{1,0:T(8,128)(2,1)S(1)}, bf16[64,3584]{1,0:T(8,128)(2,1)S(1)}, u32[]{:S(2)}, u32[]{:S(2)}) collective-permute-start(bf16[64,3584]{1,0:T(8,128)(2,1)S(1)} %shard_map.113.refs_0_), channel_id=1, source_target_pairs={{0,2},{1,3},{2,6},{3,7},{6,4},{7,5},{4,0},{5,1},{8,10},{9,11},{10,... | collective-permute-start | bytes 1376264 | tf_op jit(solution)/shard_map/ppermute | solution.py:335
  18.1 23.5 %collective-permute-start.2 = (bf16[64,3584]{1,0:T(8,128)(2,1)S(1)}, bf16[64,3584]{1,0:T(8,128)(2,1)S(1)}, u32[]{:S(2)}, u32[]{:S(2)}) collective-permute-start(bf16[64,3584]{1,0:T(8,128)(2,1)S(1)} %collective-permute-done.refs_1_), channel_id=1, source_target_pairs={{4,6},{5,7},{2,0},{3,1},{12,14},{13,15},{10,8},{11,9},{20,22},{21,... | collective-permute-start | bytes 1376264 | tf_op jit(solution)/shard_map/ppermute | solution.py:335
  19.4 22.3 %collective-permute-start.4 = (bf16[64,3584]{1,0:T(8,128)(2,1)S(1)}, bf16[64,3584]{1,0:T(8,128)(2,1)S(1)}, u32[]{:S(2)}, u32[]{:S(2)}) collective-permute-start(bf16[64,3584]{1,0:T(8,128)(2,1)S(1)} %shard_map.113.refs_0_), channel_id=1, source_target_pairs={{0,1},{1,0},{2,3},{3,2},{4,5},{5,4},{6,7},{7,6},{8,9},{9,8},{10,11... | collective-permute-start | bytes 1376264 | tf_op jit(solution)/shard_map/ppermute | solution.py:46
  19.5 23.0 %collective-permute-start.5 = (bf16[64,3584]{1,0:T(8,128)(2,1)S(1)}, bf16[64,3584]{1,0:T(8,128)(2,1)S(1)}, u32[]{:S(2)}, u32[]{:S(2)}) collective-permute-start(bf16[64,3584]{1,0:T(8,128)(2,1)S(1)} %collective-permute-done.refs_1_), channel_id=1, source_target_pairs={{0,1},{1,0},{2,3},{3,2},{4,5},{5,4},{6,7},{7,6},{8,9},{9,8},{10,11... | collective-permute-start | bytes 1376264 | tf_op jit(solution)/shard_map/ppermute | solution.py:46
  39.3 3.3 %collective-permute-start.6 = (bf16[64,3584]{1,0:T(8,128)(2,1)S(1)}, bf16[64,3584]{1,0:T(8,128)(2,1)S(1)}, u32[]{:S(2)}, u32[]{:S(2)}) collective-permute-start(bf16[64,3584]{1,0:T(8,128)(2,1)S(1)} %collective-permute-done.1.refs_2_), channel_id=1, source_target_pairs={{0,1},{1,0},{2,3},{3,2},{4,5},{5,4},{6,7},{7,6},{8,9},{9,8},{10,11... | collective-permute-start | bytes 1376264 | tf_op jit(solution)/shard_map/ppermute | solution.py:46
  41.7 1.9 %collective-permute-start.7 = (bf16[64,3584]{1,0:T(8,128)(2,1)S(1)}, bf16[64,3584]{1,0:T(8,128)(2,1)S(1)}, u32[]{:S(2)}, u32[]{:S(2)}) collective-permute-start(bf16[64,3584]{1,0:T(8,128)(2,1)S(1)} %broadcast_select_fusion.refs_3_), channel_id=1, source_target_pairs={{0,1},{1,0},{2,3},{3,2},{4,5},{5,4},{6,7},{7,6},{8,9},{9,8},{10,11... | collective-permute-start | bytes 1376264 | tf_op jit(solution)/shard_map/ppermute | solution.py:46
  41.8 0.8 copy-start.10
  43.6 4.1 %copy-start.9 = (bf16[3584,3,512]{2,0,1:T(8,128)(2,1)S(1)}, bf16[3584,3,512]{2,0,1:T(8,128)(2,1)}, u32[]{:S(2)}) copy-start(bf16[3584,3,512]{2,0,1:T(8,128)(2,1)} %param.15) | copy-start | bytes 33030148
  47.7 1.0 copy-start.11
  48.7 0.7 copy-start.12
  49.4 29.1 %copy-start.7 = (s32[4,4]{1,0:T(4,128)S(1)}, s32[4,4]{1,0:T(4,128)}, u32[]{:S(2)}) copy-start(s32[4,4]{1,0:T(4,128)} %visible.3) | copy-start | bytes 196
  49.4 29.1 %copy-start.8 = (s32[4]{0:T(128)S(1)}, s32[4]{0:T(128)}, u32[]{:S(2)}) copy-start(s32[4]{0:T(128)} %counts.3) | copy-start | bytes 52
  60.3 6.0 %collective-permute-start.10 = (bf16[2,128,512]{2,1,0:T(8,128)(2,1)S(1)}, bf16[2,128,512]{2,1,0:T(8,128)(2,1)S(1)}, u32[]{:S(2)}, u32[]{:S(2)}) collective-permute-start(bf16[2,128,512]{2,1,0:T(8,128)(2,1)S(1)} %bitcast.16), channel_id=1, source_target_pairs={{0,24},{1,25},{2,26},{3,27},{4,28},{5,29},{6,30},{7,31}} | collective-permute-start | bytes 786440 | tf_op jit(solution)/shard_map/ppermute | solution.py:52
  61.0 17.4 %collective-permute-start.9 = (bf16[2,128,512]{2,1,0:T(8,128)(2,1)S(1)}, bf16[2,128,512]{2,1,0:T(8,128)(2,1)S(1)}, u32[]{:S(2)}, u32[]{:S(2)}) collective-permute-start(bf16[2,128,512]{2,1,0:T(8,128)(2,1)S(1)} %bitcast.17), channel_id=1, source_target_pairs={{0,16},{8,24},{1,17},{9,25},{2,18},{10,26},{3,19},{11,27},{4,20},{... | collective-permute-start | bytes 786440 | tf_op jit(solution)/shard_map/ppermute | solution.py:52
  62.3 16.1 %collective-permute-start.8 = (bf16[2,128,512]{2,1,0:T(8,128)(2,1)S(1)}, bf16[2,128,512]{2,1,0:T(8,128)(2,1)S(1)}, u32[]{:S(2)}, u32[]{:S(2)}) collective-permute-start(bf16[2,128,512]{2,1,0:T(8,128)(2,1)S(1)} %bitcast.18), channel_id=1, source_target_pairs={{0,8},{8,16},{16,24},{1,9},{9,17},{17,25},{2,10},{10,18},{18,26},{... | collective-permute-start | bytes 786440 | tf_op jit(solution)/shard_map/ppermute | solution.py:52
  81.2 2.9 %copy-start = (bf16[512,3584]{1,0:T(8,128)(2,1)S(1)}, bf16[512,3584]{1,0:T(8,128)(2,1)}, u32[]{:S(2)}) copy-start(bf16[512,3584]{1,0:T(8,128)(2,1)} %w_mine.1) | copy-start | bytes 11010052
  81.2 2.9 %collective-permute-start.11 = (bf16[256,512]{1,0:T(8,128)(2,1)S(1)}, bf16[256,512]{1,0:T(8,128)(2,1)S(1)}, u32[]{:S(2)}, u32[]{:S(2)}) collective-permute-start(bf16[256,512]{1,0:T(8,128)(2,1)S(1)} %shard_map.116), channel_id=1, source_target_pairs={{0,1},{1,0},{2,3},{3,2},{4,5},{5,4},{6,7},{7,6},{8,9},{9,8},{10,11... | collective-permute-start | bytes 786440 | tf_op jit(solution)/shard_map/ppermute | solution.py:46
  84.1 42.1 %copy-start.2 = (f32[16,3,3584]{2,0,1:T(8,128)S(1)}, f32[16,3,3584]{2,0,1:T(8,128)}, u32[]{:S(2)}) copy-start(f32[16,3,3584]{2,0,1:T(8,128)} %param.14) | copy-start | bytes 2064388
  84.1 42.1 %copy-start.4 = (bf16[1,64,3584]{2,1,0:T(8,128)(2,1)S(1)}, bf16[1,64,3584]{2,1,0:T(8,128)(2,1)}, u32[]{:S(2)}) copy-start(bf16[1,64,3584]{2,1,0:T(8,128)(2,1)} %param.10) | copy-start | bytes 1376260
  84.1 42.1 %copy-start.5 = (bf16[3584,96]{0,1:T(8,128)(2,1)S(1)}, bf16[3584,96]{0,1:T(8,128)(2,1)}, u32[]{:S(2)}) copy-start(bf16[3584,96]{0,1:T(8,128)(2,1)} %param.18) | copy-start | bytes 2064388
  90.5 43.2 %copy-start.6 = (bf16[3,96,384]{2,1,0:T(8,128)(2,1)S(1)}, bf16[3,96,384]{2,1,0:T(8,128)(2,1)}, u32[]{:S(2)}) copy-start(bf16[3,96,384]{2,1,0:T(8,128)(2,1)} %weight.1) | copy-start | bytes 663556
  90.5 12.4 %collective-permute-start.15 = (bf16[64,3584]{1,0:T(8,128)(2,1)S(1)}, bf16[64,3584]{1,0:T(8,128)(2,1)S(1)}, u32[]{:S(2)}, u32[]{:S(2)}) collective-permute-start(bf16[64,3584]{1,0:T(8,128)(2,1)S(1)} %get-tuple-element.9), channel_id=1, source_target_pairs={{6,4},{7,5},{0,2},{1,3},{14,12},{15,13},{8,10},{9,11},{22,20},{23,... | collective-permute-start | bytes 1376264 | tf_op jit(solution)/shard_map/ppermute | solution.py:350
  92.1 20.6 %collective-permute-start.13 = (bf16[64,3584]{1,0:T(8,128)(2,1)S(1)}, bf16[64,3584]{1,0:T(8,128)(2,1)S(1)}, u32[]{:S(2)}, u32[]{:S(2)}) collective-permute-start(bf16[64,3584]{1,0:T(8,128)(2,1)S(1)} %get-tuple-element.9), channel_id=1, source_target_pairs={{4,2},{5,3},{2,4},{3,5},{12,10},{13,11},{10,12},{11,13},{20,18},{2... | collective-permute-start | bytes 1376264 | tf_op jit(solution)/shard_map/ppermute | solution.py:350
  92.8 19.9 %collective-permute-start.14 = (bf16[64,3584]{1,0:T(8,128)(2,1)S(1)}, bf16[64,3584]{1,0:T(8,128)(2,1)S(1)}, u32[]{:S(2)}, u32[]{:S(2)}) collective-permute-start(bf16[64,3584]{1,0:T(8,128)(2,1)S(1)} %get-tuple-element.10), channel_id=1, source_target_pairs={{2,0},{3,1},{6,2},{7,3},{4,6},{5,7},{0,4},{1,5},{10,8},{11,9},{14,... | collective-permute-start | bytes 1376264 | tf_op jit(solution)/shard_map/ppermute | solution.py:350
  103.0 23.2 %collective-permute-start.16 = (bf16[64,3584]{1,0:T(8,128)(2,1)S(1)}, bf16[64,3584]{1,0:T(8,128)(2,1)S(1)}, u32[]{:S(2)}, u32[]{:S(2)}) collective-permute-start(bf16[64,3584]{1,0:T(8,128)(2,1)S(1)} %add_convert_fusion), channel_id=1, source_target_pairs={{4,0},{5,1},{6,4},{7,5},{2,6},{3,7},{0,2},{1,3},{12,8},{13,9},{14,... | collective-permute-start | bytes 1376264 | tf_op jit(solution)/shard_map/ppermute | solution.py:350
  127.3 6.4 %collective-permute-start.17 = (bf16[16,96]{1,0:T(8,128)(2,1)S(1)}, bf16[16,96]{1,0:T(8,128)(2,1)S(1)}, u32[]{:S(2)}, u32[]{:S(2)}) collective-permute-start(bf16[16,96]{1,0:T(8,128)(2,1)S(1)} %slice.7), channel_id=1, source_target_pairs={{0,8},{8,16},{16,24},{1,9},{9,17},{17,25},{2,10},{10,18},{18,26},{... | collective-permute-start | bytes 9224 | tf_op jit(solution)/shard_map/ppermute | solution.py:52

commit v2 on v0

v2 whole, which is shorter than its diff:
```python
import functools

import jax
import jax.numpy as jnp
from jax import lax
from jax.experimental import pallas as pl
from jax.experimental.pallas import tpu as pltpu
from jax.sharding import PartitionSpec as P

HD = 128
FRAMES = 8
KEEP = 2
SPOTS = 8
TOK_DEV = 64
CORES = 2
LEAD = KEEP * SPOTS
HALO = 2 * SPOTS
BODY = TOK_DEV - LEAD
END = 32
REST = TOK_DEV - END


EPS = 1e-06
NEG = -1e30
LOG2E = 1.4426950408889634
MIB = 1 << 20


def routes(line):
    if line == 4:
        return [
            ([(0, 2), (2, 3), (3, 1), (1, 0)], None),
            ([(0, 1), (1, 3), (3, 2), (2, 0)], None),
            ([(0, 1), (1, 0), (2, 3), (3, 2)], (1, 0, 0, 1)),
        ]
    return [([(i, (i + by) % line) for i in range(line)], None) for by in range(1, line)]


def direct(table):
    def origin(place, relay):
        if relay is None:
            return place
        return next(a for a, b in table[relay[place]][0] if b == place)

    return [([(origin(a, relay), b) for a, b in pairs], None) for pairs, relay in table]


def lanes(pairs):
    return [(a * CORES + c, b * CORES + c) for a, b in pairs for c in range(CORES)]


def back(pairs):
    return [(b, a) for a, b in pairs]


def after(array, *others):
    return lax.optimization_barrier((array,) + others)[0]


def over_core(array):
    devices = lax.axis_size("tok")
    return lax.ppermute(array, "tok", [(i, i ^ 1) for i in range(devices)])


def from_behind(array, axis, by):
    devices = lax.axis_size(axis)
    pairs = [(i, i + by) for i in range(devices) if 0 <= i + by < devices]
    return lax.ppermute(array, axis, pairs)


def from_earlier(array):
    devices = lax.axis_size("span")
    if devices != 4:
        steps = range(1, devices)
        came = [from_behind(array, "span", by) for by in steps]
        return came, [lambda me, by=by: me - by for by in steps]
    beside = lax.ppermute(array, "span", [(0, 1), (2, 3)])
    behind = lax.ppermute(array, "span", [(0, 2), (1, 3)])
    across = lax.ppermute(after(behind, beside), "span", [(3, 2), (2, 3)])
    return [beside, behind, across], [
        lambda me: jnp.where(me % 2 == 1, me - 1, -1),
        lambda me: me - 2,
        lambda me: jnp.where(me % 2 == 1, me - 3, me - 1),
    ]


def vmem():
    return pl.BlockSpec(memory_space=pltpu.VMEM)


def smem():
    return pl.BlockSpec(memory_space=pltpu.SMEM)


def hbm():
    return pl.BlockSpec(memory_space=pltpu.HBM)


def in_hbm(array):
    return pltpu.with_memory_space_constraint(array, pltpu.HBM)


def in_vmem(array):
    return pltpu.with_memory_space_constraint(array, pltpu.VMEM)


CHEAP = pl.CostEstimate(flops=1, bytes_accessed=1, transcendentals=0)


def params(mib):
    return pltpu.CompilerParams(vmem_limit_bytes=mib * MIB)


def modulate_kernel(level, rows, table, lead, body, held, mods, sems):
    base = pl.multiple_of(level[0] // 8 * 8, 8)
    copies = [
        pltpu.make_async_copy(rows, held, sems.at[0]),
        pltpu.make_async_copy(table.at[pl.ds(0, 2), pl.ds(base, 8)], mods, sems.at[1]),
    ]
    for copy in copies:
        copy.start()
    for copy in copies:
        copy.wait()
    at = pl.ds(level[0] % 8, 1)
    begin = 0
    for out in (lead, body):
        values = held[begin : begin + out.shape[0]].astype(jnp.float32)
        centre = values - jnp.mean(values, -1, keepdims=True)
        spread = jnp.mean(centre * centre, -1, keepdims=True)
        out[...] = (
            centre * lax.rsqrt(spread + EPS) * (1.0 + mods[1, at, :]) + mods[0, at, :]
        ).astype(jnp.bfloat16)
        begin += out.shape[0]


def modulate(latents, levels, table):
    rows, width = latents.shape
    return pl.pallas_call(
        modulate_kernel,
        in_specs=[smem(), hbm(), hbm()],
        out_specs=[vmem()] * 2,
        out_shape=[
            jax.ShapeDtypeStruct((part, width), jnp.bfloat16) for part in (LEAD, rows - LEAD)
        ],
        scratch_shapes=[
            pltpu.VMEM((rows, width), jnp.bfloat16),
            pltpu.VMEM((2, 8, width), jnp.float32),
            pltpu.SemaphoreType.DMA((2,)),
        ],
        compiler_params=params(8),
        cost_estimate=CHEAP,
    )(levels, in_hbm(latents), in_hbm(table))


def project_kernel(count, *refs):
    tiles, (gain, weight, out, kept, held, sems) = refs[:count], refs[count:]
    cols = weight.shape[2]
    unit = cols
    blocks = [(part, begin) for part in range(3) for begin in range(0, cols, unit)]
    copies = [
        pltpu.make_async_copy(
            weight.at[part, :, pl.ds(begin, unit)],
            kept.at[part, :, pl.ds(begin, unit)],
            sems.at[i],
        )
        for i, (part, begin) in enumerate(blocks)
    ]
    for copy in copies:
        copy.start()
    begin = 0
    for tile in tiles:
        held[begin : begin + tile.shape[0]] = tile[...]
        begin += tile.shape[0]
    for copy, (part, begin) in zip(copies, blocks):
        copy.wait()
        proj = jnp.dot(
            held[...], kept[part, :, begin : begin + unit], preferred_element_type=jnp.float32
        )
        if part == 2:
            out[part, :, begin : begin + unit] = proj.astype(jnp.bfloat16)
            continue
        for h in range(unit // HD):
            cut = slice(begin + h * HD, begin + (h + 1) * HD)
            head = proj[:, h * HD : (h + 1) * HD]
            square = jnp.mean(head * head, -1, keepdims=True)
            out[part, :, cut] = (
                head * lax.rsqrt(square + EPS) * gain[part : part + 1, cut]
            ).astype(jnp.bfloat16)


def project(tiles, gain, weight):
    rows = sum(tile.shape[0] for tile in tiles)
    width, cols = weight.shape[1:]
    return pl.pallas_call(
        functools.partial(project_kernel, len(tiles)),
        in_specs=[vmem()] * (len(tiles) + 1) + [hbm()],
        out_specs=vmem(),
        out_shape=jax.ShapeDtypeStruct((3, rows, cols), jnp.bfloat16),
        scratch_shapes=[
            pltpu.VMEM(weight.shape, weight.dtype),
            pltpu.VMEM((rows, width), jnp.bfloat16),
            pltpu.SemaphoreType.DMA((3,)),
        ],
        compiler_params=params(18 + rows // 64 // 8),
        cost_estimate=CHEAP,
    )(*tiles, gain, in_hbm(weight))


def attend_kernel(cuts, own, origins, clip, visible, counts, *refs):
    parts = refs[:own]
    behind = len(origins)
    packed = refs[own : own + behind]
    weight, out, kept, sem = refs[own + behind :]
    copy = pltpu.make_async_copy(weight, kept, sem)
    copy.start()
    me = clip[0]
    scale = HD ** (-0.5) * LOG2E
    bias = []
    for origin, block in zip(origins, packed):
        source = origin(me)
        at = jnp.maximum(source, 0)
        limit = jnp.where((source >= 0) & (visible[me, at] == 1), counts[at], 0)
        row = lax.broadcasted_iota(jnp.int32, (1, block.shape[1]), 1)
        bias.append(jnp.where(row % LEAD // SPOTS < limit, 0.0, NEG))
    heads = [slice(h * HD, (h + 1) * HD) for h in range(out.shape[1] // HD)]
    scores = []
    for cut in heads:
        query = jnp.concatenate(
            [parts[part][0, begin:end, cut] for part, begin, end in cuts], 0
        )
        keys = [(ref[1, :, cut], None) for ref in parts]
        keys += [(ref[0, :, cut], add) for ref, add in zip(packed, bias)]
        row = []
        for key, add in keys:
            score = lax.dot_general(
                query, key, (((1,), (1,)), ((), ())), preferred_element_type=jnp.float32
            )
            row.append(score if add is None else score + add)
        scores.append(row)
    terms, totals = [], []
    for row in scores:
        best = functools.reduce(jnp.maximum, [jnp.max(score, -1, keepdims=True) for score in row])
        row = [jnp.exp2((score - best) * scale) for score in row]
        totals.append(sum(jnp.sum(term, -1, keepdims=True) for term in row))
        terms.append([term.astype(jnp.bfloat16) for term in row])
    for cut, row, total in zip(heads, terms, totals):
        values = [ref[2, :, cut] for ref in parts]
        values += [ref[1, :, cut] for ref in packed]
        acc = sum(
            jnp.dot(term, value, preferred_element_type=jnp.float32)
            for term, value in zip(row, values)
        )
        out[:, cut] = (acc / total).astype(jnp.bfloat16)
    copy.wait()


def attend(cuts, parts, packed, origins, clip, visible, counts, weight):
    cols = parts[0].shape[2]
    seen = sum(part.shape[1] for part in parts)
    seen += sum(block.shape[1] for block in packed)
    rows = sum(end - begin for _, begin, end in cuts)
    return pl.pallas_call(
        functools.partial(attend_kernel, cuts, len(parts), origins),
        in_specs=[smem()] * 3 + [vmem()] * (len(parts) + len(packed)) + [hbm()],
        out_specs=[vmem()] * 2,
        out_shape=[
            jax.ShapeDtypeStruct((rows, cols), jnp.bfloat16),
            pltpu.VMEM(weight.shape, weight.dtype),
        ],
        scratch_shapes=[pltpu.SemaphoreType.DMA],
        compiler_params=params(max(10, 12 * rows * seen * cols // HD // MIB)),
        cost_estimate=CHEAP,
    )(clip, visible, counts, *parts, *packed, in_hbm(weight))


def output_kernel(attended, weight, *outs):
    unit = 512
    for column in range(0, weight.shape[1], unit):
        cut = slice(column, column + unit)
        term = jnp.dot(attended[...], weight[:, cut], preferred_element_type=jnp.float32)
        term = term.astype(jnp.bfloat16)
        begin = 0
        for out in outs:
            out[:, cut] = term[begin : begin + out.shape[0]]
            begin += out.shape[0]


def output(attended, weight, slots):
    rows, cols = attended.shape
    width = weight.shape[1]
    unit = rows // (CORES * slots)
    sizes = [unit] * slots + [unit * (slots - 1), unit]
    return pl.pallas_call(
        output_kernel,
        in_specs=[vmem()] * 2,
        out_specs=[vmem()] * len(sizes),
        out_shape=[jax.ShapeDtypeStruct((size, width), jnp.bfloat16) for size in sizes],
        compiler_params=params(10),
        cost_estimate=CHEAP,
    )(attended, in_vmem(weight))


def fold(rows, gate, terms):
    total = functools.reduce(lambda a, b: a + b, [term[...].astype(jnp.float32) for term in terms])
    return (rows.astype(jnp.float32) + gate * total).astype(jnp.bfloat16)


def project_head(rows, head):
    return lax.dot_general(
        rows, head, (((1,), (1,)), ((), ())), preferred_element_type=jnp.float32
    ).astype(jnp.bfloat16)


def end_kernel(level, rows, table, head, *refs):
    terms, (new, feats) = refs[:-2], refs[-2:]
    gate = table[2, pl.ds(level[0], 1), :]
    new[...] = fold(rows[REST:, :], gate, terms)
    feats[...] = project_head(new[...], head[...])


def end_rows(latents, levels, table, head, terms):
    rows, width = terms[0].shape
    channels = head.shape[0]
    return pl.pallas_call(
        end_kernel,
        in_specs=[smem()] + [vmem()] * (3 + len(terms)),
        out_specs=[vmem()] * 2,
        out_shape=[
            jax.ShapeDtypeStruct((rows, width), jnp.bfloat16),
            jax.ShapeDtypeStruct((rows, channels), jnp.bfloat16),
        ],
        compiler_params=params(8),
        cost_estimate=CHEAP,
    )(levels, latents, table, head, *terms)


def finish_kernel(level, rows, table, head, weight, earlier, end, end_feats, *refs):
    terms, (denoised, decoded) = refs[:-2], refs[-2:]
    gate = table[2, pl.ds(level[0], 1), :]
    new = fold(rows[:REST, :], gate, terms)
    denoised[:REST] = new
    denoised[REST:] = end[...]
    feats = project_head(new, head[...])
    sequence = jnp.concatenate([earlier[...], feats, end_feats[...]], 0)
    conv = jnp.zeros(decoded.shape, jnp.float32)
    for tap in range(3):
        begin = HALO - tap * SPOTS
        conv = conv + jnp.dot(
            sequence[begin : begin + TOK_DEV], weight[tap], preferred_element_type=jnp.float32
        )
    decoded[...] = (conv / (1.0 + jnp.exp(-conv))).astype(jnp.bfloat16)


def finish(latents, levels, table, head, weight, earlier, end, end_feats, terms):
    rows, width = latents.shape
    return pl.pallas_call(
        finish_kernel,
        in_specs=[smem()] + [vmem()] * (7 + len(terms)),
        out_specs=[vmem()] * 2,
        out_shape=[
            jax.ShapeDtypeStruct((rows, width), jnp.bfloat16),
            jax.ShapeDtypeStruct((rows, weight.shape[2]), jnp.bfloat16),
        ],
        compiler_params=params(8),
        cost_estimate=CHEAP,
    )(levels, latents, table, head, weight, earlier, end, end_feats, *terms)


def passes(relay, slot, place):
    return functools.reduce(
        lambda a, b: a | b, [place == at for at, kept in enumerate(relay) if kept == slot]
    )


def take(entry, tile, held, place):
    pairs, relay = entry
    if relay is not None:
        first, *others = sorted(set(relay))
        tile = held[first]
        for slot in others:
            tile = jnp.where(passes(relay, slot, place), held[slot], tile)
    return lax.ppermute(tile, "tok", lanes(pairs))


def spread(tile, table, place):
    held = []
    for entry in table:
        held.append(take(entry, tile, held, place))
    return held


def total(*terms):
    return functools.reduce(
        lambda a, b: a + b, [term.astype(jnp.float32) for term in terms]
    ).astype(jnp.bfloat16)


def passed_back(attended, weight, table, place, *wait):
    slots = len(table) + 1
    *mine, others, last = output(attended, weight, slots)
    last = over_core(after(last, *wait))
    others = jnp.split(over_core(others), slots - 1, 0)
    sent = [[a, b] for a, b in zip(mine[1:], others[1:] + [last])]
    for slot in reversed(range(len(table))):
        pairs, relay = table[slot]
        if relay is None:
            continue
        came = lax.ppermute(total(*sent[slot]), "tok", lanes(back(pairs)))
        for kept in set(relay):
            sent[kept].append(jnp.where(passes(relay, kept, place), came, jnp.bfloat16(0.0)))
    sent = [total(*terms) for terms, (_, relay) in zip(sent, table) if relay is None]
    return [mine[0], others[0]], sent


def sent_home(sent, table):
    direct = [pairs for pairs, relay in table if relay is None]
    return [
        lax.ppermute(term, "tok", lanes(back(pairs))) for term, pairs in zip(sent, direct)
    ]


def per_device(
    latents, levels, visible, frame_counts, modulation, w_qkv, qk_gain, w_out, w_head, conv_w
):
    current = latents[0]
    line = lax.axis_size("tok") // CORES
    place = lax.axis_index("tok") // CORES
    clip = lax.axis_index("span").astype(jnp.int32).reshape(1)
    table = routes(line)
    mods = modulation.transpose(1, 0, 2)
    weight = w_qkv.transpose(1, 0, 2)
    head = w_head.transpose(1, 0)

    lead, body = modulate(current, levels, mods)
    leads = [lead] + spread(lead, direct(table), place)
    held = spread(body, table[:-1], place)
    half = line // 2
    for part in (leads[:half], leads[half:]):
        pair = over_core(jnp.concatenate(part, 0))
        leads = leads + jnp.split(pair, half, 0)
    lead_part = project(leads, qk_gain, weight)
    packed, origins = from_earlier(lead_part[1:])

    last = take(table[-1], body, [after(tile, lead_part) for tile in held], place)
    across = over_core(jnp.concatenate([body] + held, 0))
    early_part = project([body] + held + [across], qk_gain, weight)
    last = after(last, early_part)
    late_part = project([last, over_core(last)], qk_gain, weight)
    parts = [lead_part, early_part, late_part]

    def at(lane, slot):
        if slot < line - 1:
            return 1, (lane * (line - 1) + slot) * BODY
        return 2, lane * BODY

    def attended(tail, parts):
        cuts = []
        for lane in range(CORES):
            for slot in range(line):
                part, begin = at(lane, slot)
                middle = begin + BODY - END
                if tail:
                    cuts.append((part, middle, middle + END))
                else:
                    begin_lead = (lane * line + slot) * LEAD
                    cuts.append((0, begin_lead, begin_lead + LEAD))
                    cuts.append((part, begin, middle))
        return attend(cuts, parts, packed, origins, clip, visible, frame_counts, w_out)

    own_end, end_sent = passed_back(*attended(True, parts), table, place)
    parts[-1] = after(parts[-1], own_end[0])
    own, sent = passed_back(*attended(False, parts), table, place, *end_sent)

    end_sums = own_end + sent_home(end_sent, table)
    end, end_feats = end_rows(current, levels, mods, head, end_sums)
    earlier = from_behind(end_feats[END - HALO :], "span", 1)
    sums = own + sent_home([after(term, end_feats) for term in sent], table)
    denoised, decoded = finish(
        current, levels, mods, head, conv_w, earlier, end, end_feats, sums
    )
    return (denoised[None], decoded[None])


def solution(mesh):
    placed = (
        P("span", "tok", None),
        P("span"),
        P(),
        P(),
        P(),
        P(None, None, "tok"),
        P(None, "tok"),
        P("tok", None),
        P(),
        P(),
    )
    return jax.shard_map(
        per_device,
        mesh=mesh,
        in_specs=placed,
        out_specs=(P("span", "tok", None), P("span", "tok", None)),
        check_vma=False,
    )
```

time: 176 us -> 103 us (0.59)
  waiting for transfers between devices: 87.7 us -> 35.7 us
  starting transfers between devices: 3.69 us -> 33.4 us
  Pallas kernels: 0 us -> 27.8 us
  matrix products: 24.1 us -> 0 us
  local copies, waits for them, and re-layouts: 23.9 us -> 1.06 us
  between operations: 17.3 us -> 1.6 us
  other arithmetic: 17.6 us -> 2.48 us
    reduce_scatter x1 -> x0, waiting for transfers between devices: 45.2 us -> none  [per_device(): lax.psum_scatter(head_terms(attended, w_out).astype(jnp.bfloat16), 'tok',...]
    all_gather x2 -> x0, waiting for transfers between devices: 41.5 us -> none  [the longest x1 28.8 us: per_device(): lax.all_gather(modulated, 'tok', axis=0, tiled=True)]
    ppermute x0 -> x23, waiting for transfers between devices: none -> 32.4 us  [the longest x4 12.2 us: sent_home(): lax.ppermute(term, 'tok', lanes(back(pairs)))]
    ppermute x0 -> x23, starting transfers between devices: none -> 30.4 us  [the longest x6 9.59 us: take(): return lax.ppermute(tile, 'tok', lanes(pairs))]
    pallas_call x0 -> x10, Pallas kernels: none -> 27.8 us  [the longest x3 15.9 us: project(): pl.pallas_call(functools.partial(project_kernel, len(tiles)), in_specs=[v...]
    dot_general x16 -> x0, matrix products: 24.1 us -> none  [the longest x1 9.77 us: per_device(): jnp.dot(lax.all_gather(modulated, 'tok', axis=0, tiled=True), w_flat, pre...]
    unnamed x20 -> x14, local copies, waits for them, and re-layouts: 18.8 us -> 0.04 us
    reduce_sum x11 -> x0, other arithmetic: 7.82 us -> none  [the longest x2 2.13 us: lookup_one(): return jnp.sum(jnp.where(matched, table, 0))]
  transfers between devices with their start and end apart: 4 -> 24, of which waited for: 4 -> 12; matrix products, arithmetic and copies ran while one was open for 16% -> 2% of each run, Pallas kernels for 0% -> 20%
where the time goes in v2:
time: 103 us; the launch traced here: 102 us
  waiting for transfers between devices  35.7 us (35%)
  starting transfers between devices  33.4 us (32%)
  Pallas kernels  27.8 us (27%)
  other arithmetic  2.48 us (2%)
  between operations  1.6 us (2%)
  local copies, waits for them, and re-layouts  1.06 us (1%)
    pallas_call x3, Pallas kernels, project(): pl.pallas_call(functools.partial(project_kernel, len(tiles)), in_specs=[v...  15.9 us
    ppermute x4, waiting for transfers between devices, sent_home(): lax.ppermute(term, 'tok', lanes(back(pairs)))  12.2 us
    ppermute x6, waiting for transfers between devices, take(): return lax.ppermute(tile, 'tok', lanes(pairs))  11.8 us
    ppermute x6, starting transfers between devices, take(): return lax.ppermute(tile, 'tok', lanes(pairs))  9.59 us
    ppermute x4, starting transfers between devices, sent_home(): lax.ppermute(term, 'tok', lanes(back(pairs)))  5.73 us
    pallas_call x2, Pallas kernels, attend(): pl.pallas_call(functools.partial(attend_kernel, cuts, len(parts), origins...  5.57 us
    ppermute x2, waiting for transfers between devices, passed_back(): came = lax.ppermute(total(*sent[slot]), 'tok', lanes(back(pairs)))  4.91 us
    ppermute x1, starting transfers between devices, from_earlier(): across = lax.ppermute(after(behind, beside), 'span', [(3, 2), (2, 3)])  4.35 us
  transfers between devices with their start and end apart: 24, of which 12 were waited for; matrix products, arithmetic and copies ran while one was open for 2% of the time, Pallas kernels for 20%

profile of v2, /device:TPU:4, one launch (start us, length us, event | category | flops | bytes accessed | tf_op | source)
XLA Modules:
  0.0 102.0 jit_solution(12855146936734519163)
XLA Ops:
  1.3 1.5 %shard_map.113 = (bf16[16,3584]{1,0:T(8,128)(2,1)S(1)}, bf16[48,3584]{1,0:T(8,128)(2,1)S(1)}) custom-call(s32[1]{0:T(128)S(6)} %copy.12.level, bf16[64,3584]{1,0:T(8,128)(2,1)} %bitcast.10, f32[3,16,3584]{2,1,0:T(8,128)} %bitcast.7), custom_call_target="tpu_custom_call" | custom-call | flops 1 | bytes 1 | tf_op jit(solution)/shard_map/pallas_call | solution.py:138
  2.8 3.7 %collective-permute-start.2 = (bf16[16,3584]{1,0:T(8,128)(2,1)S(1)}, bf16[16,3584]{1,0:T(8,128)(2,1)S(1)}, u32[]{:S(2)}, u32[]{:S(2)}) collective-permute-start(bf16[16,3584]{1,0:T(8,128)(2,1)S(1)} %get-tuple-element.32.refs_0_), channel_id=1, source_target_pairs={{4,2},{5,3},{6,0},{7,1},{0,6},{1,7},{2,4},{3,5},{12,10},{13,11},{1... | collective-permute-start | bytes 344072 | tf_op jit(solution)/shard_map/ppermute | solution.py:382
  6.5 0.0 collective-permute-start.1
  6.5 2.9 %collective-permute-start = (bf16[16,3584]{1,0:T(8,128)(2,1)S(1)}, bf16[16,3584]{1,0:T(8,128)(2,1)S(1)}, u32[]{:S(2)}, u32[]{:S(2)}) collective-permute-start(bf16[16,3584]{1,0:T(8,128)(2,1)S(1)} %get-tuple-element.32.refs_0_), channel_id=1, source_target_pairs={{0,4},{1,5},{4,6},{5,7},{6,2},{7,3},{2,0},{3,1},{8,12},{9,13},{12,... | collective-permute-start | bytes 344072 | tf_op jit(solution)/shard_map/ppermute | solution.py:382
  9.4 2.9 %collective-permute-start.5 = (bf16[48,3584]{1,0:T(8,128)(2,1)S(1)}, bf16[48,3584]{1,0:T(8,128)(2,1)S(1)}, u32[]{:S(2)}, u32[]{:S(2)}) collective-permute-start(bf16[48,3584]{1,0:T(8,128)(2,1)S(1)} %get-tuple-element.33.refs_0_), channel_id=1, source_target_pairs={{0,4},{1,5},{4,6},{5,7},{6,2},{7,3},{2,0},{3,1},{8,12},{9,13},{12,... | collective-permute-start | bytes 1032200 | tf_op jit(solution)/shard_map/ppermute | solution.py:382
  12.4 0.0 collective-permute-done.2.refs_3_
  12.4 4.8 %collective-permute-done.1.refs_2_ = bf16[16,3584]{1,0:T(8,128)(2,1)S(1)} collective-permute-done((bf16[16,3584]{1,0:T(8,128)(2,1)S(1)}, bf16[16,3584]{1,0:T(8,128)(2,1)S(1)}, u32[]{:S(2)}, u32[]{:S(2)}) %collective-permute-start.1) | collective-permute-done | bytes 114720 | tf_op jit(solution)/shard_map/ppermute | solution.py:382
  17.2 0.1 collective-permute-start.4
  17.3 0.5 collective-permute-start.3
  17.9 0.9 collective-permute-done.4
  18.8 0.3 collective-permute-done.3
  19.1 4.9 %shard_map.114.refs_0_ = bf16[3,128,512]{2,1,0:T(8,128)(2,1)S(1)} custom-call(bf16[16,3584]{1,0:T(8,128)(2,1)S(1)} %get-tuple-element.32.refs_0_, bf16[16,3584]{1,0:T(8,128)(2,1)S(1)} %collective-permute-done.refs_1_, bf16[16,3584]{1,0:T(8,128)(2,1)S(1)} %collective-permute-done.1.refs_2_, bf16[16,3584]{1,0:T(8,128)(2,1)S(1)} %collective-permute-done.2.refs_3_, ...), custom_call_target="tpu_custom_call" | custom-call | flops 1 | bytes 1 | tf_op jit(solution)/shard_map/pallas_call | solution.py:194
  24.0 6.9 %collective-permute-done.6.refs_2_ = bf16[48,3584]{1,0:T(8,128)(2,1)S(1)} collective-permute-done((bf16[48,3584]{1,0:T(8,128)(2,1)S(1)}, bf16[48,3584]{1,0:T(8,128)(2,1)S(1)}, u32[]{:S(2)}, u32[]{:S(2)}) %collective-permute-start.6) | collective-permute-done | bytes 344096 | tf_op jit(solution)/shard_map/ppermute | solution.py:382
  30.9 0.0 collective-permute-done.5.refs_1_
  30.9 0.1 pad_maximum_fusion
  31.0 0.1 collective-permute-start.7
  31.1 0.1 collective-permute-start.8
  31.2 1.3 %collective-permute-start.11 = (bf16[2,128,512]{2,1,0:T(8,128)(2,1)S(1)}, bf16[2,128,512]{2,1,0:T(8,128)(2,1)S(1)}, u32[]{:S(2)}, u32[]{:S(2)}) collective-permute-start(bf16[2,128,512]{2,1,0:T(8,128)(2,1)S(1)} %slice.8), channel_id=1, source_target_pairs={{0,16},{8,24},{1,17},{9,25},{2,18},{10,26},{3,19},{11,27},{4,20},{... | collective-permute-start | bytes 786440 | tf_op jit(solution)/shard_map/ppermute | solution.py:78
  32.5 3.4 %collective-permute-start.10 = (bf16[2,128,512]{2,1,0:T(8,128)(2,1)S(1)}, bf16[2,128,512]{2,1,0:T(8,128)(2,1)S(1)}, u32[]{:S(2)}, u32[]{:S(2)}) collective-permute-start(bf16[2,128,512]{2,1,0:T(8,128)(2,1)S(1)} %slice.8), channel_id=1, source_target_pairs={{0,8},{16,24},{1,9},{17,25},{2,10},{18,26},{3,11},{19,27},{4,12},{... | collective-permute-start | bytes 786440 | tf_op jit(solution)/shard_map/ppermute | solution.py:77
  35.9 0.0 collective-permute-done.7.refs_3_
  36.0 6.1 %shard_map.115.refs_1_ = bf16[3,288,512]{2,1,0:T(8,128)(2,1)S(1)} custom-call(bf16[48,3584]{1,0:T(8,128)(2,1)S(1)} %get-tuple-element.33.refs_0_, bf16[48,3584]{1,0:T(8,128)(2,1)S(1)} %collective-permute-done.5.refs_1_, bf16[48,3584]{1,0:T(8,128)(2,1)S(1)} %collective-permute-done.6.refs_2_, bf16[144,3584]{1,0:T(8,128)(2,1)S(1)} %collective-permute-done.7.refs_3_, ...), custom_call_target="tpu_custom_call" | custom-call | flops 1 | bytes 1 | tf_op jit(solution)/shard_map/pallas_call | solution.py:194
  42.1 0.0 collective-permute-done.8.refs_0_
  42.1 0.3 collective-permute-start.9
  42.3 0.0 collective-permute-done.10.refs_3_
  42.3 4.3 %collective-permute-start.12 = (bf16[2,128,512]{2,1,0:T(8,128)(2,1)S(1)}, bf16[2,128,512]{2,1,0:T(8,128)(2,1)S(1)}, u32[]{:S(2)}, u32[]{:S(2)}) collective-permute-start(bf16[2,128,512]{2,1,0:T(8,128)(2,1)S(1)} %collective-permute-done.11.refs_4_), channel_id=1, source_target_pairs={{24,16},{16,24},{25,17},{17,25},{26,18},{18,26},{27,19},{19,27},{2... | collective-permute-start | bytes 786440 | tf_op jit(solution)/shard_map/ppermute | solution.py:79
  46.7 0.0 copy-start.5
  46.7 0.0 copy-start.6
  46.7 0.0 collective-permute-done.9.refs_1_
  46.7 4.9 %shard_map.116.refs_2_ = bf16[3,96,512]{2,1,0:T(8,128)(2,1)S(1)} custom-call(bf16[48,3584]{1,0:T(8,128)(2,1)S(1)} %collective-permute-done.8.refs_0_, bf16[48,3584]{1,0:T(8,128)(2,1)S(1)} %collective-permute-done.9.refs_1_, f32[2,512]{1,0:T(2,128)S(1)} %copy-done.4, bf16[3,3584,512]{2,1,0:T(8,128)(2,1)} %bitcast.17), custom_call_target="tpu_custom_call" | custom-call | flops 1 | bytes 1 | tf_op jit(solution)/shard_map/pallas_call | solution.py:194
  51.7 1.0 %collective-permute-done.12.refs_5_ = bf16[2,128,512]{2,1,0:T(8,128)(2,1)S(1)} collective-permute-done((bf16[2,128,512]{2,1,0:T(8,128)(2,1)S(1)}, bf16[2,128,512]{2,1,0:T(8,128)(2,1)S(1)}, u32[]{:S(2)}, u32[]{:S(2)}) %collective-permute-start.12) | collective-permute-done | bytes 262176 | tf_op jit(solution)/shard_map/ppermute | solution.py:79
  52.7 2.8 %shard_map.117 = (bf16[256,512]{1,0:T(8,128)(2,1)S(1)}, bf16[512,3584]{1,0:T(8,128)(2,1)S(1)}) custom-call(s32[1]{0:T(128)} %bitcast.3.clip, s32[4,4]{1,0:T(4,128)S(1)} %copy-done.5, s32[4]{0:T(128)S(1)} %copy-done.6, bf16[3,128,512]{2,1,0:T(8,128)(2,1)S(1)} %shard_map.114.refs_0_, bf16[3,288,512]{2,1,0:T(8,128)(2,1)S(1)} %shard_map.115.refs_1_, ...), custom_call_target="tpu_custom_call" | custom-call | flops 1 | bytes 1 | tf_op jit(solution)/shard_map/pallas_call | solution.py:262
  55.5 2.0 %shard_map.118 = (bf16[32,3584]{1,0:T(8,128)(2,1)S(1)}, bf16[32,3584]{1,0:T(8,128)(2,1)S(1)}, bf16[32,3584]{1,0:T(8,128)(2,1)S(1)}, bf16[32,3584]{1,0:T(8,128)(2...) custom-call(bf16[256,512]{1,0:T(8,128)(2,1)S(1)} %get-tuple-element.38.attended, ...), custom_call_target="tpu_custom_call" | custom-call | flops 1 | bytes 1 | tf_op jit(solution)/shard_map/pallas_call | solution.py:293
  57.6 0.5 collective-permute-start.13
  58.1 1.3 %collective-permute-done.14 = bf16[32,3584]{1,0:T(8,128)(2,1)S(1)} collective-permute-done((bf16[32,3584]{1,0:T(8,128)(2,1)S(1)}, bf16[32,3584]{1,0:T(8,128)(2,1)S(1)}, u32[]{:S(2)}, u32[]{:S(2)}) %collective-permute-start.14) | collective-permute-done | bytes 229408 | tf_op jit(solution)/shard_map/ppermute | solution.py:62
  59.3 0.7 add_convert_fusion.5
  60.1 2.0 %collective-permute-start.15 = (bf16[32,3584]{1,0:T(8,128)(2,1)}, bf16[32,3584]{1,0:T(8,128)(2,1)}, u32[]{:S(2)}, u32[]{:S(2)}) collective-permute-start(bf16[32,3584]{1,0:T(8,128)(2,1)} %add_convert_fusion.5), channel_id=1, source_target_pairs={{2,0},{3,1},{0,2},{1,3},{6,4},{7,5},{4,6},{5,7},{10,8},{11,9},{8,1... | collective-permute-start | bytes 688136 | tf_op jit(solution)/shard_map/ppermute | solution.py:408
  62.1 2.8 %shard_map.120 = (bf16[256,512]{1,0:T(8,128)(2,1)S(1)}, bf16[512,3584]{1,0:T(8,128)(2,1)S(1)}) custom-call(s32[1]{0:T(128)} %bitcast.3.clip, s32[4,4]{1,0:T(4,128)S(1)} %copy-done.5, s32[4]{0:T(128)S(1)} %copy-done.6, bf16[3,128,512]{2,1,0:T(8,128)(2,1)S(1)} %shard_map.114.refs_0_, bf16[3,288,512]{2,1,0:T(8,128)(2,1)S(1)} %shard_map.115.refs_1_, ...), custom_call_target="tpu_custom_call" | custom-call | flops 1 | bytes 1 | tf_op jit(solution)/shard_map/pallas_call | solution.py:262
  64.9 1.1 %shard_map.121 = (bf16[32,3584]{1,0:T(8,128)(2,1)S(1)}, bf16[32,3584]{1,0:T(8,128)(2,1)S(1)}, bf16[32,3584]{1,0:T(8,128)(2,1)S(1)}, bf16[32,3584]{1,0:T(8,128)(2...) custom-call(bf16[256,512]{1,0:T(8,128)(2,1)S(1)} %get-tuple-element.49.attended, ...), custom_call_target="tpu_custom_call" | custom-call | flops 1 | bytes 1 | tf_op jit(solution)/shard_map/pallas_call | solution.py:293
  66.0 0.0 copy-start
  66.0 0.0 copy-start.1
  66.0 0.0 copy-start.2
  66.0 2.3 %collective-permute-done.15 = bf16[32,3584]{1,0:T(8,128)(2,1)} collective-permute-done((bf16[32,3584]{1,0:T(8,128)(2,1)}, bf16[32,3584]{1,0:T(8,128)(2,1)}, u32[]{:S(2)}, u32[]{:S(2)}) %collective-permute-start.15) | collective-permute-done | bytes 229408 | tf_op jit(solution)/shard_map/ppermute | solution.py:408
  68.3 1.3 %add_convert_fusion.3 = (bf16[32,3584]{1,0:T(8,128)(2,1)S(1)}, bf16[32,3584]{1,0:T(8,128)(2,1)S(1)}) fusion(bf16[32,3584]{1,0:T(8,128)(2,1)S(1)} %get-tuple-element.45, bf16[96,3584]{1,0:T(8,128)(2,1)} %collective-permute-done.13, bf16[32,3584]{1,0:T(8,128)(2,1)} %collective-permute-done.15, pred[]{:T(512)S(6)} %or.4, pred[]{:T(512)S(6)} %or.10, ...), kind=kLoop, calls=%fused_computation.4 | loop fusion | flops 1605632 | bytes 1605634 | tf_op jit(solution)/shard_map/convert_element_type | solution.py:395
  69.7 0.1 collective-permute-start.20
  69.7 0.5 collective-permute-start.19
  70.2 2.8 %collective-permute-start.17 = (bf16[32,3584]{1,0:T(8,128)(2,1)S(1)}, bf16[32,3584]{1,0:T(8,128)(2,1)S(1)}, u32[]{:S(2)}, u32[]{:S(2)}) collective-permute-start(bf16[32,3584]{1,0:T(8,128)(2,1)S(1)} %get-tuple-element.64), channel_id=1, source_target_pairs={{2,0},{3,1},{6,2},{7,3},{4,6},{5,7},{0,4},{1,5},{10,8},{11,9},{14,... | collective-permute-start | bytes 688136 | tf_op jit(solution)/shard_map/ppermute | solution.py:418
  73.0 0.0 collective-permute-start.16
  73.0 0.0 collective-permute-done.20
  73.0 0.1 add_convert_fusion.2
  73.1 2.0 %collective-permute-start.21 = (bf16[32,3584]{1,0:T(8,128)(2,1)S(1)}, bf16[32,3584]{1,0:T(8,128)(2,1)S(1)}, u32[]{:S(2)}, u32[]{:S(2)}) collective-permute-start(bf16[32,3584]{1,0:T(8,128)(2,1)S(1)} %add_convert_fusion.2), channel_id=1, source_target_pairs={{2,0},{3,1},{0,2},{1,3},{6,4},{7,5},{4,6},{5,7},{10,8},{11,9},{8,1... | collective-permute-start | bytes 688136 | tf_op jit(solution)/shard_map/ppermute | solution.py:408
  75.0 1.0 split.44.refs_1_
  76.0 3.0 %collective-permute-done.17.refs_3_ = bf16[32,3584]{1,0:T(8,128)(2,1)S(1)} collective-permute-done((bf16[32,3584]{1,0:T(8,128)(2,1)S(1)}, bf16[32,3584]{1,0:T(8,128)(2,1)S(1)}, u32[]{:S(2)}, u32[]{:S(2)}) %collective-permute-start.17) | collective-permute-done | bytes 229408 | tf_op jit(solution)/shard_map/ppermute | solution.py:418
  79.0 5.9 %collective-permute-done.16.refs_2_ = bf16[32,3584]{1,0:T(8,128)(2,1)S(1)} collective-permute-done((bf16[32,3584]{1,0:T(8,128)(2,1)S(1)}, bf16[32,3584]{1,0:T(8,128)(2,1)S(1)}, u32[]{:S(2)}, u32[]{:S(2)}) %collective-permute-start.16) | collective-permute-done | bytes 229408 | tf_op jit(solution)/shard_map/ppermute | solution.py:418
  84.9 0.0 copy-start.3
  84.9 0.4 shard_map.119
  85.3 0.0 collective-permute-done.19
  85.3 2.6 %collective-permute-done.21 = bf16[32,3584]{1,0:T(8,128)(2,1)S(1)} collective-permute-done((bf16[32,3584]{1,0:T(8,128)(2,1)S(1)}, bf16[32,3584]{1,0:T(8,128)(2,1)S(1)}, u32[]{:S(2)}, u32[]{:S(2)}) %collective-permute-start.21) | collective-permute-done | bytes 229408 | tf_op jit(solution)/shard_map/ppermute | solution.py:408
  88.0 0.2 add_convert_fusion
  88.2 2.5 %collective-permute-start.22 = (bf16[32,3584]{1,0:T(8,128)(2,1)S(1)}, bf16[32,3584]{1,0:T(8,128)(2,1)S(1)}, u32[]{:S(2)}, u32[]{:S(2)}) collective-permute-start(bf16[32,3584]{1,0:T(8,128)(2,1)S(1)} %get-tuple-element.57), channel_id=1, source_target_pairs={{4,0},{5,1},{6,4},{7,5},{2,6},{3,7},{0,2},{1,3},{12,8},{13,9},{14,... | collective-permute-start | bytes 688136 | tf_op jit(solution)/shard_map/ppermute | solution.py:418
  90.7 0.4 collective-permute-start.23
  91.1 3.0 %collective-permute-start.18 = (bf16[16,96]{1,0:T(8,128)(2,1)S(1)}, bf16[16,96]{1,0:T(8,128)(2,1)S(1)}, u32[]{:S(2)}, u32[]{:S(2)}) collective-permute-start(bf16[16,96]{1,0:T(8,128)(2,1)S(1)} %slice.7), channel_id=1, source_target_pairs={{0,8},{8,16},{16,24},{1,9},{9,17},{17,25},{2,10},{10,18},{18,26},{... | collective-permute-start | bytes 9224 | tf_op jit(solution)/shard_map/ppermute | solution.py:68
  94.2 3.4 %collective-permute-done.18.earlier = bf16[16,96]{1,0:T(8,128)(2,1)S(1)} collective-permute-done((bf16[16,96]{1,0:T(8,128)(2,1)S(1)}, bf16[16,96]{1,0:T(8,128)(2,1)S(1)}, u32[]{:S(2)}, u32[]{:S(2)}) %collective-permute-start.18) | collective-permute-done | bytes 3104 | tf_op jit(solution)/shard_map/ppermute | solution.py:68
  97.5 3.2 %collective-permute-done.23.refs_3_ = bf16[32,3584]{1,0:T(8,128)(2,1)S(1)} collective-permute-done((bf16[32,3584]{1,0:T(8,128)(2,1)S(1)}, bf16[32,3584]{1,0:T(8,128)(2,1)S(1)}, u32[]{:S(2)}, u32[]{:S(2)}) %collective-permute-start.23) | collective-permute-done | bytes 229408 | tf_op jit(solution)/shard_map/ppermute | solution.py:418
  100.8 1.3 %shard_map.122 = (bf16[64,3584]{1,0:T(8,128)(2,1)}, bf16[64,384]{1,0:T(8,128)(2,1)}) custom-call(s32[1]{0:T(128)S(6)} %copy.12.level, bf16[64,3584]{1,0:T(8,128)(2,1)S(1)} %bitcast.12, f32[3,16,3584]{2,1,0:T(8,128)S(1)} %bitcast.9, bf16[96,3584]{1,0:T(8,128)(2,1)S(1)} %bitcast.14, bf16[3,96,384]{2,1,0:T(8,128)(2,1)S(1)} %copy-done.3, ...), custom_call_target="tpu_custom_call" | custom-call | flops 1 | bytes 1 | tf_op jit(solution)/shard_map/pallas_call | solution.py:356
  (22 shorter events, 0.2 us)
Async XLA Ops:
  0.6 18.5 %copy-start.4 = (f32[2,512]{1,0:T(2,128)S(1)}, f32[2,512]{1,0:T(2,128)}, u32[]{:S(2)}) copy-start(f32[2,512]{1,0:T(2,128)} %refs_2_.1) | copy-start | bytes 12292
  2.8 9.5 %collective-permute-start.2 = (bf16[16,3584]{1,0:T(8,128)(2,1)S(1)}, bf16[16,3584]{1,0:T(8,128)(2,1)S(1)}, u32[]{:S(2)}, u32[]{:S(2)}) collective-permute-start(bf16[16,3584]{1,0:T(8,128)(2,1)S(1)} %get-tuple-element.32.refs_0_), channel_id=1, source_target_pairs={{4,2},{5,3},{6,0},{7,1},{0,6},{1,7},{2,4},{3,5},{12,10},{13,11},{1... | collective-permute-start | bytes 344072 | tf_op jit(solution)/shard_map/ppermute | solution.py:382
  6.5 10.7 %collective-permute-start.1 = (bf16[16,3584]{1,0:T(8,128)(2,1)S(1)}, bf16[16,3584]{1,0:T(8,128)(2,1)S(1)}, u32[]{:S(2)}, u32[]{:S(2)}) collective-permute-start(bf16[16,3584]{1,0:T(8,128)(2,1)S(1)} %get-tuple-element.32.refs_0_), channel_id=1, source_target_pairs={{0,2},{1,3},{2,6},{3,7},{6,4},{7,5},{4,0},{5,1},{8,10},{9,11},{10,... | collective-permute-start | bytes 344072 | tf_op jit(solution)/shard_map/ppermute | solution.py:382
  6.5 10.8 %collective-permute-start = (bf16[16,3584]{1,0:T(8,128)(2,1)S(1)}, bf16[16,3584]{1,0:T(8,128)(2,1)S(1)}, u32[]{:S(2)}, u32[]{:S(2)}) collective-permute-start(bf16[16,3584]{1,0:T(8,128)(2,1)S(1)} %get-tuple-element.32.refs_0_), channel_id=1, source_target_pairs={{0,4},{1,5},{4,6},{5,7},{6,2},{7,3},{2,0},{3,1},{8,12},{9,13},{12,... | collective-permute-start | bytes 344072 | tf_op jit(solution)/shard_map/ppermute | solution.py:382
  9.4 21.5 %collective-permute-start.6 = (bf16[48,3584]{1,0:T(8,128)(2,1)S(1)}, bf16[48,3584]{1,0:T(8,128)(2,1)S(1)}, u32[]{:S(2)}, u32[]{:S(2)}) collective-permute-start(bf16[48,3584]{1,0:T(8,128)(2,1)S(1)} %get-tuple-element.33.refs_0_), channel_id=1, source_target_pairs={{0,2},{1,3},{2,6},{3,7},{6,4},{7,5},{4,0},{5,1},{8,10},{9,11},{10,... | collective-permute-start | bytes 1032200 | tf_op jit(solution)/shard_map/ppermute | solution.py:382
  9.4 21.5 %collective-permute-start.5 = (bf16[48,3584]{1,0:T(8,128)(2,1)S(1)}, bf16[48,3584]{1,0:T(8,128)(2,1)S(1)}, u32[]{:S(2)}, u32[]{:S(2)}) collective-permute-start(bf16[48,3584]{1,0:T(8,128)(2,1)S(1)} %get-tuple-element.33.refs_0_), channel_id=1, source_target_pairs={{0,4},{1,5},{4,6},{5,7},{6,2},{7,3},{2,0},{3,1},{8,12},{9,13},{12,... | collective-permute-start | bytes 1032200 | tf_op jit(solution)/shard_map/ppermute | solution.py:382
  17.2 1.6 %collective-permute-start.4 = (bf16[32,3584]{1,0:T(8,128)(2,1)S(1)}, bf16[32,3584]{1,0:T(8,128)(2,1)S(1)}, u32[]{:S(2)}, u32[]{:S(2)}) collective-permute-start(bf16[32,3584]{1,0:T(8,128)(2,1)S(1)} %pad_maximum_fusion.2), channel_id=1, source_target_pairs={{0,1},{1,0},{2,3},{3,2},{4,5},{5,4},{6,7},{7,6},{8,9},{9,8},{10,11... | collective-permute-start | bytes 688136 | tf_op jit(solution)/shard_map/ppermute | solution.py:62
  17.3 1.8 %collective-permute-start.3 = (bf16[32,3584]{1,0:T(8,128)(2,1)S(1)}, bf16[32,3584]{1,0:T(8,128)(2,1)S(1)}, u32[]{:S(2)}, u32[]{:S(2)}) collective-permute-start(bf16[32,3584]{1,0:T(8,128)(2,1)S(1)} %pad_maximum_fusion.1), channel_id=1, source_target_pairs={{0,1},{1,0},{2,3},{3,2},{4,5},{5,4},{6,7},{7,6},{8,9},{9,8},{10,11... | collective-permute-start | bytes 688136 | tf_op jit(solution)/shard_map/ppermute | solution.py:62
  31.0 5.0 %collective-permute-start.7 = (bf16[144,3584]{1,0:T(8,128)(2,1)S(1)}, bf16[144,3584]{1,0:T(8,128)(2,1)S(1)}, u32[]{:S(2)}, u32[]{:S(2)}) collective-permute-start(bf16[144,3584]{1,0:T(8,128)(2,1)S(1)} %pad_maximum_fusion), channel_id=1, source_target_pairs={{0,1},{1,0},{2,3},{3,2},{4,5},{5,4},{6,7},{7,6},{8,9},{9,8},{10,11... | collective-permute-start | bytes 3096584 | tf_op jit(solution)/shard_map/ppermute | solution.py:62
  31.1 10.9 %collective-permute-start.8 = (bf16[48,3584]{1,0:T(8,128)(2,1)S(1)}, bf16[48,3584]{1,0:T(8,128)(2,1)S(1)}, u32[]{:S(2)}, u32[]{:S(2)}) collective-permute-start(bf16[48,3584]{1,0:T(8,128)(2,1)S(1)} %broadcast_select_fusion), channel_id=1, source_target_pairs={{0,2},{1,3},{2,0},{3,1},{4,6},{5,7},{6,4},{7,5},{8,10},{9,11},{10,... | collective-permute-start | bytes 1032200 | tf_op jit(solution)/shard_map/ppermute | solution.py:382
  31.2 11.1 %collective-permute-start.11 = (bf16[2,128,512]{2,1,0:T(8,128)(2,1)S(1)}, bf16[2,128,512]{2,1,0:T(8,128)(2,1)S(1)}, u32[]{:S(2)}, u32[]{:S(2)}) collective-permute-start(bf16[2,128,512]{2,1,0:T(8,128)(2,1)S(1)} %slice.8), channel_id=1, source_target_pairs={{0,16},{8,24},{1,17},{9,25},{2,18},{10,26},{3,19},{11,27},{4,20},{... | collective-permute-start | bytes 786440 | tf_op jit(solution)/shard_map/ppermute | solution.py:78
  32.5 9.8 %collective-permute-start.10 = (bf16[2,128,512]{2,1,0:T(8,128)(2,1)S(1)}, bf16[2,128,512]{2,1,0:T(8,128)(2,1)S(1)}, u32[]{:S(2)}, u32[]{:S(2)}) collective-permute-start(bf16[2,128,512]{2,1,0:T(8,128)(2,1)S(1)} %slice.8), channel_id=1, source_target_pairs={{0,8},{16,24},{1,9},{17,25},{2,10},{18,26},{3,11},{19,27},{4,12},{... | collective-permute-start | bytes 786440 | tf_op jit(solution)/shard_map/ppermute | solution.py:77
  42.1 4.7 %collective-permute-start.9 = (bf16[48,3584]{1,0:T(8,128)(2,1)S(1)}, bf16[48,3584]{1,0:T(8,128)(2,1)S(1)}, u32[]{:S(2)}, u32[]{:S(2)}) collective-permute-start(bf16[48,3584]{1,0:T(8,128)(2,1)S(1)} %collective-permute-done.8.refs_0_), channel_id=1, source_target_pairs={{0,1},{1,0},{2,3},{3,2},{4,5},{5,4},{6,7},{7,6},{8,9},{9,8},{10,11... | collective-permute-start | bytes 1032200 | tf_op jit(solution)/shard_map/ppermute | solution.py:62
  42.3 10.4 %collective-permute-start.12 = (bf16[2,128,512]{2,1,0:T(8,128)(2,1)S(1)}, bf16[2,128,512]{2,1,0:T(8,128)(2,1)S(1)}, u32[]{:S(2)}, u32[]{:S(2)}) collective-permute-start(bf16[2,128,512]{2,1,0:T(8,128)(2,1)S(1)} %collective-permute-done.11.refs_4_), channel_id=1, source_target_pairs={{24,16},{16,24},{25,17},{17,25},{26,18},{18,26},{27,19},{19,27},{2... | collective-permute-start | bytes 786440 | tf_op jit(solution)/shard_map/ppermute | solution.py:79
  46.7 6.0 %copy-start.5 = (s32[4,4]{1,0:T(4,128)S(1)}, s32[4,4]{1,0:T(4,128)}, u32[]{:S(2)}) copy-start(s32[4,4]{1,0:T(4,128)} %visible.3) | copy-start | bytes 196
  46.7 6.0 %copy-start.6 = (s32[4]{0:T(128)S(1)}, s32[4]{0:T(128)}, u32[]{:S(2)}) copy-start(s32[4]{0:T(128)} %counts.3) | copy-start | bytes 52
  57.5 1.8 %collective-permute-start.14 = (bf16[32,3584]{1,0:T(8,128)(2,1)S(1)}, bf16[32,3584]{1,0:T(8,128)(2,1)S(1)}, u32[]{:S(2)}, u32[]{:S(2)}) collective-permute-start(bf16[32,3584]{1,0:T(8,128)(2,1)S(1)} %get-tuple-element.44), channel_id=1, source_target_pairs={{0,1},{1,0},{2,3},{3,2},{4,5},{5,4},{6,7},{7,6},{8,9},{9,8},{10,11... | collective-permute-start | bytes 688136 | tf_op jit(solution)/shard_map/ppermute | solution.py:62
  57.6 10.8 %collective-permute-start.13 = (bf16[96,3584]{1,0:T(8,128)(2,1)}, bf16[96,3584]{1,0:T(8,128)(2,1)}, u32[]{:S(2)}, u32[]{:S(2)}) collective-permute-start(bf16[96,3584]{1,0:T(8,128)(2,1)} %get-tuple-element.41), channel_id=1, source_target_pairs={{0,1},{1,0},{2,3},{3,2},{4,5},{5,4},{6,7},{7,6},{8,9},{9,8},{10,11... | collective-permute-start | bytes 2064392 | tf_op jit(solution)/shard_map/ppermute | solution.py:62
  60.1 8.2 %collective-permute-start.15 = (bf16[32,3584]{1,0:T(8,128)(2,1)}, bf16[32,3584]{1,0:T(8,128)(2,1)}, u32[]{:S(2)}, u32[]{:S(2)}) collective-permute-start(bf16[32,3584]{1,0:T(8,128)(2,1)} %add_convert_fusion.5), channel_id=1, source_target_pairs={{2,0},{3,1},{0,2},{1,3},{6,4},{7,5},{4,6},{5,7},{10,8},{11,9},{8,1... | collective-permute-start | bytes 688136 | tf_op jit(solution)/shard_map/ppermute | solution.py:408
  66.0 18.9 %copy-start = (f32[16,3,3584]{2,0,1:T(8,128)S(1)}, f32[16,3,3584]{2,0,1:T(8,128)}, u32[]{:S(2)}) copy-start(f32[16,3,3584]{2,0,1:T(8,128)} %param.14) | copy-start | bytes 2064388
  66.0 18.9 %copy-start.1 = (bf16[1,64,3584]{2,1,0:T(8,128)(2,1)S(1)}, bf16[1,64,3584]{2,1,0:T(8,128)(2,1)}, u32[]{:S(2)}) copy-start(bf16[1,64,3584]{2,1,0:T(8,128)(2,1)} %param.10) | copy-start | bytes 1376260
  66.0 18.9 %copy-start.2 = (bf16[3584,96]{0,1:T(8,128)(2,1)S(1)}, bf16[3584,96]{0,1:T(8,128)(2,1)}, u32[]{:S(2)}) copy-start(bf16[3584,96]{0,1:T(8,128)(2,1)} %param.18) | copy-start | bytes 2064388
  69.7 3.3 %collective-permute-start.20 = (bf16[32,3584]{1,0:T(8,128)(2,1)S(1)}, bf16[32,3584]{1,0:T(8,128)(2,1)S(1)}, u32[]{:S(2)}, u32[]{:S(2)}) collective-permute-start(bf16[32,3584]{1,0:T(8,128)(2,1)S(1)} %get-tuple-element.56), channel_id=1, source_target_pairs={{0,1},{1,0},{2,3},{3,2},{4,5},{5,4},{6,7},{7,6},{8,9},{9,8},{10,11... | collective-permute-start | bytes 688136 | tf_op jit(solution)/shard_map/ppermute | solution.py:62
  69.7 15.6 %collective-permute-start.19 = (bf16[96,3584]{1,0:T(8,128)(2,1)S(1)}, bf16[96,3584]{1,0:T(8,128)(2,1)S(1)}, u32[]{:S(2)}, u32[]{:S(2)}) collective-permute-start(bf16[96,3584]{1,0:T(8,128)(2,1)S(1)} %get-tuple-element.52), channel_id=1, source_target_pairs={{0,1},{1,0},{2,3},{3,2},{4,5},{5,4},{6,7},{7,6},{8,9},{9,8},{10,11... | collective-permute-start | bytes 2064392 | tf_op jit(solution)/shard_map/ppermute | solution.py:62
  70.2 8.8 %collective-permute-start.17 = (bf16[32,3584]{1,0:T(8,128)(2,1)S(1)}, bf16[32,3584]{1,0:T(8,128)(2,1)S(1)}, u32[]{:S(2)}, u32[]{:S(2)}) collective-permute-start(bf16[32,3584]{1,0:T(8,128)(2,1)S(1)} %get-tuple-element.64), channel_id=1, source_target_pairs={{2,0},{3,1},{6,2},{7,3},{4,6},{5,7},{0,4},{1,5},{10,8},{11,9},{14,... | collective-permute-start | bytes 688136 | tf_op jit(solution)/shard_map/ppermute | solution.py:418
  73.0 11.9 %collective-permute-start.16 = (bf16[32,3584]{1,0:T(8,128)(2,1)S(1)}, bf16[32,3584]{1,0:T(8,128)(2,1)S(1)}, u32[]{:S(2)}, u32[]{:S(2)}) collective-permute-start(bf16[32,3584]{1,0:T(8,128)(2,1)S(1)} %get-tuple-element.65), channel_id=1, source_target_pairs={{4,0},{5,1},{6,4},{7,5},{2,6},{3,7},{0,2},{1,3},{12,8},{13,9},{14,... | collective-permute-start | bytes 688136 | tf_op jit(solution)/shard_map/ppermute | solution.py:418
  73.1 14.9 %collective-permute-start.21 = (bf16[32,3584]{1,0:T(8,128)(2,1)S(1)}, bf16[32,3584]{1,0:T(8,128)(2,1)S(1)}, u32[]{:S(2)}, u32[]{:S(2)}) collective-permute-start(bf16[32,3584]{1,0:T(8,128)(2,1)S(1)} %add_convert_fusion.2), channel_id=1, source_target_pairs={{2,0},{3,1},{0,2},{1,3},{6,4},{7,5},{4,6},{5,7},{10,8},{11,9},{8,1... | collective-permute-start | bytes 688136 | tf_op jit(solution)/shard_map/ppermute | solution.py:408
  84.9 15.9 %copy-start.3 = (bf16[3,96,384]{2,1,0:T(8,128)(2,1)S(1)}, bf16[3,96,384]{2,1,0:T(8,128)(2,1)}, u32[]{:S(2)}) copy-start(bf16[3,96,384]{2,1,0:T(8,128)(2,1)} %weight.1) | copy-start | bytes 663556
  88.2 9.4 %collective-permute-start.22 = (bf16[32,3584]{1,0:T(8,128)(2,1)S(1)}, bf16[32,3584]{1,0:T(8,128)(2,1)S(1)}, u32[]{:S(2)}, u32[]{:S(2)}) collective-permute-start(bf16[32,3584]{1,0:T(8,128)(2,1)S(1)} %get-tuple-element.57), channel_id=1, source_target_pairs={{4,0},{5,1},{6,4},{7,5},{2,6},{3,7},{0,2},{1,3},{12,8},{13,9},{14,... | collective-permute-start | bytes 688136 | tf_op jit(solution)/shard_map/ppermute | solution.py:418
  90.7 10.1 %collective-permute-start.23 = (bf16[32,3584]{1,0:T(8,128)(2,1)S(1)}, bf16[32,3584]{1,0:T(8,128)(2,1)S(1)}, u32[]{:S(2)}, u32[]{:S(2)}) collective-permute-start(bf16[32,3584]{1,0:T(8,128)(2,1)S(1)} %get-tuple-element.59), channel_id=1, source_target_pairs={{2,0},{3,1},{6,2},{7,3},{4,6},{5,7},{0,4},{1,5},{10,8},{11,9},{14,... | collective-permute-start | bytes 688136 | tf_op jit(solution)/shard_map/ppermute | solution.py:418
  91.1 6.4 %collective-permute-start.18 = (bf16[16,96]{1,0:T(8,128)(2,1)S(1)}, bf16[16,96]{1,0:T(8,128)(2,1)S(1)}, u32[]{:S(2)}, u32[]{:S(2)}) collective-permute-start(bf16[16,96]{1,0:T(8,128)(2,1)S(1)} %slice.7), channel_id=1, source_target_pairs={{0,8},{8,16},{16,24},{1,9},{9,17},{17,25},{2,10},{10,18},{18,26},{... | collective-permute-start | bytes 9224 | tf_op jit(solution)/shard_map/ppermute | solution.py:68

commit v3 on v2

--- a/solution.py
+++ b/solution.py
@@ -301,7 +301,8 @@
 
 
 def fold(rows, gate, terms):
-    total = functools.reduce(lambda a, b: a + b, [term[...].astype(jnp.float32) for term in terms])
+    size = rows.shape[0]
+    total = functools.reduce(lambda a, b: a + b, [term[:size].astype(jnp.float32) for term in terms])
     return (rows.astype(jnp.float32) + gate * total).astype(jnp.bfloat16)
 
 
@@ -389,27 +390,56 @@
     return held
 
 
-def total(*terms):
-    return functools.reduce(
-        lambda a, b: a + b, [term.astype(jnp.float32) for term in terms]
-    ).astype(jnp.bfloat16)
-
-
-def passed_back(attended, weight, table, place, *wait):
-    slots = len(table) + 1
-    *mine, others, last = output(attended, weight, slots)
-    last = over_core(after(last, *wait))
-    others = jnp.split(over_core(others), slots - 1, 0)
-    sent = [[a, b] for a, b in zip(mine[1:], others[1:] + [last])]
-    for slot in reversed(range(len(table))):
-        pairs, relay = table[slot]
-        if relay is None:
+def merge_kernel(groups, count, place, *refs):
+    arrays, outs = refs[:count], refs[count:]
+    for out, group in zip(outs, groups):
+        rows = out.shape[0]
+        sums = 0.0
+        for which, block, places in group:
+            term = arrays[which][block * rows : (block + 1) * rows].astype(jnp.float32)
+            if places is not None:
+                here = functools.reduce(lambda a, b: a | b, [place[0] == p for p in places])
+                term = jnp.where(here, term, 0.0)
+            sums = sums + term
+        out[...] = sums.astype(jnp.bfloat16)
+
+
+def merge(place, arrays, groups):
+    unit = arrays[0].shape
+    return pl.pallas_call(
+        functools.partial(merge_kernel, groups, len(arrays)),
+        in_specs=[smem()] + [vmem()] * len(arrays),
+        out_specs=[vmem()] * len(groups),
+        out_shape=[jax.ShapeDtypeStruct(unit, jnp.bfloat16)] * len(groups),
+        compiler_params=params(8),
+        cost_estimate=CHEAP,
+    )(place, *arrays)
+
+
+def passed_back(terms, table, place):
+    *mine, others, last = terms
+    last = over_core(last)
+    others = over_core(others)
+    final = len(table) - 1
+    passed = []
+    for slot, (pairs, relay) in enumerate(table):
+        if relay is not None:
+            theirs = (last, 0) if slot == final else (others, slot + 1)
+            (sums,) = merge(place, [mine[slot + 1], theirs[0]], [[(0, 0, None), (1, theirs[1], None)]])
+            came = lax.ppermute(sums, "tok", lanes(back(pairs)))
+            passed.append((came, relay))
+    arrays = mine[1:] + [others, last] + [came for came, _ in passed]
+    groups = []
+    for slot, (_, relay) in enumerate(table):
+        if relay is not None:
             continue
-        came = lax.ppermute(total(*sent[slot]), "tok", lanes(back(pairs)))
-        for kept in set(relay):
-            sent[kept].append(jnp.where(passes(relay, kept, place), came, jnp.bfloat16(0.0)))
-    sent = [total(*terms) for terms, (_, relay) in zip(sent, table) if relay is None]
-    return [mine[0], others[0]], sent
+        group = [(slot, 0, None)]
+        group.append((final + 2, 0, None) if slot == final else (final + 1, slot + 1, None))
+        for i, (_, kept) in enumerate(passed):
+            places = [at for at, which in enumerate(kept) if which == slot]
+            group.append((final + 3 + i, 0, places))
+        groups.append(group)
+    return [mine[0], others], merge(place, arrays, groups)
 
 
 def sent_home(sent, table):
@@ -442,7 +472,8 @@
     packed, origins = from_earlier(lead_part[1:])
 
     last = take(table[-1], body, [after(tile, lead_part) for tile in held], place)
-    across = over_core(jnp.concatenate([body] + held, 0))
+    first = [body] + [after(tile, lead_part) for tile in held]
+    across = over_core(jnp.concatenate(first, 0))
     early_part = project([body] + held + [across], qk_gain, weight)
     last = after(last, early_part)
     late_part = project([last, over_core(last)], qk_gain, weight)
@@ -467,9 +498,11 @@
                     cuts.append((part, begin, middle))
         return attend(cuts, parts, packed, origins, clip, visible, frame_counts, w_out)
 
-    own_end, end_sent = passed_back(*attended(True, parts), table, place)
+    at_place = place.astype(jnp.int32).reshape(1)
+    own_end, end_sent = passed_back(output(*attended(True, parts), line), table, at_place)
     parts[-1] = after(parts[-1], own_end[0])
-    own, sent = passed_back(*attended(False, parts), table, place, *end_sent)
+    *terms, last = output(*attended(False, parts), line)
+    own, sent = passed_back(terms + [after(last, *end_sent)], table, at_place)
 
     end_sums = own_end + sent_home(end_sent, table)
     end, end_feats = end_rows(current, levels, mods, head, end_sums)

time: 103 us -> 101 us (0.981)
  waiting for transfers between devices: 35.7 us -> 40.3 us
  other arithmetic: 2.48 us -> 0.14 us
  starting transfers between devices: 33.4 us -> 31.5 us
    ppermute x4, waiting for transfers between devices: 12.2 us -> 14.8 us  [sent_home(): lax.ppermute(term, 'tok', lanes(back(pairs)))]
    convert_element_type x4 -> x0, other arithmetic: 2.34 us -> none  [total(): return functools.reduce(lambda a, b: a + b, [term.astype(jnp.float32) for...]
    ppermute x2, waiting for transfers between devices: 4.91 us -> 6.31 us  [passed_back(): came = lax.ppermute(sums, 'tok', lanes(back(pairs)))]
  transfers between devices with their start and end apart: 24 -> 24, of which waited for: 12 -> 12; matrix products, arithmetic and copies ran while one was open for 2% -> 0% of each run, Pallas kernels for 20% -> 20%
where the time goes in v3:
time: 101 us
  waiting for transfers between devices  40.3 us (40%)
  starting transfers between devices  31.5 us (31%)
  Pallas kernels  27.4 us (27%)
  between operations  1.61 us (2%)
    pallas_call x3, Pallas kernels, project(): pl.pallas_call(functools.partial(project_kernel, len(tiles)), in_specs=[v...  15.9 us
    ppermute x4, waiting for transfers between devices, sent_home(): lax.ppermute(term, 'tok', lanes(back(pairs)))  14.8 us
    ppermute x6, waiting for transfers between devices, take(): return lax.ppermute(tile, 'tok', lanes(pairs))  11.8 us
    ppermute x6, starting transfers between devices, take(): return lax.ppermute(tile, 'tok', lanes(pairs))  9.59 us
    ppermute x2, waiting for transfers between devices, passed_back(): came = lax.ppermute(sums, 'tok', lanes(back(pairs)))  6.31 us
    pallas_call x2, Pallas kernels, attend(): pl.pallas_call(functools.partial(attend_kernel, cuts, len(parts), origins...  5.57 us
    ppermute x4, starting transfers between devices, sent_home(): lax.ppermute(term, 'tok', lanes(back(pairs)))  5.06 us
    ppermute x1, starting transfers between devices, from_earlier(): across = lax.ppermute(after(behind, beside), 'span', [(3, 2), (2, 3)])  4.35 us
  transfers between devices with their start and end apart: 24, of which 12 were waited for; matrix products, arithmetic and copies ran while one was open for 0% of the time, Pallas kernels for 20%

profile of v3, /device:TPU:4, one launch (start us, length us, event | category | flops | bytes accessed | tf_op | source)
XLA Modules:
  0.0 101.0 jit_solution(13032509704471089064)
XLA Ops:
  1.3 1.5 %shard_map.113 = (bf16[16,3584]{1,0:T(8,128)(2,1)S(1)}, bf16[48,3584]{1,0:T(8,128)(2,1)S(1)}) custom-call(s32[1]{0:T(128)S(6)} %copy.12.level, bf16[64,3584]{1,0:T(8,128)(2,1)} %bitcast.11, f32[3,16,3584]{2,1,0:T(8,128)} %bitcast.8), custom_call_target="tpu_custom_call" | custom-call | flops 1 | bytes 1 | tf_op jit(solution)/shard_map/pallas_call | solution.py:138
  2.8 3.7 %collective-permute-start.2 = (bf16[16,3584]{1,0:T(8,128)(2,1)S(1)}, bf16[16,3584]{1,0:T(8,128)(2,1)S(1)}, u32[]{:S(2)}, u32[]{:S(2)}) collective-permute-start(bf16[16,3584]{1,0:T(8,128)(2,1)S(1)} %get-tuple-element.36.refs_0_), channel_id=1, source_target_pairs={{4,2},{5,3},{6,0},{7,1},{0,6},{1,7},{2,4},{3,5},{12,10},{13,11},{1... | collective-permute-start | bytes 344072 | tf_op jit(solution)/shard_map/ppermute | solution.py:383
  6.5 0.0 collective-permute-start.1
  6.5 2.9 %collective-permute-start = (bf16[16,3584]{1,0:T(8,128)(2,1)S(1)}, bf16[16,3584]{1,0:T(8,128)(2,1)S(1)}, u32[]{:S(2)}, u32[]{:S(2)}) collective-permute-start(bf16[16,3584]{1,0:T(8,128)(2,1)S(1)} %get-tuple-element.36.refs_0_), channel_id=1, source_target_pairs={{0,4},{1,5},{4,6},{5,7},{6,2},{7,3},{2,0},{3,1},{8,12},{9,13},{12,... | collective-permute-start | bytes 344072 | tf_op jit(solution)/shard_map/ppermute | solution.py:383
  9.4 0.0 collective-permute-start.6
  9.4 2.9 %collective-permute-start.5 = (bf16[48,3584]{1,0:T(8,128)(2,1)S(1)}, bf16[48,3584]{1,0:T(8,128)(2,1)S(1)}, u32[]{:S(2)}, u32[]{:S(2)}) collective-permute-start(bf16[48,3584]{1,0:T(8,128)(2,1)S(1)} %get-tuple-element.37.refs_0_), channel_id=1, source_target_pairs={{0,4},{1,5},{4,6},{5,7},{6,2},{7,3},{2,0},{3,1},{8,12},{9,13},{12,... | collective-permute-start | bytes 1032200 | tf_op jit(solution)/shard_map/ppermute | solution.py:383
  12.4 0.0 collective-permute-done.2.refs_3_
  12.4 4.8 %collective-permute-done.1.refs_2_ = bf16[16,3584]{1,0:T(8,128)(2,1)S(1)} collective-permute-done((bf16[16,3584]{1,0:T(8,128)(2,1)S(1)}, bf16[16,3584]{1,0:T(8,128)(2,1)S(1)}, u32[]{:S(2)}, u32[]{:S(2)}) %collective-permute-start.1) | collective-permute-done | bytes 114720 | tf_op jit(solution)/shard_map/ppermute | solution.py:383
  17.2 0.1 collective-permute-start.4
  17.3 0.5 collective-permute-start.3
  17.9 0.9 collective-permute-done.4
  18.8 0.3 collective-permute-done.3
  19.1 4.9 %shard_map.114.refs_0_ = bf16[3,128,512]{2,1,0:T(8,128)(2,1)S(1)} custom-call(bf16[16,3584]{1,0:T(8,128)(2,1)S(1)} %get-tuple-element.36.refs_0_, bf16[16,3584]{1,0:T(8,128)(2,1)S(1)} %collective-permute-done.refs_1_, bf16[16,3584]{1,0:T(8,128)(2,1)S(1)} %collective-permute-done.1.refs_2_, bf16[16,3584]{1,0:T(8,128)(2,1)S(1)} %collective-permute-done.2.refs_3_, ...), custom_call_target="tpu_custom_call" | custom-call | flops 1 | bytes 1 | tf_op jit(solution)/shard_map/pallas_call | solution.py:194
  24.0 6.9 %collective-permute-done.6.refs_2_ = bf16[48,3584]{1,0:T(8,128)(2,1)S(1)} collective-permute-done((bf16[48,3584]{1,0:T(8,128)(2,1)S(1)}, bf16[48,3584]{1,0:T(8,128)(2,1)S(1)}, u32[]{:S(2)}, u32[]{:S(2)}) %collective-permute-start.6) | collective-permute-done | bytes 344096 | tf_op jit(solution)/shard_map/ppermute | solution.py:383
  30.9 0.1 pad_maximum_fusion
  31.0 0.1 collective-permute-start.7
  31.1 0.1 collective-permute-start.8
  31.2 1.3 %collective-permute-start.11 = (bf16[2,128,512]{2,1,0:T(8,128)(2,1)S(1)}, bf16[2,128,512]{2,1,0:T(8,128)(2,1)S(1)}, u32[]{:S(2)}, u32[]{:S(2)}) collective-permute-start(bf16[2,128,512]{2,1,0:T(8,128)(2,1)S(1)} %slice.8), channel_id=1, source_target_pairs={{0,16},{8,24},{1,17},{9,25},{2,18},{10,26},{3,19},{11,27},{4,20},{... | collective-permute-start | bytes 786440 | tf_op jit(solution)/shard_map/ppermute | solution.py:78
  32.5 3.4 %collective-permute-start.10 = (bf16[2,128,512]{2,1,0:T(8,128)(2,1)S(1)}, bf16[2,128,512]{2,1,0:T(8,128)(2,1)S(1)}, u32[]{:S(2)}, u32[]{:S(2)}) collective-permute-start(bf16[2,128,512]{2,1,0:T(8,128)(2,1)S(1)} %slice.8), channel_id=1, source_target_pairs={{0,8},{16,24},{1,9},{17,25},{2,10},{18,26},{3,11},{19,27},{4,12},{... | collective-permute-start | bytes 786440 | tf_op jit(solution)/shard_map/ppermute | solution.py:77
  36.0 0.0 collective-permute-done.7.refs_3_
  36.0 6.1 %shard_map.115.refs_1_ = bf16[3,288,512]{2,1,0:T(8,128)(2,1)S(1)} custom-call(bf16[48,3584]{1,0:T(8,128)(2,1)S(1)} %get-tuple-element.37.refs_0_, bf16[48,3584]{1,0:T(8,128)(2,1)S(1)} %collective-permute-done.5.refs_1_, bf16[48,3584]{1,0:T(8,128)(2,1)S(1)} %collective-permute-done.6.refs_2_, bf16[144,3584]{1,0:T(8,128)(2,1)S(1)} %collective-permute-done.7.refs_3_, ...), custom_call_target="tpu_custom_call" | custom-call | flops 1 | bytes 1 | tf_op jit(solution)/shard_map/pallas_call | solution.py:194
  42.1 0.0 collective-permute-done.8.refs_0_
  42.1 0.3 collective-permute-start.9
  42.3 4.3 %collective-permute-start.12 = (bf16[2,128,512]{2,1,0:T(8,128)(2,1)S(1)}, bf16[2,128,512]{2,1,0:T(8,128)(2,1)S(1)}, u32[]{:S(2)}, u32[]{:S(2)}) collective-permute-start(bf16[2,128,512]{2,1,0:T(8,128)(2,1)S(1)} %collective-permute-done.11.refs_4_), channel_id=1, source_target_pairs={{24,16},{16,24},{25,17},{17,25},{26,18},{18,26},{27,19},{19,27},{2... | collective-permute-start | bytes 786440 | tf_op jit(solution)/shard_map/ppermute | solution.py:79
  46.7 0.0 copy-start.5
  46.7 0.0 copy-start.6
  46.7 0.0 collective-permute-done.9.refs_1_
  46.7 4.9 %shard_map.116.refs_2_ = bf16[3,96,512]{2,1,0:T(8,128)(2,1)S(1)} custom-call(bf16[48,3584]{1,0:T(8,128)(2,1)S(1)} %collective-permute-done.8.refs_0_, bf16[48,3584]{1,0:T(8,128)(2,1)S(1)} %collective-permute-done.9.refs_1_, f32[2,512]{1,0:T(2,128)S(1)} %copy-done.4, bf16[3,3584,512]{2,1,0:T(8,128)(2,1)} %bitcast.18), custom_call_target="tpu_custom_call" | custom-call | flops 1 | bytes 1 | tf_op jit(solution)/shard_map/pallas_call | solution.py:194
  51.7 1.0 %collective-permute-done.12.refs_5_ = bf16[2,128,512]{2,1,0:T(8,128)(2,1)S(1)} collective-permute-done((bf16[2,128,512]{2,1,0:T(8,128)(2,1)S(1)}, bf16[2,128,512]{2,1,0:T(8,128)(2,1)S(1)}, u32[]{:S(2)}, u32[]{:S(2)}) %collective-permute-start.12) | collective-permute-done | bytes 262176 | tf_op jit(solution)/shard_map/ppermute | solution.py:79
  52.7 2.8 %shard_map.117 = (bf16[256,512]{1,0:T(8,128)(2,1)S(1)}, bf16[512,3584]{1,0:T(8,128)(2,1)S(1)}) custom-call(s32[1]{0:T(128)} %bitcast.3.clip, s32[4,4]{1,0:T(4,128)S(1)} %copy-done.5, s32[4]{0:T(128)S(1)} %copy-done.6, bf16[3,128,512]{2,1,0:T(8,128)(2,1)S(1)} %shard_map.114.refs_0_, bf16[3,288,512]{2,1,0:T(8,128)(2,1)S(1)} %shard_map.115.refs_1_, ...), custom_call_target="tpu_custom_call" | custom-call | flops 1 | bytes 1 | tf_op jit(solution)/shard_map/pallas_call | solution.py:262
  55.5 1.1 %shard_map.118 = (bf16[32,3584]{1,0:T(8,128)(2,1)S(1)}, bf16[32,3584]{1,0:T(8,128)(2,1)S(1)}, bf16[32,3584]{1,0:T(8,128)(2,1)S(1)}, bf16[32,3584]{1,0:T(8,128)(2...) custom-call(bf16[256,512]{1,0:T(8,128)(2,1)S(1)} %get-tuple-element.42.attended, ...), custom_call_target="tpu_custom_call" | custom-call | flops 1 | bytes 1 | tf_op jit(solution)/shard_map/pallas_call | solution.py:293
  56.7 0.1 collective-permute-start.13
  56.7 0.5 collective-permute-start.14
  57.2 2.0 %collective-permute-done.14.refs_1_.refs_4_ = bf16[32,3584]{1,0:T(8,128)(2,1)S(1)} collective-permute-done((bf16[32,3584]{1,0:T(8,128)(2,1)S(1)}, bf16[32,3584]{1,0:T(8,128)(2,1)S(1)}, u32[]{:S(2)}, u32[]{:S(2)}) %collective-permute-start.14) | collective-permute-done | bytes 229408 | tf_op jit(solution)/shard_map/ppermute | solution.py:62
  59.2 0.1 shard_map.119
  59.3 2.1 %collective-permute-start.15 = (bf16[32,3584]{1,0:T(8,128)(2,1)S(1)}, bf16[32,3584]{1,0:T(8,128)(2,1)S(1)}, u32[]{:S(2)}, u32[]{:S(2)}) collective-permute-start(bf16[32,3584]{1,0:T(8,128)(2,1)S(1)} %shard_map.119), channel_id=1, source_target_pairs={{2,0},{3,1},{0,2},{1,3},{6,4},{7,5},{4,6},{5,7},{10,8},{11,9},{8,1... | collective-permute-start | bytes 688136 | tf_op jit(solution)/shard_map/ppermute | solution.py:429
  61.3 2.8 %shard_map.122 = (bf16[256,512]{1,0:T(8,128)(2,1)S(1)}, bf16[512,3584]{1,0:T(8,128)(2,1)S(1)}) custom-call(s32[1]{0:T(128)} %bitcast.3.clip, s32[4,4]{1,0:T(4,128)S(1)} %copy-done.5, s32[4]{0:T(128)S(1)} %copy-done.6, bf16[3,128,512]{2,1,0:T(8,128)(2,1)S(1)} %shard_map.114.refs_0_, bf16[3,288,512]{2,1,0:T(8,128)(2,1)S(1)} %shard_map.115.refs_1_, ...), custom_call_target="tpu_custom_call" | custom-call | flops 1 | bytes 1 | tf_op jit(solution)/shard_map/pallas_call | solution.py:262
  64.1 1.1 %shard_map.123 = (bf16[32,3584]{1,0:T(8,128)(2,1)S(1)}, bf16[32,3584]{1,0:T(8,128)(2,1)S(1)}, bf16[32,3584]{1,0:T(8,128)(2,1)S(1)}, bf16[32,3584]{1,0:T(8,128)(2...) custom-call(bf16[256,512]{1,0:T(8,128)(2,1)S(1)} %get-tuple-element.55.attended, ...), custom_call_target="tpu_custom_call" | custom-call | flops 1 | bytes 1 | tf_op jit(solution)/shard_map/pallas_call | solution.py:293
  65.3 0.0 copy-start
  65.3 0.0 copy-start.1
  65.3 0.0 copy-start.2
  65.3 0.1 collective-permute-start.19
  65.4 1.9 %collective-permute-done.15.refs_5_ = bf16[32,3584]{1,0:T(8,128)(2,1)S(1)} collective-permute-done((bf16[32,3584]{1,0:T(8,128)(2,1)S(1)}, bf16[32,3584]{1,0:T(8,128)(2,1)S(1)}, u32[]{:S(2)}, u32[]{:S(2)}) %collective-permute-start.15) | collective-permute-done | bytes 229408 | tf_op jit(solution)/shard_map/ppermute | solution.py:429
  67.2 0.2 shard_map.120
  67.4 0.1 collective-permute-start.20
  67.5 1.8 %collective-permute-start.16 = (bf16[32,3584]{1,0:T(8,128)(2,1)S(1)}, bf16[32,3584]{1,0:T(8,128)(2,1)S(1)}, u32[]{:S(2)}, u32[]{:S(2)}) collective-permute-start(bf16[32,3584]{1,0:T(8,128)(2,1)S(1)} %get-tuple-element.50), channel_id=1, source_target_pairs={{4,0},{5,1},{6,4},{7,5},{2,6},{3,7},{0,2},{1,3},{12,8},{13,9},{14,... | collective-permute-start | bytes 688136 | tf_op jit(solution)/shard_map/ppermute | solution.py:448
  69.3 1.2 %collective-permute-start.17 = (bf16[32,3584]{1,0:T(8,128)(2,1)S(1)}, bf16[32,3584]{1,0:T(8,128)(2,1)S(1)}, u32[]{:S(2)}, u32[]{:S(2)}) collective-permute-start(bf16[32,3584]{1,0:T(8,128)(2,1)S(1)} %get-tuple-element.51), channel_id=1, source_target_pairs={{2,0},{3,1},{6,2},{7,3},{4,6},{5,7},{0,4},{1,5},{10,8},{11,9},{14,... | collective-permute-start | bytes 688136 | tf_op jit(solution)/shard_map/ppermute | solution.py:448
  70.5 0.0 collective-permute-done.20.refs_1_.refs_4_
  70.5 0.1 shard_map.124
  70.6 0.9 collective-permute-start.21
  71.5 5.2 %collective-permute-done.16.refs_2_ = bf16[32,3584]{1,0:T(8,128)(2,1)S(1)} collective-permute-done((bf16[32,3584]{1,0:T(8,128)(2,1)S(1)}, bf16[32,3584]{1,0:T(8,128)(2,1)S(1)}, u32[]{:S(2)}, u32[]{:S(2)}) %collective-permute-start.16) | collective-permute-done | bytes 229408 | tf_op jit(solution)/shard_map/ppermute | solution.py:448
  76.6 4.9 %collective-permute-done.17.refs_3_ = bf16[32,3584]{1,0:T(8,128)(2,1)S(1)} collective-permute-done((bf16[32,3584]{1,0:T(8,128)(2,1)S(1)}, bf16[32,3584]{1,0:T(8,128)(2,1)S(1)}, u32[]{:S(2)}, u32[]{:S(2)}) %collective-permute-start.17) | collective-permute-done | bytes 229408 | tf_op jit(solution)/shard_map/ppermute | solution.py:448
  81.5 0.0 copy-start.3
  81.6 0.4 shard_map.121
  81.9 0.0 collective-permute-done.19.refs_3_.refs_1_
  81.9 4.4 %collective-permute-done.21.refs_5_ = bf16[32,3584]{1,0:T(8,128)(2,1)S(1)} collective-permute-done((bf16[32,3584]{1,0:T(8,128)(2,1)S(1)}, bf16[32,3584]{1,0:T(8,128)(2,1)S(1)}, u32[]{:S(2)}, u32[]{:S(2)}) %collective-permute-start.21) | collective-permute-done | bytes 229408 | tf_op jit(solution)/shard_map/ppermute | solution.py:429
  86.4 0.2 shard_map.125
  86.6 1.8 %collective-permute-start.23 = (bf16[32,3584]{1,0:T(8,128)(2,1)S(1)}, bf16[32,3584]{1,0:T(8,128)(2,1)S(1)}, u32[]{:S(2)}, u32[]{:S(2)}) collective-permute-start(bf16[32,3584]{1,0:T(8,128)(2,1)S(1)} %get-tuple-element.67), channel_id=1, source_target_pairs={{2,0},{3,1},{6,2},{7,3},{4,6},{5,7},{0,4},{1,5},{10,8},{11,9},{14,... | collective-permute-start | bytes 688136 | tf_op jit(solution)/shard_map/ppermute | solution.py:448
  88.4 0.3 collective-permute-start.22
  88.7 3.2 %collective-permute-start.18 = (bf16[16,96]{1,0:T(8,128)(2,1)S(1)}, bf16[16,96]{1,0:T(8,128)(2,1)S(1)}, u32[]{:S(2)}, u32[]{:S(2)}) collective-permute-start(bf16[16,96]{1,0:T(8,128)(2,1)S(1)} %slice.7), channel_id=1, source_target_pairs={{0,8},{8,16},{16,24},{1,9},{9,17},{17,25},{2,10},{10,18},{18,26},{... | collective-permute-start | bytes 9224 | tf_op jit(solution)/shard_map/ppermute | solution.py:68
  91.9 3.2 %collective-permute-done.18.earlier = bf16[16,96]{1,0:T(8,128)(2,1)S(1)} collective-permute-done((bf16[16,96]{1,0:T(8,128)(2,1)S(1)}, bf16[16,96]{1,0:T(8,128)(2,1)S(1)}, u32[]{:S(2)}, u32[]{:S(2)}) %collective-permute-start.18) | collective-permute-done | bytes 3104 | tf_op jit(solution)/shard_map/ppermute | solution.py:68
  95.0 0.0 collective-permute-done.23.refs_3_
  95.0 4.7 %collective-permute-done.22.refs_2_ = bf16[32,3584]{1,0:T(8,128)(2,1)S(1)} collective-permute-done((bf16[32,3584]{1,0:T(8,128)(2,1)S(1)}, bf16[32,3584]{1,0:T(8,128)(2,1)S(1)}, u32[]{:S(2)}, u32[]{:S(2)}) %collective-permute-start.22) | collective-permute-done | bytes 229408 | tf_op jit(solution)/shard_map/ppermute | solution.py:448
  99.8 1.3 %shard_map.126 = (bf16[64,3584]{1,0:T(8,128)(2,1)}, bf16[64,384]{1,0:T(8,128)(2,1)}) custom-call(s32[1]{0:T(128)S(6)} %copy.12.level, bf16[64,3584]{1,0:T(8,128)(2,1)S(1)} %bitcast.13, f32[3,16,3584]{2,1,0:T(8,128)S(1)} %bitcast.10, bf16[96,3584]{1,0:T(8,128)(2,1)S(1)} %bitcast.15, bf16[3,96,384]{2,1,0:T(8,128)(2,1)S(1)} %copy-done.3, ...), custom_call_target="tpu_custom_call" | custom-call | flops 1 | bytes 1 | tf_op jit(solution)/shard_map/pallas_call | solution.py:357
  (20 shorter events, 0.2 us)
Async XLA Ops:
  0.6 18.5 %copy-start.4 = (f32[2,512]{1,0:T(2,128)S(1)}, f32[2,512]{1,0:T(2,128)}, u32[]{:S(2)}) copy-start(f32[2,512]{1,0:T(2,128)} %refs_2_.1) | copy-start | bytes 12292
  2.8 9.5 %collective-permute-start.2 = (bf16[16,3584]{1,0:T(8,128)(2,1)S(1)}, bf16[16,3584]{1,0:T(8,128)(2,1)S(1)}, u32[]{:S(2)}, u32[]{:S(2)}) collective-permute-start(bf16[16,3584]{1,0:T(8,128)(2,1)S(1)} %get-tuple-element.36.refs_0_), channel_id=1, source_target_pairs={{4,2},{5,3},{6,0},{7,1},{0,6},{1,7},{2,4},{3,5},{12,10},{13,11},{1... | collective-permute-start | bytes 344072 | tf_op jit(solution)/shard_map/ppermute | solution.py:383
  6.5 10.7 %collective-permute-start.1 = (bf16[16,3584]{1,0:T(8,128)(2,1)S(1)}, bf16[16,3584]{1,0:T(8,128)(2,1)S(1)}, u32[]{:S(2)}, u32[]{:S(2)}) collective-permute-start(bf16[16,3584]{1,0:T(8,128)(2,1)S(1)} %get-tuple-element.36.refs_0_), channel_id=1, source_target_pairs={{0,2},{1,3},{2,6},{3,7},{6,4},{7,5},{4,0},{5,1},{8,10},{9,11},{10,... | collective-permute-start | bytes 344072 | tf_op jit(solution)/shard_map/ppermute | solution.py:383
  6.5 10.8 %collective-permute-start = (bf16[16,3584]{1,0:T(8,128)(2,1)S(1)}, bf16[16,3584]{1,0:T(8,128)(2,1)S(1)}, u32[]{:S(2)}, u32[]{:S(2)}) collective-permute-start(bf16[16,3584]{1,0:T(8,128)(2,1)S(1)} %get-tuple-element.36.refs_0_), channel_id=1, source_target_pairs={{0,4},{1,5},{4,6},{5,7},{6,2},{7,3},{2,0},{3,1},{8,12},{9,13},{12,... | collective-permute-start | bytes 344072 | tf_op jit(solution)/shard_map/ppermute | solution.py:383
  9.4 21.5 %collective-permute-start.6 = (bf16[48,3584]{1,0:T(8,128)(2,1)S(1)}, bf16[48,3584]{1,0:T(8,128)(2,1)S(1)}, u32[]{:S(2)}, u32[]{:S(2)}) collective-permute-start(bf16[48,3584]{1,0:T(8,128)(2,1)S(1)} %get-tuple-element.37.refs_0_), channel_id=1, source_target_pairs={{0,2},{1,3},{2,6},{3,7},{6,4},{7,5},{4,0},{5,1},{8,10},{9,11},{10,... | collective-permute-start | bytes 1032200 | tf_op jit(solution)/shard_map/ppermute | solution.py:383
  9.4 21.5 %collective-permute-start.5 = (bf16[48,3584]{1,0:T(8,128)(2,1)S(1)}, bf16[48,3584]{1,0:T(8,128)(2,1)S(1)}, u32[]{:S(2)}, u32[]{:S(2)}) collective-permute-start(bf16[48,3584]{1,0:T(8,128)(2,1)S(1)} %get-tuple-element.37.refs_0_), channel_id=1, source_target_pairs={{0,4},{1,5},{4,6},{5,7},{6,2},{7,3},{2,0},{3,1},{8,12},{9,13},{12,... | collective-permute-start | bytes 1032200 | tf_op jit(solution)/shard_map/ppermute | solution.py:383
  17.2 1.6 %collective-permute-start.4 = (bf16[32,3584]{1,0:T(8,128)(2,1)S(1)}, bf16[32,3584]{1,0:T(8,128)(2,1)S(1)}, u32[]{:S(2)}, u32[]{:S(2)}) collective-permute-start(bf16[32,3584]{1,0:T(8,128)(2,1)S(1)} %pad_maximum_fusion.2), channel_id=1, source_target_pairs={{0,1},{1,0},{2,3},{3,2},{4,5},{5,4},{6,7},{7,6},{8,9},{9,8},{10,11... | collective-permute-start | bytes 688136 | tf_op jit(solution)/shard_map/ppermute | solution.py:62
  17.3 1.8 %collective-permute-start.3 = (bf16[32,3584]{1,0:T(8,128)(2,1)S(1)}, bf16[32,3584]{1,0:T(8,128)(2,1)S(1)}, u32[]{:S(2)}, u32[]{:S(2)}) collective-permute-start(bf16[32,3584]{1,0:T(8,128)(2,1)S(1)} %pad_maximum_fusion.1), channel_id=1, source_target_pairs={{0,1},{1,0},{2,3},{3,2},{4,5},{5,4},{6,7},{7,6},{8,9},{9,8},{10,11... | collective-permute-start | bytes 688136 | tf_op jit(solution)/shard_map/ppermute | solution.py:62
  31.0 5.0 %collective-permute-start.7 = (bf16[144,3584]{1,0:T(8,128)(2,1)S(1)}, bf16[144,3584]{1,0:T(8,128)(2,1)S(1)}, u32[]{:S(2)}, u32[]{:S(2)}) collective-permute-start(bf16[144,3584]{1,0:T(8,128)(2,1)S(1)} %pad_maximum_fusion), channel_id=1, source_target_pairs={{0,1},{1,0},{2,3},{3,2},{4,5},{5,4},{6,7},{7,6},{8,9},{9,8},{10,11... | collective-permute-start | bytes 3096584 | tf_op jit(solution)/shard_map/ppermute | solution.py:62
  31.1 10.9 %collective-permute-start.8 = (bf16[48,3584]{1,0:T(8,128)(2,1)S(1)}, bf16[48,3584]{1,0:T(8,128)(2,1)S(1)}, u32[]{:S(2)}, u32[]{:S(2)}) collective-permute-start(bf16[48,3584]{1,0:T(8,128)(2,1)S(1)} %broadcast_select_fusion), channel_id=1, source_target_pairs={{0,2},{1,3},{2,0},{3,1},{4,6},{5,7},{6,4},{7,5},{8,10},{9,11},{10,... | collective-permute-start | bytes 1032200 | tf_op jit(solution)/shard_map/ppermute | solution.py:383
  31.2 11.1 %collective-permute-start.11 = (bf16[2,128,512]{2,1,0:T(8,128)(2,1)S(1)}, bf16[2,128,512]{2,1,0:T(8,128)(2,1)S(1)}, u32[]{:S(2)}, u32[]{:S(2)}) collective-permute-start(bf16[2,128,512]{2,1,0:T(8,128)(2,1)S(1)} %slice.8), channel_id=1, source_target_pairs={{0,16},{8,24},{1,17},{9,25},{2,18},{10,26},{3,19},{11,27},{4,20},{... | collective-permute-start | bytes 786440 | tf_op jit(solution)/shard_map/ppermute | solution.py:78
  32.5 9.8 %collective-permute-start.10 = (bf16[2,128,512]{2,1,0:T(8,128)(2,1)S(1)}, bf16[2,128,512]{2,1,0:T(8,128)(2,1)S(1)}, u32[]{:S(2)}, u32[]{:S(2)}) collective-permute-start(bf16[2,128,512]{2,1,0:T(8,128)(2,1)S(1)} %slice.8), channel_id=1, source_target_pairs={{0,8},{16,24},{1,9},{17,25},{2,10},{18,26},{3,11},{19,27},{4,12},{... | collective-permute-start | bytes 786440 | tf_op jit(solution)/shard_map/ppermute | solution.py:77
  42.1 4.7 %collective-permute-start.9 = (bf16[48,3584]{1,0:T(8,128)(2,1)S(1)}, bf16[48,3584]{1,0:T(8,128)(2,1)S(1)}, u32[]{:S(2)}, u32[]{:S(2)}) collective-permute-start(bf16[48,3584]{1,0:T(8,128)(2,1)S(1)} %collective-permute-done.8.refs_0_), channel_id=1, source_target_pairs={{0,1},{1,0},{2,3},{3,2},{4,5},{5,4},{6,7},{7,6},{8,9},{9,8},{10,11... | collective-permute-start | bytes 1032200 | tf_op jit(solution)/shard_map/ppermute | solution.py:62
  42.3 10.4 %collective-permute-start.12 = (bf16[2,128,512]{2,1,0:T(8,128)(2,1)S(1)}, bf16[2,128,512]{2,1,0:T(8,128)(2,1)S(1)}, u32[]{:S(2)}, u32[]{:S(2)}) collective-permute-start(bf16[2,128,512]{2,1,0:T(8,128)(2,1)S(1)} %collective-permute-done.11.refs_4_), channel_id=1, source_target_pairs={{24,16},{16,24},{25,17},{17,25},{26,18},{18,26},{27,19},{19,27},{2... | collective-permute-start | bytes 786440 | tf_op jit(solution)/shard_map/ppermute | solution.py:79
  46.7 6.0 %copy-start.5 = (s32[4,4]{1,0:T(4,128)S(1)}, s32[4,4]{1,0:T(4,128)}, u32[]{:S(2)}) copy-start(s32[4,4]{1,0:T(4,128)} %visible.3) | copy-start | bytes 196
  46.7 6.0 %copy-start.6 = (s32[4]{0:T(128)S(1)}, s32[4]{0:T(128)}, u32[]{:S(2)}) copy-start(s32[4]{0:T(128)} %counts.3) | copy-start | bytes 52
  56.7 10.6 %collective-permute-start.13 = (bf16[96,3584]{1,0:T(8,128)(2,1)S(1)}, bf16[96,3584]{1,0:T(8,128)(2,1)S(1)}, u32[]{:S(2)}, u32[]{:S(2)}) collective-permute-start(bf16[96,3584]{1,0:T(8,128)(2,1)S(1)} %get-tuple-element.45), channel_id=1, source_target_pairs={{0,1},{1,0},{2,3},{3,2},{4,5},{5,4},{6,7},{7,6},{8,9},{9,8},{10,11... | collective-permute-start | bytes 2064392 | tf_op jit(solution)/shard_map/ppermute | solution.py:62
  56.7 2.5 %collective-permute-start.14 = (bf16[32,3584]{1,0:T(8,128)(2,1)S(1)}, bf16[32,3584]{1,0:T(8,128)(2,1)S(1)}, u32[]{:S(2)}, u32[]{:S(2)}) collective-permute-start(bf16[32,3584]{1,0:T(8,128)(2,1)S(1)} %get-tuple-element.49), channel_id=1, source_target_pairs={{0,1},{1,0},{2,3},{3,2},{4,5},{5,4},{6,7},{7,6},{8,9},{9,8},{10,11... | collective-permute-start | bytes 688136 | tf_op jit(solution)/shard_map/ppermute | solution.py:62
  59.3 8.0 %collective-permute-start.15 = (bf16[32,3584]{1,0:T(8,128)(2,1)S(1)}, bf16[32,3584]{1,0:T(8,128)(2,1)S(1)}, u32[]{:S(2)}, u32[]{:S(2)}) collective-permute-start(bf16[32,3584]{1,0:T(8,128)(2,1)S(1)} %shard_map.119), channel_id=1, source_target_pairs={{2,0},{3,1},{0,2},{1,3},{6,4},{7,5},{4,6},{5,7},{10,8},{11,9},{8,1... | collective-permute-start | bytes 688136 | tf_op jit(solution)/shard_map/ppermute | solution.py:429
  65.3 16.3 %copy-start = (f32[16,3,3584]{2,0,1:T(8,128)S(1)}, f32[16,3,3584]{2,0,1:T(8,128)}, u32[]{:S(2)}) copy-start(f32[16,3,3584]{2,0,1:T(8,128)} %param.14) | copy-start | bytes 2064388
  65.3 16.3 %copy-start.1 = (bf16[1,64,3584]{2,1,0:T(8,128)(2,1)S(1)}, bf16[1,64,3584]{2,1,0:T(8,128)(2,1)}, u32[]{:S(2)}) copy-start(bf16[1,64,3584]{2,1,0:T(8,128)(2,1)} %param.10) | copy-start | bytes 1376260
  65.3 16.3 %copy-start.2 = (bf16[3584,96]{0,1:T(8,128)(2,1)S(1)}, bf16[3584,96]{0,1:T(8,128)(2,1)}, u32[]{:S(2)}) copy-start(bf16[3584,96]{0,1:T(8,128)(2,1)} %param.18) | copy-start | bytes 2064388
  65.3 16.6 %collective-permute-start.19 = (bf16[96,3584]{1,0:T(8,128)(2,1)S(1)}, bf16[96,3584]{1,0:T(8,128)(2,1)S(1)}, u32[]{:S(2)}, u32[]{:S(2)}) collective-permute-start(bf16[96,3584]{1,0:T(8,128)(2,1)S(1)} %get-tuple-element.58), channel_id=1, source_target_pairs={{0,1},{1,0},{2,3},{3,2},{4,5},{5,4},{6,7},{7,6},{8,9},{9,8},{10,11... | collective-permute-start | bytes 2064392 | tf_op jit(solution)/shard_map/ppermute | solution.py:62
  67.4 3.1 %collective-permute-start.20 = (bf16[32,3584]{1,0:T(8,128)(2,1)S(1)}, bf16[32,3584]{1,0:T(8,128)(2,1)S(1)}, u32[]{:S(2)}, u32[]{:S(2)}) collective-permute-start(bf16[32,3584]{1,0:T(8,128)(2,1)S(1)} %get-tuple-element.63), channel_id=1, source_target_pairs={{0,1},{1,0},{2,3},{3,2},{4,5},{5,4},{6,7},{7,6},{8,9},{9,8},{10,11... | collective-permute-start | bytes 688136 | tf_op jit(solution)/shard_map/ppermute | solution.py:62
  67.5 9.1 %collective-permute-start.16 = (bf16[32,3584]{1,0:T(8,128)(2,1)S(1)}, bf16[32,3584]{1,0:T(8,128)(2,1)S(1)}, u32[]{:S(2)}, u32[]{:S(2)}) collective-permute-start(bf16[32,3584]{1,0:T(8,128)(2,1)S(1)} %get-tuple-element.50), channel_id=1, source_target_pairs={{4,0},{5,1},{6,4},{7,5},{2,6},{3,7},{0,2},{1,3},{12,8},{13,9},{14,... | collective-permute-start | bytes 688136 | tf_op jit(solution)/shard_map/ppermute | solution.py:448
  69.3 12.2 %collective-permute-start.17 = (bf16[32,3584]{1,0:T(8,128)(2,1)S(1)}, bf16[32,3584]{1,0:T(8,128)(2,1)S(1)}, u32[]{:S(2)}, u32[]{:S(2)}) collective-permute-start(bf16[32,3584]{1,0:T(8,128)(2,1)S(1)} %get-tuple-element.51), channel_id=1, source_target_pairs={{2,0},{3,1},{6,2},{7,3},{4,6},{5,7},{0,4},{1,5},{10,8},{11,9},{14,... | collective-permute-start | bytes 688136 | tf_op jit(solution)/shard_map/ppermute | solution.py:448
  70.6 15.8 %collective-permute-start.21 = (bf16[32,3584]{1,0:T(8,128)(2,1)S(1)}, bf16[32,3584]{1,0:T(8,128)(2,1)S(1)}, u32[]{:S(2)}, u32[]{:S(2)}) collective-permute-start(bf16[32,3584]{1,0:T(8,128)(2,1)S(1)} %shard_map.124), channel_id=1, source_target_pairs={{2,0},{3,1},{0,2},{1,3},{6,4},{7,5},{4,6},{5,7},{10,8},{11,9},{8,1... | collective-permute-start | bytes 688136 | tf_op jit(solution)/shard_map/ppermute | solution.py:429
  81.5 18.2 %copy-start.3 = (bf16[3,96,384]{2,1,0:T(8,128)(2,1)S(1)}, bf16[3,96,384]{2,1,0:T(8,128)(2,1)}, u32[]{:S(2)}) copy-start(bf16[3,96,384]{2,1,0:T(8,128)(2,1)} %weight.1) | copy-start | bytes 663556
  86.6 8.5 %collective-permute-start.23 = (bf16[32,3584]{1,0:T(8,128)(2,1)S(1)}, bf16[32,3584]{1,0:T(8,128)(2,1)S(1)}, u32[]{:S(2)}, u32[]{:S(2)}) collective-permute-start(bf16[32,3584]{1,0:T(8,128)(2,1)S(1)} %get-tuple-element.67), channel_id=1, source_target_pairs={{2,0},{3,1},{6,2},{7,3},{4,6},{5,7},{0,4},{1,5},{10,8},{11,9},{14,... | collective-permute-start | bytes 688136 | tf_op jit(solution)/shard_map/ppermute | solution.py:448
  88.4 11.4 %collective-permute-start.22 = (bf16[32,3584]{1,0:T(8,128)(2,1)S(1)}, bf16[32,3584]{1,0:T(8,128)(2,1)S(1)}, u32[]{:S(2)}, u32[]{:S(2)}) collective-permute-start(bf16[32,3584]{1,0:T(8,128)(2,1)S(1)} %get-tuple-element.65), channel_id=1, source_target_pairs={{4,0},{5,1},{6,4},{7,5},{2,6},{3,7},{0,2},{1,3},{12,8},{13,9},{14,... | collective-permute-start | bytes 688136 | tf_op jit(solution)/shard_map/ppermute | solution.py:448
  88.7 6.4 %collective-permute-start.18 = (bf16[16,96]{1,0:T(8,128)(2,1)S(1)}, bf16[16,96]{1,0:T(8,128)(2,1)S(1)}, u32[]{:S(2)}, u32[]{:S(2)}) collective-permute-start(bf16[16,96]{1,0:T(8,128)(2,1)S(1)} %slice.7), channel_id=1, source_target_pairs={{0,8},{8,16},{16,24},{1,9},{9,17},{17,25},{2,10},{10,18},{18,26},{... | collective-permute-start | bytes 9224 | tf_op jit(solution)/shard_map/ppermute | solution.py:68

commit v4 on v3

--- a/solution.py
+++ b/solution.py
@@ -152,58 +152,53 @@
     )(levels, in_hbm(latents), in_hbm(table))
 
 
-def project_kernel(count, *refs):
-    tiles, (gain, weight, out, kept, held, sems) = refs[:count], refs[count:]
-    cols = weight.shape[2]
-    unit = cols
-    blocks = [(part, begin) for part in range(3) for begin in range(0, cols, unit)]
-    copies = [
-        pltpu.make_async_copy(
-            weight.at[part, :, pl.ds(begin, unit)],
-            kept.at[part, :, pl.ds(begin, unit)],
-            sems.at[i],
-        )
-        for i, (part, begin) in enumerate(blocks)
-    ]
-    for copy in copies:
-        copy.start()
+def project_kernel(count, load, *refs):
+    tiles, (gain, weight, out), refs = refs[:count], refs[count : count + 3], refs[count + 3 :]
+    copies = []
+    if load:
+        kept, held, sems = refs
+        for part in range(3):
+            copies.append(pltpu.make_async_copy(weight.at[part], kept.at[part], sems.at[part]))
+            copies[-1].start()
+        weight = kept
+    else:
+        (held,) = refs
     begin = 0
     for tile in tiles:
         held[begin : begin + tile.shape[0]] = tile[...]
         begin += tile.shape[0]
-    for copy, (part, begin) in zip(copies, blocks):
-        copy.wait()
-        proj = jnp.dot(
-            held[...], kept[part, :, begin : begin + unit], preferred_element_type=jnp.float32
-        )
+    for part in range(3):
+        if load:
+            copies[part].wait()
+        proj = jnp.dot(held[...], weight[part], preferred_element_type=jnp.float32)
         if part == 2:
-            out[part, :, begin : begin + unit] = proj.astype(jnp.bfloat16)
+            out[part] = proj.astype(jnp.bfloat16)
             continue
-        for h in range(unit // HD):
-            cut = slice(begin + h * HD, begin + (h + 1) * HD)
-            head = proj[:, h * HD : (h + 1) * HD]
+        for h in range(proj.shape[1] // HD):
+            cut = slice(h * HD, (h + 1) * HD)
+            head = proj[:, cut]
             square = jnp.mean(head * head, -1, keepdims=True)
             out[part, :, cut] = (
                 head * lax.rsqrt(square + EPS) * gain[part : part + 1, cut]
             ).astype(jnp.bfloat16)
 
 
-def project(tiles, gain, weight):
+def project(tiles, gain, weight, load=True):
     rows = sum(tile.shape[0] for tile in tiles)
     width, cols = weight.shape[1:]
-    return pl.pallas_call(
-        functools.partial(project_kernel, len(tiles)),
-        in_specs=[vmem()] * (len(tiles) + 1) + [hbm()],
+    scratch = [pltpu.VMEM((rows, width), jnp.bfloat16)]
+    if load:
+        scratch = [pltpu.VMEM(weight.shape, weight.dtype)] + scratch
+        scratch.append(pltpu.SemaphoreType.DMA((3,)))
+    return pl.pallas_call(
+        functools.partial(project_kernel, len(tiles), load),
+        in_specs=[vmem()] * (len(tiles) + 1) + [hbm() if load else vmem()],
         out_specs=vmem(),
         out_shape=jax.ShapeDtypeStruct((3, rows, cols), jnp.bfloat16),
-        scratch_shapes=[
-            pltpu.VMEM(weight.shape, weight.dtype),
-            pltpu.VMEM((rows, width), jnp.bfloat16),
-            pltpu.SemaphoreType.DMA((3,)),
-        ],
-        compiler_params=params(18 + rows // 64 // 8),
-        cost_estimate=CHEAP,
-    )(*tiles, gain, in_hbm(weight))
+        scratch_shapes=scratch,
+        compiler_params=params((18 if load else 7) + rows // 64 // 8),
+        cost_estimate=CHEAP,
+    )(*tiles, gain, in_hbm(weight) if load else weight)
 
 
 def attend_kernel(cuts, own, origins, clip, visible, counts, *refs):
@@ -373,21 +368,25 @@
     )
 
 
-def take(entry, tile, held, place):
+def masks(table, place):
+    return [
+        [passes(relay, slot, place) for slot in sorted(set(relay))[1:]] if relay else []
+        for _, relay in table
+    ]
+
+
+def take(entry, tile, held, mask):
     pairs, relay = entry
     if relay is not None:
         first, *others = sorted(set(relay))
         tile = held[first]
-        for slot in others:
-            tile = jnp.where(passes(relay, slot, place), held[slot], tile)
+        for slot, here in zip(others, mask):
+            tile = jnp.where(here, held[slot], tile)
     return lax.ppermute(tile, "tok", lanes(pairs))
 
 
-def spread(tile, table, place):
-    held = []
-    for entry in table:
-        held.append(take(entry, tile, held, place))
-    return held
+def spread(tile, table):
+    return [take(entry, tile, [], []) for entry in table]
 
 
 def merge_kernel(groups, count, place, *refs):
@@ -462,8 +461,12 @@
     head = w_head.transpose(1, 0)
 
     lead, body = modulate(current, levels, mods)
-    leads = [lead] + spread(lead, direct(table), place)
-    held = spread(body, table[:-1], place)
+    at_place = place.astype(jnp.int32).reshape(1)
+    lead, body, clip, at_place, mask = lax.optimization_barrier(
+        (lead, body, clip, at_place, masks(table, place))
+    )
+    leads = [lead] + spread(lead, direct(table))
+    held = spread(body, table[:-1])
     half = line // 2
     for part in (leads[:half], leads[half:]):
         pair = over_core(jnp.concatenate(part, 0))
@@ -471,12 +474,12 @@
     lead_part = project(leads, qk_gain, weight)
     packed, origins = from_earlier(lead_part[1:])
 
-    last = take(table[-1], body, [after(tile, lead_part) for tile in held], place)
+    last = take(table[-1], body, [after(tile, *packed[:2]) for tile in held], mask[-1])
     first = [body] + [after(tile, lead_part) for tile in held]
     across = over_core(jnp.concatenate(first, 0))
-    early_part = project([body] + held + [across], qk_gain, weight)
-    last = after(last, early_part)
-    late_part = project([last, over_core(last)], qk_gain, weight)
+    early_part = project([body] + held + [across], qk_gain, weight, False)
+    last = after(last, early_part, *packed)
+    late_part = project([last, over_core(last)], qk_gain, weight, False)
     parts = [lead_part, early_part, late_part]
 
     def at(lane, slot):
@@ -498,7 +501,6 @@
                     cuts.append((part, begin, middle))
         return attend(cuts, parts, packed, origins, clip, visible, frame_counts, w_out)
 
-    at_place = place.astype(jnp.int32).reshape(1)
     own_end, end_sent = passed_back(output(*attended(True, parts), line), table, at_place)
     parts[-1] = after(parts[-1], own_end[0])
     *terms, last = output(*attended(False, parts), line)

time: 101 us -> 99 us (0.980); the launches traced: 101 us -> 97.6 us
  Pallas kernels: 27.4 us -> 22.2 us
  waiting for transfers between devices: 40.3 us -> 41.7 us
    pallas_call x3, Pallas kernels: 15.9 us -> 10.4 us  [project(): pl.pallas_call(functools.partial(project_kernel, len(tiles), load), in_sp...]
    ppermute x6, waiting for transfers between devices: 11.8 us -> 6.43 us  [take(): return lax.ppermute(tile, 'tok', lanes(pairs))]
    ppermute x1, waiting for transfers between devices: 0.01 us -> 3.92 us  [from_earlier(): behind = lax.ppermute(array, 'span', [(0, 2), (1, 3)])]
    ppermute x8, waiting for transfers between devices: 3.17 us -> 4.82 us  [over_core(): return lax.ppermute(array, 'tok', [(i, i ^ 1) for i in range(devices)])]
    ppermute x1, waiting for transfers between devices: 1.05 us -> 2.27 us  [from_earlier(): across = lax.ppermute(after(behind, beside), 'span', [(3, 2), (2, 3)])]
  transfers between devices with their start and end apart: 24 -> 24, of which waited for: 12 -> 15; matrix products, arithmetic and copies ran while one was open for 0% -> 0% of each run, Pallas kernels for 20% -> 14%
where the time goes in v4:
time: 99 us; the launch traced here: 97.6 us
  waiting for transfers between devices  41.7 us (42%)
  starting transfers between devices  31.9 us (32%)
  Pallas kernels  22.2 us (22%)
  between operations  1.6 us (2%)
    ppermute x4, waiting for transfers between devices, sent_home(): lax.ppermute(term, 'tok', lanes(back(pairs)))  14.9 us
    pallas_call x3, Pallas kernels, project(): pl.pallas_call(functools.partial(project_kernel, len(tiles), load), in_sp...  10.4 us
    ppermute x6, starting transfers between devices, take(): return lax.ppermute(tile, 'tok', lanes(pairs))  9.59 us
    ppermute x6, waiting for transfers between devices, take(): return lax.ppermute(tile, 'tok', lanes(pairs))  6.43 us
    ppermute x2, waiting for transfers between devices, passed_back(): came = lax.ppermute(sums, 'tok', lanes(back(pairs)))  6.24 us
    pallas_call x2, Pallas kernels, attend(): pl.pallas_call(functools.partial(attend_kernel, cuts, len(parts), origins...  5.79 us
    ppermute x4, starting transfers between devices, sent_home(): lax.ppermute(term, 'tok', lanes(back(pairs)))  5.14 us
    ppermute x8, waiting for transfers between devices, over_core(): return lax.ppermute(array, 'tok', [(i, i ^ 1) for i in range(devices)])  4.82 us
  transfers between devices with their start and end apart: 24, of which 15 were waited for; matrix products, arithmetic and copies ran while one was open for 0% of the time, Pallas kernels for 14%

profile of v4, /device:TPU:4, one launch (start us, length us, event | category | flops | bytes accessed | tf_op | source)
XLA Modules:
  0.0 97.6 jit_solution(4508543118564612297)
XLA Ops:
  1.3 1.5 %shard_map.113 = (bf16[16,3584]{1,0:T(8,128)(2,1)S(1)}, bf16[48,3584]{1,0:T(8,128)(2,1)S(1)}) custom-call(s32[1]{0:T(128)S(6)} %copy.12.level, bf16[64,3584]{1,0:T(8,128)(2,1)} %bitcast.14, f32[3,16,3584]{2,1,0:T(8,128)} %bitcast.11), custom_call_target="tpu_custom_call" | custom-call | flops 1 | bytes 1 | tf_op jit(solution)/shard_map/pallas_call | solution.py:138
  2.8 3.7 %collective-permute-start.2 = (bf16[16,3584]{1,0:T(8,128)(2,1)S(1)}, bf16[16,3584]{1,0:T(8,128)(2,1)S(1)}, u32[]{:S(2)}, u32[]{:S(2)}) collective-permute-start(bf16[16,3584]{1,0:T(8,128)(2,1)S(1)} %get-tuple-element.46.refs_0_), channel_id=1, source_target_pairs={{4,2},{5,3},{6,0},{7,1},{0,6},{1,7},{2,4},{3,5},{12,10},{13,11},{1... | collective-permute-start | bytes 344072 | tf_op jit(solution)/shard_map/ppermute | solution.py:385
  6.5 0.0 collective-permute-start.1
  6.5 2.9 %collective-permute-start = (bf16[16,3584]{1,0:T(8,128)(2,1)S(1)}, bf16[16,3584]{1,0:T(8,128)(2,1)S(1)}, u32[]{:S(2)}, u32[]{:S(2)}) collective-permute-start(bf16[16,3584]{1,0:T(8,128)(2,1)S(1)} %get-tuple-element.46.refs_0_), channel_id=1, source_target_pairs={{0,4},{1,5},{4,6},{5,7},{6,2},{7,3},{2,0},{3,1},{8,12},{9,13},{12,... | collective-permute-start | bytes 344072 | tf_op jit(solution)/shard_map/ppermute | solution.py:385
  9.4 0.0 collective-permute-start.6
  9.4 2.9 %collective-permute-start.5 = (bf16[48,3584]{1,0:T(8,128)(2,1)S(1)}, bf16[48,3584]{1,0:T(8,128)(2,1)S(1)}, u32[]{:S(2)}, u32[]{:S(2)}) collective-permute-start(bf16[48,3584]{1,0:T(8,128)(2,1)S(1)} %get-tuple-element.47.refs_0_), channel_id=1, source_target_pairs={{0,4},{1,5},{4,6},{5,7},{6,2},{7,3},{2,0},{3,1},{8,12},{9,13},{12,... | collective-permute-start | bytes 1032200 | tf_op jit(solution)/shard_map/ppermute | solution.py:385
  12.4 4.8 %collective-permute-done.1.refs_2_ = bf16[16,3584]{1,0:T(8,128)(2,1)S(1)} collective-permute-done((bf16[16,3584]{1,0:T(8,128)(2,1)S(1)}, bf16[16,3584]{1,0:T(8,128)(2,1)S(1)}, u32[]{:S(2)}, u32[]{:S(2)}) %collective-permute-start.1) | collective-permute-done | bytes 114720 | tf_op jit(solution)/shard_map/ppermute | solution.py:385
  17.2 0.1 collective-permute-start.4
  17.3 0.0 collective-permute-done.refs_1_
  17.3 0.6 collective-permute-start.3
  17.9 0.9 collective-permute-done.4
  18.8 0.3 collective-permute-done.3
  19.1 0.0 copy-start
  19.1 5.2 %shard_map.114.refs_0_ = bf16[3,128,512]{2,1,0:T(8,128)(2,1)S(1)} custom-call(bf16[16,3584]{1,0:T(8,128)(2,1)S(1)} %get-tuple-element.46.refs_0_, bf16[16,3584]{1,0:T(8,128)(2,1)S(1)} %collective-permute-done.refs_1_, bf16[16,3584]{1,0:T(8,128)(2,1)S(1)} %collective-permute-done.1.refs_2_, bf16[16,3584]{1,0:T(8,128)(2,1)S(1)} %collective-permute-done.2.refs_3_, ...), custom_call_target="tpu_custom_call" | custom-call | flops 1 | bytes 1 | tf_op jit(solution)/shard_map/pallas_call | solution.py:193
  24.3 1.6 %collective-permute-start.9 = (bf16[2,128,512]{2,1,0:T(8,128)(2,1)S(1)}, bf16[2,128,512]{2,1,0:T(8,128)(2,1)S(1)}, u32[]{:S(2)}, u32[]{:S(2)}) collective-permute-start(bf16[2,128,512]{2,1,0:T(8,128)(2,1)S(1)} %slice.8), channel_id=1, source_target_pairs={{0,16},{8,24},{1,17},{9,25},{2,18},{10,26},{3,19},{11,27},{4,20},{... | collective-permute-start | bytes 786440 | tf_op jit(solution)/shard_map/ppermute | solution.py:78
  25.9 3.4 %collective-permute-start.8 = (bf16[2,128,512]{2,1,0:T(8,128)(2,1)S(1)}, bf16[2,128,512]{2,1,0:T(8,128)(2,1)S(1)}, u32[]{:S(2)}, u32[]{:S(2)}) collective-permute-start(bf16[2,128,512]{2,1,0:T(8,128)(2,1)S(1)} %slice.8), channel_id=1, source_target_pairs={{0,8},{16,24},{1,9},{17,25},{2,10},{18,26},{3,11},{19,27},{4,12},{... | collective-permute-start | bytes 786440 | tf_op jit(solution)/shard_map/ppermute | solution.py:77
  29.3 1.6 %collective-permute-done.6.refs_2_ = bf16[48,3584]{1,0:T(8,128)(2,1)S(1)} collective-permute-done((bf16[48,3584]{1,0:T(8,128)(2,1)S(1)}, bf16[48,3584]{1,0:T(8,128)(2,1)S(1)}, u32[]{:S(2)}, u32[]{:S(2)}) %collective-permute-start.6) | collective-permute-done | bytes 344096 | tf_op jit(solution)/shard_map/ppermute | solution.py:385
  30.9 0.0 collective-permute-done.5.refs_1_
  30.9 0.1 pad_maximum_fusion
  31.0 0.1 collective-permute-start.7
  31.1 3.9 %collective-permute-done.9.refs_4_ = bf16[2,128,512]{2,1,0:T(8,128)(2,1)S(1)} collective-permute-done((bf16[2,128,512]{2,1,0:T(8,128)(2,1)S(1)}, bf16[2,128,512]{2,1,0:T(8,128)(2,1)S(1)}, u32[]{:S(2)}, u32[]{:S(2)}) %collective-permute-start.9) | collective-permute-done | bytes 262176 | tf_op jit(solution)/shard_map/ppermute | solution.py:78
  35.0 0.3 collective-permute-done.8.refs_3_
  35.3 0.1 collective-permute-start.10
  35.4 4.6 %collective-permute-start.11 = (bf16[2,128,512]{2,1,0:T(8,128)(2,1)S(1)}, bf16[2,128,512]{2,1,0:T(8,128)(2,1)S(1)}, u32[]{:S(2)}, u32[]{:S(2)}) collective-permute-start(bf16[2,128,512]{2,1,0:T(8,128)(2,1)S(1)} %collective-permute-done.9.refs_4_), channel_id=1, source_target_pairs={{24,16},{16,24},{25,17},{17,25},{26,18},{18,26},{27,19},{19,27},{2... | collective-permute-start | bytes 786440 | tf_op jit(solution)/shard_map/ppermute | solution.py:79
  40.0 0.0 collective-permute-done.7.refs_3_
  40.0 3.4 %shard_map.115.refs_1_ = bf16[3,288,512]{2,1,0:T(8,128)(2,1)S(1)} custom-call(bf16[48,3584]{1,0:T(8,128)(2,1)S(1)} %get-tuple-element.47.refs_0_, bf16[48,3584]{1,0:T(8,128)(2,1)S(1)} %collective-permute-done.5.refs_1_, bf16[48,3584]{1,0:T(8,128)(2,1)S(1)} %collective-permute-done.6.refs_2_, bf16[144,3584]{1,0:T(8,128)(2,1)S(1)} %collective-permute-done.7.refs_3_, ...), custom_call_target="tpu_custom_call" | custom-call | flops 1 | bytes 1 | tf_op jit(solution)/shard_map/pallas_call | solution.py:193
  43.4 0.0 copy-start.6
  43.4 0.0 copy-start.7
  43.5 2.3 %collective-permute-done.11.refs_5_ = bf16[2,128,512]{2,1,0:T(8,128)(2,1)S(1)} collective-permute-done((bf16[2,128,512]{2,1,0:T(8,128)(2,1)S(1)}, bf16[2,128,512]{2,1,0:T(8,128)(2,1)S(1)}, u32[]{:S(2)}, u32[]{:S(2)}) %collective-permute-start.11) | collective-permute-done | bytes 262176 | tf_op jit(solution)/shard_map/ppermute | solution.py:79
  45.7 1.7 %collective-permute-done.12.refs_1_ = bf16[48,3584]{1,0:T(8,128)(2,1)S(1)} collective-permute-done((bf16[48,3584]{1,0:T(8,128)(2,1)S(1)}, bf16[48,3584]{1,0:T(8,128)(2,1)S(1)}, u32[]{:S(2)}, u32[]{:S(2)}) %collective-permute-start.12) | collective-permute-done | bytes 344096 | tf_op jit(solution)/shard_map/ppermute | solution.py:62
  47.4 1.9 %shard_map.116.refs_2_ = bf16[3,96,512]{2,1,0:T(8,128)(2,1)S(1)} custom-call(bf16[48,3584]{1,0:T(8,128)(2,1)S(1)} %collective-permute-done.10.refs_0_, bf16[48,3584]{1,0:T(8,128)(2,1)S(1)} %collective-permute-done.12.refs_1_, f32[2,512]{1,0:T(2,128)S(1)} %copy-done.5, bf16[3,3584,512]{2,1,0:T(8,128)(2,1)S(1)} %bitcast.10), custom_call_target="tpu_custom_call" | custom-call | flops 1 | bytes 1 | tf_op jit(solution)/shard_map/pallas_call | solution.py:193
  49.3 2.9 %shard_map.117 = (bf16[256,512]{1,0:T(8,128)(2,1)S(1)}, bf16[512,3584]{1,0:T(8,128)(2,1)S(1)}) custom-call(s32[1]{0:T(128)} %bitcast.3.clip, s32[4,4]{1,0:T(4,128)S(1)} %copy-done.6, s32[4]{0:T(128)S(1)} %copy-done.7, bf16[3,128,512]{2,1,0:T(8,128)(2,1)S(1)} %shard_map.114.refs_0_, bf16[3,288,512]{2,1,0:T(8,128)(2,1)S(1)} %shard_map.115.refs_1_, ...), custom_call_target="tpu_custom_call" | custom-call | flops 1 | bytes 1 | tf_op jit(solution)/shard_map/pallas_call | solution.py:257
  52.2 1.1 %shard_map.118 = (bf16[32,3584]{1,0:T(8,128)(2,1)S(1)}, bf16[32,3584]{1,0:T(8,128)(2,1)S(1)}, bf16[32,3584]{1,0:T(8,128)(2,1)S(1)}, bf16[32,3584]{1,0:T(8,128)(2...) custom-call(bf16[256,512]{1,0:T(8,128)(2,1)S(1)} %get-tuple-element.55.attended, ...), custom_call_target="tpu_custom_call" | custom-call | flops 1 | bytes 1 | tf_op jit(solution)/shard_map/pallas_call | solution.py:288
  53.3 0.2 collective-permute-start.13
  53.5 0.4 collective-permute-start.14
  53.9 2.0 %collective-permute-done.14.refs_1_.refs_4_ = bf16[32,3584]{1,0:T(8,128)(2,1)S(1)} collective-permute-done((bf16[32,3584]{1,0:T(8,128)(2,1)S(1)}, bf16[32,3584]{1,0:T(8,128)(2,1)S(1)}, u32[]{:S(2)}, u32[]{:S(2)}) %collective-permute-start.14) | collective-permute-done | bytes 229408 | tf_op jit(solution)/shard_map/ppermute | solution.py:62
  55.9 0.1 shard_map.119
  55.9 1.8 %collective-permute-start.15 = (bf16[32,3584]{1,0:T(8,128)(2,1)S(1)}, bf16[32,3584]{1,0:T(8,128)(2,1)S(1)}, u32[]{:S(2)}, u32[]{:S(2)}) collective-permute-start(bf16[32,3584]{1,0:T(8,128)(2,1)S(1)} %shard_map.119), channel_id=1, source_target_pairs={{2,0},{3,1},{0,2},{1,3},{6,4},{7,5},{4,6},{5,7},{10,8},{11,9},{8,1... | collective-permute-start | bytes 688136 | tf_op jit(solution)/shard_map/ppermute | solution.py:428
  57.7 2.9 %shard_map.122 = (bf16[256,512]{1,0:T(8,128)(2,1)S(1)}, bf16[512,3584]{1,0:T(8,128)(2,1)S(1)}) custom-call(s32[1]{0:T(128)} %bitcast.3.clip, s32[4,4]{1,0:T(4,128)S(1)} %copy-done.6, s32[4]{0:T(128)S(1)} %copy-done.7, bf16[3,128,512]{2,1,0:T(8,128)(2,1)S(1)} %shard_map.114.refs_0_, bf16[3,288,512]{2,1,0:T(8,128)(2,1)S(1)} %shard_map.115.refs_1_, ...), custom_call_target="tpu_custom_call" | custom-call | flops 1 | bytes 1 | tf_op jit(solution)/shard_map/pallas_call | solution.py:257
  60.6 1.1 %shard_map.123 = (bf16[32,3584]{1,0:T(8,128)(2,1)S(1)}, bf16[32,3584]{1,0:T(8,128)(2,1)S(1)}, bf16[32,3584]{1,0:T(8,128)(2,1)S(1)}, bf16[32,3584]{1,0:T(8,128)(2...) custom-call(bf16[256,512]{1,0:T(8,128)(2,1)S(1)} %get-tuple-element.69.attended, ...), custom_call_target="tpu_custom_call" | custom-call | flops 1 | bytes 1 | tf_op jit(solution)/shard_map/pallas_call | solution.py:288
  61.7 0.0 copy-start.1
  61.7 0.0 copy-start.2
  61.8 0.0 copy-start.3
  61.8 0.1 collective-permute-start.19
  61.8 1.8 %collective-permute-done.15.refs_5_ = bf16[32,3584]{1,0:T(8,128)(2,1)S(1)} collective-permute-done((bf16[32,3584]{1,0:T(8,128)(2,1)S(1)}, bf16[32,3584]{1,0:T(8,128)(2,1)S(1)}, u32[]{:S(2)}, u32[]{:S(2)}) %collective-permute-start.15) | collective-permute-done | bytes 229408 | tf_op jit(solution)/shard_map/ppermute | solution.py:428
  63.6 0.2 shard_map.120
  63.8 0.1 collective-permute-start.20
  63.9 1.8 %collective-permute-start.16 = (bf16[32,3584]{1,0:T(8,128)(2,1)S(1)}, bf16[32,3584]{1,0:T(8,128)(2,1)S(1)}, u32[]{:S(2)}, u32[]{:S(2)}) collective-permute-start(bf16[32,3584]{1,0:T(8,128)(2,1)S(1)} %get-tuple-element.64), channel_id=1, source_target_pairs={{4,0},{5,1},{6,4},{7,5},{2,6},{3,7},{0,2},{1,3},{12,8},{13,9},{14,... | collective-permute-start | bytes 688136 | tf_op jit(solution)/shard_map/ppermute | solution.py:447
  65.7 1.3 %collective-permute-start.17 = (bf16[32,3584]{1,0:T(8,128)(2,1)S(1)}, bf16[32,3584]{1,0:T(8,128)(2,1)S(1)}, u32[]{:S(2)}, u32[]{:S(2)}) collective-permute-start(bf16[32,3584]{1,0:T(8,128)(2,1)S(1)} %get-tuple-element.65), channel_id=1, source_target_pairs={{2,0},{3,1},{6,2},{7,3},{4,6},{5,7},{0,4},{1,5},{10,8},{11,9},{14,... | collective-permute-start | bytes 688136 | tf_op jit(solution)/shard_map/ppermute | solution.py:447
  67.0 0.1 shard_map.124
  67.0 0.8 collective-permute-start.21
  67.8 5.4 %collective-permute-done.16.refs_2_ = bf16[32,3584]{1,0:T(8,128)(2,1)S(1)} collective-permute-done((bf16[32,3584]{1,0:T(8,128)(2,1)S(1)}, bf16[32,3584]{1,0:T(8,128)(2,1)S(1)}, u32[]{:S(2)}, u32[]{:S(2)}) %collective-permute-start.16) | collective-permute-done | bytes 229408 | tf_op jit(solution)/shard_map/ppermute | solution.py:447
  73.2 4.9 %collective-permute-done.17.refs_3_ = bf16[32,3584]{1,0:T(8,128)(2,1)S(1)} collective-permute-done((bf16[32,3584]{1,0:T(8,128)(2,1)S(1)}, bf16[32,3584]{1,0:T(8,128)(2,1)S(1)}, u32[]{:S(2)}, u32[]{:S(2)}) %collective-permute-start.17) | collective-permute-done | bytes 229408 | tf_op jit(solution)/shard_map/ppermute | solution.py:447
  78.1 0.0 copy-start.4
  78.1 0.4 shard_map.121
  78.5 4.5 %collective-permute-done.21.refs_5_ = bf16[32,3584]{1,0:T(8,128)(2,1)S(1)} collective-permute-done((bf16[32,3584]{1,0:T(8,128)(2,1)S(1)}, bf16[32,3584]{1,0:T(8,128)(2,1)S(1)}, u32[]{:S(2)}, u32[]{:S(2)}) %collective-permute-start.21) | collective-permute-done | bytes 229408 | tf_op jit(solution)/shard_map/ppermute | solution.py:428
  82.9 0.2 shard_map.125
  83.1 1.8 %collective-permute-start.23 = (bf16[32,3584]{1,0:T(8,128)(2,1)S(1)}, bf16[32,3584]{1,0:T(8,128)(2,1)S(1)}, u32[]{:S(2)}, u32[]{:S(2)}) collective-permute-start(bf16[32,3584]{1,0:T(8,128)(2,1)S(1)} %get-tuple-element.81), channel_id=1, source_target_pairs={{2,0},{3,1},{6,2},{7,3},{4,6},{5,7},{0,4},{1,5},{10,8},{11,9},{14,... | collective-permute-start | bytes 688136 | tf_op jit(solution)/shard_map/ppermute | solution.py:447
  84.9 0.3 collective-permute-start.22
  85.2 3.6 %collective-permute-start.18 = (bf16[16,96]{1,0:T(8,128)(2,1)S(1)}, bf16[16,96]{1,0:T(8,128)(2,1)S(1)}, u32[]{:S(2)}, u32[]{:S(2)}) collective-permute-start(bf16[16,96]{1,0:T(8,128)(2,1)S(1)} %slice.7), channel_id=1, source_target_pairs={{0,8},{8,16},{16,24},{1,9},{9,17},{17,25},{2,10},{10,18},{18,26},{... | collective-permute-start | bytes 9224 | tf_op jit(solution)/shard_map/ppermute | solution.py:68
  88.8 2.8 %collective-permute-done.18.earlier = bf16[16,96]{1,0:T(8,128)(2,1)S(1)} collective-permute-done((bf16[16,96]{1,0:T(8,128)(2,1)S(1)}, bf16[16,96]{1,0:T(8,128)(2,1)S(1)}, u32[]{:S(2)}, u32[]{:S(2)}) %collective-permute-start.18) | collective-permute-done | bytes 3104 | tf_op jit(solution)/shard_map/ppermute | solution.py:68
  91.6 0.0 collective-permute-done.23.refs_3_
  91.6 4.7 %collective-permute-done.22.refs_2_ = bf16[32,3584]{1,0:T(8,128)(2,1)S(1)} collective-permute-done((bf16[32,3584]{1,0:T(8,128)(2,1)S(1)}, bf16[32,3584]{1,0:T(8,128)(2,1)S(1)}, u32[]{:S(2)}, u32[]{:S(2)}) %collective-permute-start.22) | collective-permute-done | bytes 229408 | tf_op jit(solution)/shard_map/ppermute | solution.py:447
  96.3 1.3 %shard_map.126 = (bf16[64,3584]{1,0:T(8,128)(2,1)}, bf16[64,384]{1,0:T(8,128)(2,1)}) custom-call(s32[1]{0:T(128)S(6)} %copy.12.level, bf16[64,3584]{1,0:T(8,128)(2,1)S(1)} %bitcast.16, f32[3,16,3584]{2,1,0:T(8,128)S(1)} %bitcast.13, bf16[96,3584]{1,0:T(8,128)(2,1)S(1)} %bitcast.18, bf16[3,96,384]{2,1,0:T(8,128)(2,1)S(1)} %copy-done.4, ...), custom_call_target="tpu_custom_call" | custom-call | flops 1 | bytes 1 | tf_op jit(solution)/shard_map/pallas_call | solution.py:352
  (22 shorter events, 0.2 us)
Async XLA Ops:
  0.6 18.5 %copy-start.5 = (f32[2,512]{1,0:T(2,128)S(1)}, f32[2,512]{1,0:T(2,128)}, u32[]{:S(2)}) copy-start(f32[2,512]{1,0:T(2,128)} %refs_2_.1) | copy-start | bytes 12292
  2.8 9.5 %collective-permute-start.2 = (bf16[16,3584]{1,0:T(8,128)(2,1)S(1)}, bf16[16,3584]{1,0:T(8,128)(2,1)S(1)}, u32[]{:S(2)}, u32[]{:S(2)}) collective-permute-start(bf16[16,3584]{1,0:T(8,128)(2,1)S(1)} %get-tuple-element.46.refs_0_), channel_id=1, source_target_pairs={{4,2},{5,3},{6,0},{7,1},{0,6},{1,7},{2,4},{3,5},{12,10},{13,11},{1... | collective-permute-start | bytes 344072 | tf_op jit(solution)/shard_map/ppermute | solution.py:385
  6.5 10.7 %collective-permute-start.1 = (bf16[16,3584]{1,0:T(8,128)(2,1)S(1)}, bf16[16,3584]{1,0:T(8,128)(2,1)S(1)}, u32[]{:S(2)}, u32[]{:S(2)}) collective-permute-start(bf16[16,3584]{1,0:T(8,128)(2,1)S(1)} %get-tuple-element.46.refs_0_), channel_id=1, source_target_pairs={{0,2},{1,3},{2,6},{3,7},{6,4},{7,5},{4,0},{5,1},{8,10},{9,11},{10,... | collective-permute-start | bytes 344072 | tf_op jit(solution)/shard_map/ppermute | solution.py:385
  6.5 10.8 %collective-permute-start = (bf16[16,3584]{1,0:T(8,128)(2,1)S(1)}, bf16[16,3584]{1,0:T(8,128)(2,1)S(1)}, u32[]{:S(2)}, u32[]{:S(2)}) collective-permute-start(bf16[16,3584]{1,0:T(8,128)(2,1)S(1)} %get-tuple-element.46.refs_0_), channel_id=1, source_target_pairs={{0,4},{1,5},{4,6},{5,7},{6,2},{7,3},{2,0},{3,1},{8,12},{9,13},{12,... | collective-permute-start | bytes 344072 | tf_op jit(solution)/shard_map/ppermute | solution.py:385
  9.4 21.5 %collective-permute-start.6 = (bf16[48,3584]{1,0:T(8,128)(2,1)S(1)}, bf16[48,3584]{1,0:T(8,128)(2,1)S(1)}, u32[]{:S(2)}, u32[]{:S(2)}) collective-permute-start(bf16[48,3584]{1,0:T(8,128)(2,1)S(1)} %get-tuple-element.47.refs_0_), channel_id=1, source_target_pairs={{0,2},{1,3},{2,6},{3,7},{6,4},{7,5},{4,0},{5,1},{8,10},{9,11},{10,... | collective-permute-start | bytes 1032200 | tf_op jit(solution)/shard_map/ppermute | solution.py:385
  9.4 21.5 %collective-permute-start.5 = (bf16[48,3584]{1,0:T(8,128)(2,1)S(1)}, bf16[48,3584]{1,0:T(8,128)(2,1)S(1)}, u32[]{:S(2)}, u32[]{:S(2)}) collective-permute-start(bf16[48,3584]{1,0:T(8,128)(2,1)S(1)} %get-tuple-element.47.refs_0_), channel_id=1, source_target_pairs={{0,4},{1,5},{4,6},{5,7},{6,2},{7,3},{2,0},{3,1},{8,12},{9,13},{12,... | collective-permute-start | bytes 1032200 | tf_op jit(solution)/shard_map/ppermute | solution.py:385
  17.2 1.6 %collective-permute-start.4 = (bf16[32,3584]{1,0:T(8,128)(2,1)S(1)}, bf16[32,3584]{1,0:T(8,128)(2,1)S(1)}, u32[]{:S(2)}, u32[]{:S(2)}) collective-permute-start(bf16[32,3584]{1,0:T(8,128)(2,1)S(1)} %pad_maximum_fusion.2), channel_id=1, source_target_pairs={{0,1},{1,0},{2,3},{3,2},{4,5},{5,4},{6,7},{7,6},{8,9},{9,8},{10,11... | collective-permute-start | bytes 688136 | tf_op jit(solution)/shard_map/ppermute | solution.py:62
  17.3 1.8 %collective-permute-start.3 = (bf16[32,3584]{1,0:T(8,128)(2,1)S(1)}, bf16[32,3584]{1,0:T(8,128)(2,1)S(1)}, u32[]{:S(2)}, u32[]{:S(2)}) collective-permute-start(bf16[32,3584]{1,0:T(8,128)(2,1)S(1)} %pad_maximum_fusion.1), channel_id=1, source_target_pairs={{0,1},{1,0},{2,3},{3,2},{4,5},{5,4},{6,7},{7,6},{8,9},{9,8},{10,11... | collective-permute-start | bytes 688136 | tf_op jit(solution)/shard_map/ppermute | solution.py:62
  19.1 20.9 %copy-start = (bf16[3584,3,512]{2,0,1:T(8,128)(2,1)S(1)}, bf16[3584,3,512]{2,0,1:T(8,128)(2,1)}, u32[]{:S(2)}) copy-start(bf16[3584,3,512]{2,0,1:T(8,128)(2,1)} %param.15) | copy-start | bytes 33030148
  24.3 10.7 %collective-permute-start.9 = (bf16[2,128,512]{2,1,0:T(8,128)(2,1)S(1)}, bf16[2,128,512]{2,1,0:T(8,128)(2,1)S(1)}, u32[]{:S(2)}, u32[]{:S(2)}) collective-permute-start(bf16[2,128,512]{2,1,0:T(8,128)(2,1)S(1)} %slice.8), channel_id=1, source_target_pairs={{0,16},{8,24},{1,17},{9,25},{2,18},{10,26},{3,19},{11,27},{4,20},{... | collective-permute-start | bytes 786440 | tf_op jit(solution)/shard_map/ppermute | solution.py:78
  25.9 9.4 %collective-permute-start.8 = (bf16[2,128,512]{2,1,0:T(8,128)(2,1)S(1)}, bf16[2,128,512]{2,1,0:T(8,128)(2,1)S(1)}, u32[]{:S(2)}, u32[]{:S(2)}) collective-permute-start(bf16[2,128,512]{2,1,0:T(8,128)(2,1)S(1)} %slice.8), channel_id=1, source_target_pairs={{0,8},{16,24},{1,9},{17,25},{2,10},{18,26},{3,11},{19,27},{4,12},{... | collective-permute-start | bytes 786440 | tf_op jit(solution)/shard_map/ppermute | solution.py:77
  31.0 9.0 %collective-permute-start.7 = (bf16[144,3584]{1,0:T(8,128)(2,1)S(1)}, bf16[144,3584]{1,0:T(8,128)(2,1)S(1)}, u32[]{:S(2)}, u32[]{:S(2)}) collective-permute-start(bf16[144,3584]{1,0:T(8,128)(2,1)S(1)} %pad_maximum_fusion), channel_id=1, source_target_pairs={{0,1},{1,0},{2,3},{3,2},{4,5},{5,4},{6,7},{7,6},{8,9},{9,8},{10,11... | collective-permute-start | bytes 3096584 | tf_op jit(solution)/shard_map/ppermute | solution.py:62
  35.3 10.4 %collective-permute-start.10 = (bf16[48,3584]{1,0:T(8,128)(2,1)S(1)}, bf16[48,3584]{1,0:T(8,128)(2,1)S(1)}, u32[]{:S(2)}, u32[]{:S(2)}) collective-permute-start(bf16[48,3584]{1,0:T(8,128)(2,1)S(1)} %broadcast_select_fusion), channel_id=1, source_target_pairs={{0,2},{1,3},{2,0},{3,1},{4,6},{5,7},{6,4},{7,5},{8,10},{9,11},{10,... | collective-permute-start | bytes 1032200 | tf_op jit(solution)/shard_map/ppermute | solution.py:385
  35.4 10.3 %collective-permute-start.11 = (bf16[2,128,512]{2,1,0:T(8,128)(2,1)S(1)}, bf16[2,128,512]{2,1,0:T(8,128)(2,1)S(1)}, u32[]{:S(2)}, u32[]{:S(2)}) collective-permute-start(bf16[2,128,512]{2,1,0:T(8,128)(2,1)S(1)} %collective-permute-done.9.refs_4_), channel_id=1, source_target_pairs={{24,16},{16,24},{25,17},{17,25},{26,18},{18,26},{27,19},{19,27},{2... | collective-permute-start | bytes 786440 | tf_op jit(solution)/shard_map/ppermute | solution.py:79
  43.4 5.8 %copy-start.6 = (s32[4,4]{1,0:T(4,128)S(1)}, s32[4,4]{1,0:T(4,128)}, u32[]{:S(2)}) copy-start(s32[4,4]{1,0:T(4,128)} %visible.3) | copy-start | bytes 196
  43.4 5.8 %copy-start.7 = (s32[4]{0:T(128)S(1)}, s32[4]{0:T(128)}, u32[]{:S(2)}) copy-start(s32[4]{0:T(128)} %counts.3) | copy-start | bytes 52
  45.7 1.7 %collective-permute-start.12 = (bf16[48,3584]{1,0:T(8,128)(2,1)S(1)}, bf16[48,3584]{1,0:T(8,128)(2,1)S(1)}, u32[]{:S(2)}, u32[]{:S(2)}) collective-permute-start(bf16[48,3584]{1,0:T(8,128)(2,1)S(1)} %collective-permute-done.10.refs_0_), channel_id=1, source_target_pairs={{0,1},{1,0},{2,3},{3,2},{4,5},{5,4},{6,7},{7,6},{8,9},{9,8},{10,11... | collective-permute-start | bytes 1032200 | tf_op jit(solution)/shard_map/ppermute | solution.py:62
  53.3 10.3 %collective-permute-start.13 = (bf16[96,3584]{1,0:T(8,128)(2,1)S(1)}, bf16[96,3584]{1,0:T(8,128)(2,1)S(1)}, u32[]{:S(2)}, u32[]{:S(2)}) collective-permute-start(bf16[96,3584]{1,0:T(8,128)(2,1)S(1)} %get-tuple-element.58), channel_id=1, source_target_pairs={{0,1},{1,0},{2,3},{3,2},{4,5},{5,4},{6,7},{7,6},{8,9},{9,8},{10,11... | collective-permute-start | bytes 2064392 | tf_op jit(solution)/shard_map/ppermute | solution.py:62
  53.5 2.3 %collective-permute-start.14 = (bf16[32,3584]{1,0:T(8,128)(2,1)S(1)}, bf16[32,3584]{1,0:T(8,128)(2,1)S(1)}, u32[]{:S(2)}, u32[]{:S(2)}) collective-permute-start(bf16[32,3584]{1,0:T(8,128)(2,1)S(1)} %get-tuple-element.63), channel_id=1, source_target_pairs={{0,1},{1,0},{2,3},{3,2},{4,5},{5,4},{6,7},{7,6},{8,9},{9,8},{10,11... | collective-permute-start | bytes 688136 | tf_op jit(solution)/shard_map/ppermute | solution.py:62
  55.9 7.7 %collective-permute-start.15 = (bf16[32,3584]{1,0:T(8,128)(2,1)S(1)}, bf16[32,3584]{1,0:T(8,128)(2,1)S(1)}, u32[]{:S(2)}, u32[]{:S(2)}) collective-permute-start(bf16[32,3584]{1,0:T(8,128)(2,1)S(1)} %shard_map.119), channel_id=1, source_target_pairs={{2,0},{3,1},{0,2},{1,3},{6,4},{7,5},{4,6},{5,7},{10,8},{11,9},{8,1... | collective-permute-start | bytes 688136 | tf_op jit(solution)/shard_map/ppermute | solution.py:428
  61.7 16.4 %copy-start.1 = (f32[16,3,3584]{2,0,1:T(8,128)S(1)}, f32[16,3,3584]{2,0,1:T(8,128)}, u32[]{:S(2)}) copy-start(f32[16,3,3584]{2,0,1:T(8,128)} %param.14) | copy-start | bytes 2064388
  61.7 16.3 %copy-start.2 = (bf16[1,64,3584]{2,1,0:T(8,128)(2,1)S(1)}, bf16[1,64,3584]{2,1,0:T(8,128)(2,1)}, u32[]{:S(2)}) copy-start(bf16[1,64,3584]{2,1,0:T(8,128)(2,1)} %param.10) | copy-start | bytes 1376260
  61.8 16.3 %copy-start.3 = (bf16[3584,96]{0,1:T(8,128)(2,1)S(1)}, bf16[3584,96]{0,1:T(8,128)(2,1)}, u32[]{:S(2)}) copy-start(bf16[3584,96]{0,1:T(8,128)(2,1)} %param.18) | copy-start | bytes 2064388
  61.8 16.7 %collective-permute-start.19 = (bf16[96,3584]{1,0:T(8,128)(2,1)S(1)}, bf16[96,3584]{1,0:T(8,128)(2,1)S(1)}, u32[]{:S(2)}, u32[]{:S(2)}) collective-permute-start(bf16[96,3584]{1,0:T(8,128)(2,1)S(1)} %get-tuple-element.72), channel_id=1, source_target_pairs={{0,1},{1,0},{2,3},{3,2},{4,5},{5,4},{6,7},{7,6},{8,9},{9,8},{10,11... | collective-permute-start | bytes 2064392 | tf_op jit(solution)/shard_map/ppermute | solution.py:62
  63.8 3.1 %collective-permute-start.20 = (bf16[32,3584]{1,0:T(8,128)(2,1)S(1)}, bf16[32,3584]{1,0:T(8,128)(2,1)S(1)}, u32[]{:S(2)}, u32[]{:S(2)}) collective-permute-start(bf16[32,3584]{1,0:T(8,128)(2,1)S(1)} %get-tuple-element.77), channel_id=1, source_target_pairs={{0,1},{1,0},{2,3},{3,2},{4,5},{5,4},{6,7},{7,6},{8,9},{9,8},{10,11... | collective-permute-start | bytes 688136 | tf_op jit(solution)/shard_map/ppermute | solution.py:62
  63.9 9.3 %collective-permute-start.16 = (bf16[32,3584]{1,0:T(8,128)(2,1)S(1)}, bf16[32,3584]{1,0:T(8,128)(2,1)S(1)}, u32[]{:S(2)}, u32[]{:S(2)}) collective-permute-start(bf16[32,3584]{1,0:T(8,128)(2,1)S(1)} %get-tuple-element.64), channel_id=1, source_target_pairs={{4,0},{5,1},{6,4},{7,5},{2,6},{3,7},{0,2},{1,3},{12,8},{13,9},{14,... | collective-permute-start | bytes 688136 | tf_op jit(solution)/shard_map/ppermute | solution.py:447
  65.7 12.4 %collective-permute-start.17 = (bf16[32,3584]{1,0:T(8,128)(2,1)S(1)}, bf16[32,3584]{1,0:T(8,128)(2,1)S(1)}, u32[]{:S(2)}, u32[]{:S(2)}) collective-permute-start(bf16[32,3584]{1,0:T(8,128)(2,1)S(1)} %get-tuple-element.65), channel_id=1, source_target_pairs={{2,0},{3,1},{6,2},{7,3},{4,6},{5,7},{0,4},{1,5},{10,8},{11,9},{14,... | collective-permute-start | bytes 688136 | tf_op jit(solution)/shard_map/ppermute | solution.py:447
  67.0 15.9 %collective-permute-start.21 = (bf16[32,3584]{1,0:T(8,128)(2,1)S(1)}, bf16[32,3584]{1,0:T(8,128)(2,1)S(1)}, u32[]{:S(2)}, u32[]{:S(2)}) collective-permute-start(bf16[32,3584]{1,0:T(8,128)(2,1)S(1)} %shard_map.124), channel_id=1, source_target_pairs={{2,0},{3,1},{0,2},{1,3},{6,4},{7,5},{4,6},{5,7},{10,8},{11,9},{8,1... | collective-permute-start | bytes 688136 | tf_op jit(solution)/shard_map/ppermute | solution.py:428
  78.1 18.2 %copy-start.4 = (bf16[3,96,384]{2,1,0:T(8,128)(2,1)S(1)}, bf16[3,96,384]{2,1,0:T(8,128)(2,1)}, u32[]{:S(2)}) copy-start(bf16[3,96,384]{2,1,0:T(8,128)(2,1)} %weight.1) | copy-start | bytes 663556
  83.1 8.5 %collective-permute-start.23 = (bf16[32,3584]{1,0:T(8,128)(2,1)S(1)}, bf16[32,3584]{1,0:T(8,128)(2,1)S(1)}, u32[]{:S(2)}, u32[]{:S(2)}) collective-permute-start(bf16[32,3584]{1,0:T(8,128)(2,1)S(1)} %get-tuple-element.81), channel_id=1, source_target_pairs={{2,0},{3,1},{6,2},{7,3},{4,6},{5,7},{0,4},{1,5},{10,8},{11,9},{14,... | collective-permute-start | bytes 688136 | tf_op jit(solution)/shard_map/ppermute | solution.py:447
  84.9 11.4 %collective-permute-start.22 = (bf16[32,3584]{1,0:T(8,128)(2,1)S(1)}, bf16[32,3584]{1,0:T(8,128)(2,1)S(1)}, u32[]{:S(2)}, u32[]{:S(2)}) collective-permute-start(bf16[32,3584]{1,0:T(8,128)(2,1)S(1)} %get-tuple-element.79), channel_id=1, source_target_pairs={{4,0},{5,1},{6,4},{7,5},{2,6},{3,7},{0,2},{1,3},{12,8},{13,9},{14,... | collective-permute-start | bytes 688136 | tf_op jit(solution)/shard_map/ppermute | solution.py:447
  85.2 6.4 %collective-permute-start.18 = (bf16[16,96]{1,0:T(8,128)(2,1)S(1)}, bf16[16,96]{1,0:T(8,128)(2,1)S(1)}, u32[]{:S(2)}, u32[]{:S(2)}) collective-permute-start(bf16[16,96]{1,0:T(8,128)(2,1)S(1)} %slice.7), channel_id=1, source_target_pairs={{0,8},{8,16},{16,24},{1,9},{9,17},{17,25},{2,10},{10,18},{18,26},{... | collective-permute-start | bytes 9224 | tf_op jit(solution)/shard_map/ppermute | solution.py:68

commit v5 on v4

--- a/solution.py
+++ b/solution.py
@@ -474,7 +474,7 @@
     lead_part = project(leads, qk_gain, weight)
     packed, origins = from_earlier(lead_part[1:])
 
-    last = take(table[-1], body, [after(tile, *packed[:2]) for tile in held], mask[-1])
+    last = take(table[-1], body, [after(tile, lead_part) for tile in held], mask[-1])
     first = [body] + [after(tile, lead_part) for tile in held]
     across = over_core(jnp.concatenate(first, 0))
     early_part = project([body] + held + [across], qk_gain, weight, False)

time: 99 us -> 97.1 us (0.981)
  starting transfers between devices: 31.9 us -> 29.8 us
  waiting for transfers between devices: 41.7 us -> 42.7 us
    ppermute x2, starting transfers between devices: 2.59 us -> 0.44 us  [passed_back(): came = lax.ppermute(sums, 'tok', lanes(back(pairs)))]
    ppermute x2, waiting for transfers between devices: 6.24 us -> 7.83 us  [passed_back(): came = lax.ppermute(sums, 'tok', lanes(back(pairs)))]
where the time goes in v5:
time: 97.1 us; the launch traced here: 96.5 us
  waiting for transfers between devices  42.7 us (44%)
  starting transfers between devices  29.8 us (31%)
  Pallas kernels  22.2 us (23%)
  between operations  1.62 us (2%)
    ppermute x4, waiting for transfers between devices, sent_home(): lax.ppermute(term, 'tok', lanes(back(pairs)))  14.5 us
    pallas_call x3, Pallas kernels, project(): pl.pallas_call(functools.partial(project_kernel, len(tiles), load), in_sp...  10.4 us
    ppermute x6, starting transfers between devices, take(): return lax.ppermute(tile, 'tok', lanes(pairs))  9.59 us
    ppermute x2, waiting for transfers between devices, passed_back(): came = lax.ppermute(sums, 'tok', lanes(back(pairs)))  7.83 us
    ppermute x6, waiting for transfers between devices, take(): return lax.ppermute(tile, 'tok', lanes(pairs))  6.43 us
    pallas_call x2, Pallas kernels, attend(): pl.pallas_call(functools.partial(attend_kernel, cuts, len(parts), origins...  5.8 us
    ppermute x4, starting transfers between devices, sent_home(): lax.ppermute(term, 'tok', lanes(back(pairs)))  5.06 us
    ppermute x8, waiting for transfers between devices, over_core(): return lax.ppermute(array, 'tok', [(i, i ^ 1) for i in range(devices)])  4.82 us
  transfers between devices with their start and end apart: 24, of which 15 were waited for; matrix products, arithmetic and copies ran while one was open for 0% of the time, Pallas kernels for 14%

profile of v5, /device:TPU:4, one launch (start us, length us, event | category | flops | bytes accessed | tf_op | source)
XLA Modules:
  0.0 96.5 jit_solution(16775669779804380704)
XLA Ops:
  1.3 1.5 %shard_map.113 = (bf16[16,3584]{1,0:T(8,128)(2,1)S(1)}, bf16[48,3584]{1,0:T(8,128)(2,1)S(1)}) custom-call(s32[1]{0:T(128)S(6)} %copy.12.level, bf16[64,3584]{1,0:T(8,128)(2,1)} %bitcast.14, f32[3,16,3584]{2,1,0:T(8,128)} %bitcast.11), custom_call_target="tpu_custom_call" | custom-call | flops 1 | bytes 1 | tf_op jit(solution)/shard_map/pallas_call | solution.py:138
  2.8 3.7 %collective-permute-start.2 = (bf16[16,3584]{1,0:T(8,128)(2,1)S(1)}, bf16[16,3584]{1,0:T(8,128)(2,1)S(1)}, u32[]{:S(2)}, u32[]{:S(2)}) collective-permute-start(bf16[16,3584]{1,0:T(8,128)(2,1)S(1)} %get-tuple-element.44.refs_0_), channel_id=1, source_target_pairs={{4,2},{5,3},{6,0},{7,1},{0,6},{1,7},{2,4},{3,5},{12,10},{13,11},{1... | collective-permute-start | bytes 344072 | tf_op jit(solution)/shard_map/ppermute | solution.py:385
  6.5 0.0 collective-permute-start.1
  6.5 2.9 %collective-permute-start = (bf16[16,3584]{1,0:T(8,128)(2,1)S(1)}, bf16[16,3584]{1,0:T(8,128)(2,1)S(1)}, u32[]{:S(2)}, u32[]{:S(2)}) collective-permute-start(bf16[16,3584]{1,0:T(8,128)(2,1)S(1)} %get-tuple-element.44.refs_0_), channel_id=1, source_target_pairs={{0,4},{1,5},{4,6},{5,7},{6,2},{7,3},{2,0},{3,1},{8,12},{9,13},{12,... | collective-permute-start | bytes 344072 | tf_op jit(solution)/shard_map/ppermute | solution.py:385
  9.4 2.9 %collective-permute-start.5 = (bf16[48,3584]{1,0:T(8,128)(2,1)S(1)}, bf16[48,3584]{1,0:T(8,128)(2,1)S(1)}, u32[]{:S(2)}, u32[]{:S(2)}) collective-permute-start(bf16[48,3584]{1,0:T(8,128)(2,1)S(1)} %get-tuple-element.45.refs_0_), channel_id=1, source_target_pairs={{0,4},{1,5},{4,6},{5,7},{6,2},{7,3},{2,0},{3,1},{8,12},{9,13},{12,... | collective-permute-start | bytes 1032200 | tf_op jit(solution)/shard_map/ppermute | solution.py:385
  12.4 0.0 collective-permute-done.2.refs_3_
  12.4 4.8 %collective-permute-done.1.refs_2_ = bf16[16,3584]{1,0:T(8,128)(2,1)S(1)} collective-permute-done((bf16[16,3584]{1,0:T(8,128)(2,1)S(1)}, bf16[16,3584]{1,0:T(8,128)(2,1)S(1)}, u32[]{:S(2)}, u32[]{:S(2)}) %collective-permute-start.1) | collective-permute-done | bytes 114720 | tf_op jit(solution)/shard_map/ppermute | solution.py:385
  17.2 0.1 collective-permute-start.4
  17.3 0.6 collective-permute-start.3
  17.9 0.9 collective-permute-done.4
  18.8 0.3 collective-permute-done.3
  19.1 0.0 copy-start
  19.1 5.2 %shard_map.114.refs_0_ = bf16[3,128,512]{2,1,0:T(8,128)(2,1)S(1)} custom-call(bf16[16,3584]{1,0:T(8,128)(2,1)S(1)} %get-tuple-element.44.refs_0_, bf16[16,3584]{1,0:T(8,128)(2,1)S(1)} %collective-permute-done.refs_1_, bf16[16,3584]{1,0:T(8,128)(2,1)S(1)} %collective-permute-done.1.refs_2_, bf16[16,3584]{1,0:T(8,128)(2,1)S(1)} %collective-permute-done.2.refs_3_, ...), custom_call_target="tpu_custom_call" | custom-call | flops 1 | bytes 1 | tf_op jit(solution)/shard_map/pallas_call | solution.py:193
  24.3 1.6 %collective-permute-start.10 = (bf16[2,128,512]{2,1,0:T(8,128)(2,1)S(1)}, bf16[2,128,512]{2,1,0:T(8,128)(2,1)S(1)}, u32[]{:S(2)}, u32[]{:S(2)}) collective-permute-start(bf16[2,128,512]{2,1,0:T(8,128)(2,1)S(1)} %slice.8), channel_id=1, source_target_pairs={{0,16},{8,24},{1,17},{9,25},{2,18},{10,26},{3,19},{11,27},{4,20},{... | collective-permute-start | bytes 786440 | tf_op jit(solution)/shard_map/ppermute | solution.py:78
  25.9 3.4 %collective-permute-start.9 = (bf16[2,128,512]{2,1,0:T(8,128)(2,1)S(1)}, bf16[2,128,512]{2,1,0:T(8,128)(2,1)S(1)}, u32[]{:S(2)}, u32[]{:S(2)}) collective-permute-start(bf16[2,128,512]{2,1,0:T(8,128)(2,1)S(1)} %slice.8), channel_id=1, source_target_pairs={{0,8},{16,24},{1,9},{17,25},{2,10},{18,26},{3,11},{19,27},{4,12},{... | collective-permute-start | bytes 786440 | tf_op jit(solution)/shard_map/ppermute | solution.py:77
  29.3 1.6 %collective-permute-done.6.refs_2_ = bf16[48,3584]{1,0:T(8,128)(2,1)S(1)} collective-permute-done((bf16[48,3584]{1,0:T(8,128)(2,1)S(1)}, bf16[48,3584]{1,0:T(8,128)(2,1)S(1)}, u32[]{:S(2)}, u32[]{:S(2)}) %collective-permute-start.6) | collective-permute-done | bytes 344096 | tf_op jit(solution)/shard_map/ppermute | solution.py:385
  30.9 0.0 collective-permute-done.5.refs_1_
  30.9 0.1 pad_maximum_fusion
  31.0 0.1 collective-permute-start.7
  31.1 0.1 collective-permute-start.8
  31.2 3.8 %collective-permute-done.10.refs_4_ = bf16[2,128,512]{2,1,0:T(8,128)(2,1)S(1)} collective-permute-done((bf16[2,128,512]{2,1,0:T(8,128)(2,1)S(1)}, bf16[2,128,512]{2,1,0:T(8,128)(2,1)S(1)}, u32[]{:S(2)}, u32[]{:S(2)}) %collective-permute-start.10) | collective-permute-done | bytes 262176 | tf_op jit(solution)/shard_map/ppermute | solution.py:78
  35.0 0.3 collective-permute-done.9.refs_3_
  35.3 4.6 %collective-permute-start.11 = (bf16[2,128,512]{2,1,0:T(8,128)(2,1)S(1)}, bf16[2,128,512]{2,1,0:T(8,128)(2,1)S(1)}, u32[]{:S(2)}, u32[]{:S(2)}) collective-permute-start(bf16[2,128,512]{2,1,0:T(8,128)(2,1)S(1)} %collective-permute-done.10.refs_4_), channel_id=1, source_target_pairs={{24,16},{16,24},{25,17},{17,25},{26,18},{18,26},{27,19},{19,27},{2... | collective-permute-start | bytes 786440 | tf_op jit(solution)/shard_map/ppermute | solution.py:79
  39.9 0.0 collective-permute-done.7.refs_3_
  39.9 3.4 %shard_map.115.refs_1_ = bf16[3,288,512]{2,1,0:T(8,128)(2,1)S(1)} custom-call(bf16[48,3584]{1,0:T(8,128)(2,1)S(1)} %get-tuple-element.45.refs_0_, bf16[48,3584]{1,0:T(8,128)(2,1)S(1)} %collective-permute-done.5.refs_1_, bf16[48,3584]{1,0:T(8,128)(2,1)S(1)} %collective-permute-done.6.refs_2_, bf16[144,3584]{1,0:T(8,128)(2,1)S(1)} %collective-permute-done.7.refs_3_, ...), custom_call_target="tpu_custom_call" | custom-call | flops 1 | bytes 1 | tf_op jit(solution)/shard_map/pallas_call | solution.py:193
  43.3 0.0 copy-start.6
  43.3 0.0 copy-start.7
  43.3 2.3 %collective-permute-done.11.refs_5_ = bf16[2,128,512]{2,1,0:T(8,128)(2,1)S(1)} collective-permute-done((bf16[2,128,512]{2,1,0:T(8,128)(2,1)S(1)}, bf16[2,128,512]{2,1,0:T(8,128)(2,1)S(1)}, u32[]{:S(2)}, u32[]{:S(2)}) %collective-permute-start.11) | collective-permute-done | bytes 262176 | tf_op jit(solution)/shard_map/ppermute | solution.py:79
  45.6 0.0 collective-permute-start.12
  45.6 1.6 %collective-permute-done.12.refs_1_ = bf16[48,3584]{1,0:T(8,128)(2,1)S(1)} collective-permute-done((bf16[48,3584]{1,0:T(8,128)(2,1)S(1)}, bf16[48,3584]{1,0:T(8,128)(2,1)S(1)}, u32[]{:S(2)}, u32[]{:S(2)}) %collective-permute-start.12) | collective-permute-done | bytes 344096 | tf_op jit(solution)/shard_map/ppermute | solution.py:62
  47.2 1.9 %shard_map.116.refs_2_ = bf16[3,96,512]{2,1,0:T(8,128)(2,1)S(1)} custom-call(bf16[48,3584]{1,0:T(8,128)(2,1)S(1)} %collective-permute-done.8.refs_0_, bf16[48,3584]{1,0:T(8,128)(2,1)S(1)} %collective-permute-done.12.refs_1_, f32[2,512]{1,0:T(2,128)S(1)} %copy-done.5, bf16[3,3584,512]{2,1,0:T(8,128)(2,1)S(1)} %bitcast.10), custom_call_target="tpu_custom_call" | custom-call | flops 1 | bytes 1 | tf_op jit(solution)/shard_map/pallas_call | solution.py:193
  49.1 2.9 %shard_map.117 = (bf16[256,512]{1,0:T(8,128)(2,1)S(1)}, bf16[512,3584]{1,0:T(8,128)(2,1)S(1)}) custom-call(s32[1]{0:T(128)} %bitcast.3.clip, s32[4,4]{1,0:T(4,128)S(1)} %copy-done.6, s32[4]{0:T(128)S(1)} %copy-done.7, bf16[3,128,512]{2,1,0:T(8,128)(2,1)S(1)} %shard_map.114.refs_0_, bf16[3,288,512]{2,1,0:T(8,128)(2,1)S(1)} %shard_map.115.refs_1_, ...), custom_call_target="tpu_custom_call" | custom-call | flops 1 | bytes 1 | tf_op jit(solution)/shard_map/pallas_call | solution.py:257
  52.0 1.1 %shard_map.118 = (bf16[32,3584]{1,0:T(8,128)(2,1)S(1)}, bf16[32,3584]{1,0:T(8,128)(2,1)S(1)}, bf16[32,3584]{1,0:T(8,128)(2,1)S(1)}, bf16[32,3584]{1,0:T(8,128)(2...) custom-call(bf16[256,512]{1,0:T(8,128)(2,1)S(1)} %get-tuple-element.51.attended, ...), custom_call_target="tpu_custom_call" | custom-call | flops 1 | bytes 1 | tf_op jit(solution)/shard_map/pallas_call | solution.py:288
  53.2 0.2 collective-permute-start.13
  53.4 0.4 collective-permute-start.14
  53.8 2.0 %collective-permute-done.14.refs_1_.refs_4_ = bf16[32,3584]{1,0:T(8,128)(2,1)S(1)} collective-permute-done((bf16[32,3584]{1,0:T(8,128)(2,1)S(1)}, bf16[32,3584]{1,0:T(8,128)(2,1)S(1)}, u32[]{:S(2)}, u32[]{:S(2)}) %collective-permute-start.14) | collective-permute-done | bytes 229408 | tf_op jit(solution)/shard_map/ppermute | solution.py:62
  55.7 0.1 shard_map.119
  55.8 0.1 collective-permute-start.15
  55.8 2.9 %shard_map.122 = (bf16[256,512]{1,0:T(8,128)(2,1)S(1)}, bf16[512,3584]{1,0:T(8,128)(2,1)S(1)}) custom-call(s32[1]{0:T(128)} %bitcast.3.clip, s32[4,4]{1,0:T(4,128)S(1)} %copy-done.6, s32[4]{0:T(128)S(1)} %copy-done.7, bf16[3,128,512]{2,1,0:T(8,128)(2,1)S(1)} %shard_map.114.refs_0_, bf16[3,288,512]{2,1,0:T(8,128)(2,1)S(1)} %shard_map.115.refs_1_, ...), custom_call_target="tpu_custom_call" | custom-call | flops 1 | bytes 1 | tf_op jit(solution)/shard_map/pallas_call | solution.py:257
  58.8 1.1 %shard_map.123 = (bf16[32,3584]{1,0:T(8,128)(2,1)S(1)}, bf16[32,3584]{1,0:T(8,128)(2,1)S(1)}, bf16[32,3584]{1,0:T(8,128)(2,1)S(1)}, bf16[32,3584]{1,0:T(8,128)(2...) custom-call(bf16[256,512]{1,0:T(8,128)(2,1)S(1)} %get-tuple-element.65.attended, ...), custom_call_target="tpu_custom_call" | custom-call | flops 1 | bytes 1 | tf_op jit(solution)/shard_map/pallas_call | solution.py:288
  59.9 0.0 copy-start.1
  59.9 0.0 copy-start.2
  59.9 0.0 copy-start.3
  59.9 0.2 collective-permute-start.19
  60.1 3.4 %collective-permute-done.15.refs_5_ = bf16[32,3584]{1,0:T(8,128)(2,1)S(1)} collective-permute-done((bf16[32,3584]{1,0:T(8,128)(2,1)S(1)}, bf16[32,3584]{1,0:T(8,128)(2,1)S(1)}, u32[]{:S(2)}, u32[]{:S(2)}) %collective-permute-start.15) | collective-permute-done | bytes 229408 | tf_op jit(solution)/shard_map/ppermute | solution.py:428
  63.5 0.0 collective-permute-done.13.refs_3_.refs_1_
  63.5 0.2 shard_map.120
  63.7 0.1 collective-permute-start.20
  63.8 0.3 collective-permute-start.16
  64.1 2.6 %collective-permute-start.17 = (bf16[32,3584]{1,0:T(8,128)(2,1)S(1)}, bf16[32,3584]{1,0:T(8,128)(2,1)S(1)}, u32[]{:S(2)}, u32[]{:S(2)}) collective-permute-start(bf16[32,3584]{1,0:T(8,128)(2,1)S(1)} %get-tuple-element.61), channel_id=1, source_target_pairs={{2,0},{3,1},{6,2},{7,3},{4,6},{5,7},{0,4},{1,5},{10,8},{11,9},{14,... | collective-permute-start | bytes 688136 | tf_op jit(solution)/shard_map/ppermute | solution.py:447
  66.8 0.1 shard_map.124
  66.8 0.4 collective-permute-start.21
  67.2 6.0 %collective-permute-done.16.refs_2_ = bf16[32,3584]{1,0:T(8,128)(2,1)S(1)} collective-permute-done((bf16[32,3584]{1,0:T(8,128)(2,1)S(1)}, bf16[32,3584]{1,0:T(8,128)(2,1)S(1)}, u32[]{:S(2)}, u32[]{:S(2)}) %collective-permute-start.16) | collective-permute-done | bytes 229408 | tf_op jit(solution)/shard_map/ppermute | solution.py:447
  73.2 4.5 %collective-permute-done.17.refs_3_ = bf16[32,3584]{1,0:T(8,128)(2,1)S(1)} collective-permute-done((bf16[32,3584]{1,0:T(8,128)(2,1)S(1)}, bf16[32,3584]{1,0:T(8,128)(2,1)S(1)}, u32[]{:S(2)}, u32[]{:S(2)}) %collective-permute-start.17) | collective-permute-done | bytes 229408 | tf_op jit(solution)/shard_map/ppermute | solution.py:447
  77.7 0.0 copy-start.4
  77.7 0.4 shard_map.121
  78.0 4.5 %collective-permute-done.21.refs_5_ = bf16[32,3584]{1,0:T(8,128)(2,1)S(1)} collective-permute-done((bf16[32,3584]{1,0:T(8,128)(2,1)S(1)}, bf16[32,3584]{1,0:T(8,128)(2,1)S(1)}, u32[]{:S(2)}, u32[]{:S(2)}) %collective-permute-start.21) | collective-permute-done | bytes 229408 | tf_op jit(solution)/shard_map/ppermute | solution.py:428
  82.5 0.2 shard_map.125
  82.7 0.6 collective-permute-start.23
  83.4 1.4 %collective-permute-start.22 = (bf16[32,3584]{1,0:T(8,128)(2,1)S(1)}, bf16[32,3584]{1,0:T(8,128)(2,1)S(1)}, u32[]{:S(2)}, u32[]{:S(2)}) collective-permute-start(bf16[32,3584]{1,0:T(8,128)(2,1)S(1)} %get-tuple-element.75), channel_id=1, source_target_pairs={{4,0},{5,1},{6,4},{7,5},{2,6},{3,7},{0,2},{1,3},{12,8},{13,9},{14,... | collective-permute-start | bytes 688136 | tf_op jit(solution)/shard_map/ppermute | solution.py:447
  84.8 3.6 %collective-permute-start.18 = (bf16[16,96]{1,0:T(8,128)(2,1)S(1)}, bf16[16,96]{1,0:T(8,128)(2,1)S(1)}, u32[]{:S(2)}, u32[]{:S(2)}) collective-permute-start(bf16[16,96]{1,0:T(8,128)(2,1)S(1)} %slice.7), channel_id=1, source_target_pairs={{0,8},{8,16},{16,24},{1,9},{9,17},{17,25},{2,10},{10,18},{18,26},{... | collective-permute-start | bytes 9224 | tf_op jit(solution)/shard_map/ppermute | solution.py:68
  88.4 2.8 %collective-permute-done.18.earlier = bf16[16,96]{1,0:T(8,128)(2,1)S(1)} collective-permute-done((bf16[16,96]{1,0:T(8,128)(2,1)S(1)}, bf16[16,96]{1,0:T(8,128)(2,1)S(1)}, u32[]{:S(2)}, u32[]{:S(2)}) %collective-permute-start.18) | collective-permute-done | bytes 3104 | tf_op jit(solution)/shard_map/ppermute | solution.py:68
  91.2 4.1 %collective-permute-done.23.refs_3_ = bf16[32,3584]{1,0:T(8,128)(2,1)S(1)} collective-permute-done((bf16[32,3584]{1,0:T(8,128)(2,1)S(1)}, bf16[32,3584]{1,0:T(8,128)(2,1)S(1)}, u32[]{:S(2)}, u32[]{:S(2)}) %collective-permute-start.23) | collective-permute-done | bytes 229408 | tf_op jit(solution)/shard_map/ppermute | solution.py:447
  95.3 1.3 %shard_map.126 = (bf16[64,3584]{1,0:T(8,128)(2,1)}, bf16[64,384]{1,0:T(8,128)(2,1)}) custom-call(s32[1]{0:T(128)S(6)} %copy.12.level, bf16[64,3584]{1,0:T(8,128)(2,1)S(1)} %bitcast.16, f32[3,16,3584]{2,1,0:T(8,128)S(1)} %bitcast.13, bf16[96,3584]{1,0:T(8,128)(2,1)S(1)} %bitcast.18, bf16[3,96,384]{2,1,0:T(8,128)(2,1)S(1)} %copy-done.4, ...), custom_call_target="tpu_custom_call" | custom-call | flops 1 | bytes 1 | tf_op jit(solution)/shard_map/pallas_call | solution.py:352
  (22 shorter events, 0.2 us)
Async XLA Ops:
  0.6 18.5 %copy-start.5 = (f32[2,512]{1,0:T(2,128)S(1)}, f32[2,512]{1,0:T(2,128)}, u32[]{:S(2)}) copy-start(f32[2,512]{1,0:T(2,128)} %refs_2_.1) | copy-start | bytes 12292
  2.8 9.5 %collective-permute-start.2 = (bf16[16,3584]{1,0:T(8,128)(2,1)S(1)}, bf16[16,3584]{1,0:T(8,128)(2,1)S(1)}, u32[]{:S(2)}, u32[]{:S(2)}) collective-permute-start(bf16[16,3584]{1,0:T(8,128)(2,1)S(1)} %get-tuple-element.44.refs_0_), channel_id=1, source_target_pairs={{4,2},{5,3},{6,0},{7,1},{0,6},{1,7},{2,4},{3,5},{12,10},{13,11},{1... | collective-permute-start | bytes 344072 | tf_op jit(solution)/shard_map/ppermute | solution.py:385
  6.5 10.7 %collective-permute-start.1 = (bf16[16,3584]{1,0:T(8,128)(2,1)S(1)}, bf16[16,3584]{1,0:T(8,128)(2,1)S(1)}, u32[]{:S(2)}, u32[]{:S(2)}) collective-permute-start(bf16[16,3584]{1,0:T(8,128)(2,1)S(1)} %get-tuple-element.44.refs_0_), channel_id=1, source_target_pairs={{0,2},{1,3},{2,6},{3,7},{6,4},{7,5},{4,0},{5,1},{8,10},{9,11},{10,... | collective-permute-start | bytes 344072 | tf_op jit(solution)/shard_map/ppermute | solution.py:385
  6.5 10.8 %collective-permute-start = (bf16[16,3584]{1,0:T(8,128)(2,1)S(1)}, bf16[16,3584]{1,0:T(8,128)(2,1)S(1)}, u32[]{:S(2)}, u32[]{:S(2)}) collective-permute-start(bf16[16,3584]{1,0:T(8,128)(2,1)S(1)} %get-tuple-element.44.refs_0_), channel_id=1, source_target_pairs={{0,4},{1,5},{4,6},{5,7},{6,2},{7,3},{2,0},{3,1},{8,12},{9,13},{12,... | collective-permute-start | bytes 344072 | tf_op jit(solution)/shard_map/ppermute | solution.py:385
  9.4 21.5 %collective-permute-start.6 = (bf16[48,3584]{1,0:T(8,128)(2,1)S(1)}, bf16[48,3584]{1,0:T(8,128)(2,1)S(1)}, u32[]{:S(2)}, u32[]{:S(2)}) collective-permute-start(bf16[48,3584]{1,0:T(8,128)(2,1)S(1)} %get-tuple-element.45.refs_0_), channel_id=1, source_target_pairs={{0,2},{1,3},{2,6},{3,7},{6,4},{7,5},{4,0},{5,1},{8,10},{9,11},{10,... | collective-permute-start | bytes 1032200 | tf_op jit(solution)/shard_map/ppermute | solution.py:385
  9.4 21.5 %collective-permute-start.5 = (bf16[48,3584]{1,0:T(8,128)(2,1)S(1)}, bf16[48,3584]{1,0:T(8,128)(2,1)S(1)}, u32[]{:S(2)}, u32[]{:S(2)}) collective-permute-start(bf16[48,3584]{1,0:T(8,128)(2,1)S(1)} %get-tuple-element.45.refs_0_), channel_id=1, source_target_pairs={{0,4},{1,5},{4,6},{5,7},{6,2},{7,3},{2,0},{3,1},{8,12},{9,13},{12,... | collective-permute-start | bytes 1032200 | tf_op jit(solution)/shard_map/ppermute | solution.py:385
  17.2 1.6 %collective-permute-start.4 = (bf16[32,3584]{1,0:T(8,128)(2,1)S(1)}, bf16[32,3584]{1,0:T(8,128)(2,1)S(1)}, u32[]{:S(2)}, u32[]{:S(2)}) collective-permute-start(bf16[32,3584]{1,0:T(8,128)(2,1)S(1)} %pad_maximum_fusion.2), channel_id=1, source_target_pairs={{0,1},{1,0},{2,3},{3,2},{4,5},{5,4},{6,7},{7,6},{8,9},{9,8},{10,11... | collective-permute-start | bytes 688136 | tf_op jit(solution)/shard_map/ppermute | solution.py:62
  17.3 1.8 %collective-permute-start.3 = (bf16[32,3584]{1,0:T(8,128)(2,1)S(1)}, bf16[32,3584]{1,0:T(8,128)(2,1)S(1)}, u32[]{:S(2)}, u32[]{:S(2)}) collective-permute-start(bf16[32,3584]{1,0:T(8,128)(2,1)S(1)} %pad_maximum_fusion.1), channel_id=1, source_target_pairs={{0,1},{1,0},{2,3},{3,2},{4,5},{5,4},{6,7},{7,6},{8,9},{9,8},{10,11... | collective-permute-start | bytes 688136 | tf_op jit(solution)/shard_map/ppermute | solution.py:62
  19.1 20.8 %copy-start = (bf16[3584,3,512]{2,0,1:T(8,128)(2,1)S(1)}, bf16[3584,3,512]{2,0,1:T(8,128)(2,1)}, u32[]{:S(2)}) copy-start(bf16[3584,3,512]{2,0,1:T(8,128)(2,1)} %param.15) | copy-start | bytes 33030148
  24.3 10.7 %collective-permute-start.10 = (bf16[2,128,512]{2,1,0:T(8,128)(2,1)S(1)}, bf16[2,128,512]{2,1,0:T(8,128)(2,1)S(1)}, u32[]{:S(2)}, u32[]{:S(2)}) collective-permute-start(bf16[2,128,512]{2,1,0:T(8,128)(2,1)S(1)} %slice.8), channel_id=1, source_target_pairs={{0,16},{8,24},{1,17},{9,25},{2,18},{10,26},{3,19},{11,27},{4,20},{... | collective-permute-start | bytes 786440 | tf_op jit(solution)/shard_map/ppermute | solution.py:78
  25.9 9.4 %collective-permute-start.9 = (bf16[2,128,512]{2,1,0:T(8,128)(2,1)S(1)}, bf16[2,128,512]{2,1,0:T(8,128)(2,1)S(1)}, u32[]{:S(2)}, u32[]{:S(2)}) collective-permute-start(bf16[2,128,512]{2,1,0:T(8,128)(2,1)S(1)} %slice.8), channel_id=1, source_target_pairs={{0,8},{16,24},{1,9},{17,25},{2,10},{18,26},{3,11},{19,27},{4,12},{... | collective-permute-start | bytes 786440 | tf_op jit(solution)/shard_map/ppermute | solution.py:77
  31.0 8.9 %collective-permute-start.7 = (bf16[144,3584]{1,0:T(8,128)(2,1)S(1)}, bf16[144,3584]{1,0:T(8,128)(2,1)S(1)}, u32[]{:S(2)}, u32[]{:S(2)}) collective-permute-start(bf16[144,3584]{1,0:T(8,128)(2,1)S(1)} %pad_maximum_fusion), channel_id=1, source_target_pairs={{0,1},{1,0},{2,3},{3,2},{4,5},{5,4},{6,7},{7,6},{8,9},{9,8},{10,11... | collective-permute-start | bytes 3096584 | tf_op jit(solution)/shard_map/ppermute | solution.py:62
  31.1 12.2 %collective-permute-start.8 = (bf16[48,3584]{1,0:T(8,128)(2,1)S(1)}, bf16[48,3584]{1,0:T(8,128)(2,1)S(1)}, u32[]{:S(2)}, u32[]{:S(2)}) collective-permute-start(bf16[48,3584]{1,0:T(8,128)(2,1)S(1)} %broadcast_select_fusion), channel_id=1, source_target_pairs={{0,2},{1,3},{2,0},{3,1},{4,6},{5,7},{6,4},{7,5},{8,10},{9,11},{10,... | collective-permute-start | bytes 1032200 | tf_op jit(solution)/shard_map/ppermute | solution.py:385
  35.3 10.3 %collective-permute-start.11 = (bf16[2,128,512]{2,1,0:T(8,128)(2,1)S(1)}, bf16[2,128,512]{2,1,0:T(8,128)(2,1)S(1)}, u32[]{:S(2)}, u32[]{:S(2)}) collective-permute-start(bf16[2,128,512]{2,1,0:T(8,128)(2,1)S(1)} %collective-permute-done.10.refs_4_), channel_id=1, source_target_pairs={{24,16},{16,24},{25,17},{17,25},{26,18},{18,26},{27,19},{19,27},{2... | collective-permute-start | bytes 786440 | tf_op jit(solution)/shard_map/ppermute | solution.py:79
  43.3 5.8 %copy-start.6 = (s32[4,4]{1,0:T(4,128)S(1)}, s32[4,4]{1,0:T(4,128)}, u32[]{:S(2)}) copy-start(s32[4,4]{1,0:T(4,128)} %visible.3) | copy-start | bytes 196
  43.3 5.8 %copy-start.7 = (s32[4]{0:T(128)S(1)}, s32[4]{0:T(128)}, u32[]{:S(2)}) copy-start(s32[4]{0:T(128)} %counts.3) | copy-start | bytes 52
  45.6 1.7 %collective-permute-start.12 = (bf16[48,3584]{1,0:T(8,128)(2,1)S(1)}, bf16[48,3584]{1,0:T(8,128)(2,1)S(1)}, u32[]{:S(2)}, u32[]{:S(2)}) collective-permute-start(bf16[48,3584]{1,0:T(8,128)(2,1)S(1)} %collective-permute-done.8.refs_0_), channel_id=1, source_target_pairs={{0,1},{1,0},{2,3},{3,2},{4,5},{5,4},{6,7},{7,6},{8,9},{9,8},{10,11... | collective-permute-start | bytes 1032200 | tf_op jit(solution)/shard_map/ppermute | solution.py:62
  53.2 10.3 %collective-permute-start.13 = (bf16[96,3584]{1,0:T(8,128)(2,1)S(1)}, bf16[96,3584]{1,0:T(8,128)(2,1)S(1)}, u32[]{:S(2)}, u32[]{:S(2)}) collective-permute-start(bf16[96,3584]{1,0:T(8,128)(2,1)S(1)} %get-tuple-element.54), channel_id=1, source_target_pairs={{0,1},{1,0},{2,3},{3,2},{4,5},{5,4},{6,7},{7,6},{8,9},{9,8},{10,11... | collective-permute-start | bytes 2064392 | tf_op jit(solution)/shard_map/ppermute | solution.py:62
  53.4 2.3 %collective-permute-start.14 = (bf16[32,3584]{1,0:T(8,128)(2,1)S(1)}, bf16[32,3584]{1,0:T(8,128)(2,1)S(1)}, u32[]{:S(2)}, u32[]{:S(2)}) collective-permute-start(bf16[32,3584]{1,0:T(8,128)(2,1)S(1)} %get-tuple-element.59), channel_id=1, source_target_pairs={{0,1},{1,0},{2,3},{3,2},{4,5},{5,4},{6,7},{7,6},{8,9},{9,8},{10,11... | collective-permute-start | bytes 688136 | tf_op jit(solution)/shard_map/ppermute | solution.py:62
  55.8 7.7 %collective-permute-start.15 = (bf16[32,3584]{1,0:T(8,128)(2,1)S(1)}, bf16[32,3584]{1,0:T(8,128)(2,1)S(1)}, u32[]{:S(2)}, u32[]{:S(2)}) collective-permute-start(bf16[32,3584]{1,0:T(8,128)(2,1)S(1)} %shard_map.119), channel_id=1, source_target_pairs={{2,0},{3,1},{0,2},{1,3},{6,4},{7,5},{4,6},{5,7},{10,8},{11,9},{8,1... | collective-permute-start | bytes 688136 | tf_op jit(solution)/shard_map/ppermute | solution.py:428
  59.9 17.8 %copy-start.1 = (f32[16,3,3584]{2,0,1:T(8,128)S(1)}, f32[16,3,3584]{2,0,1:T(8,128)}, u32[]{:S(2)}) copy-start(f32[16,3,3584]{2,0,1:T(8,128)} %param.14) | copy-start | bytes 2064388
  59.9 17.7 %copy-start.2 = (bf16[1,64,3584]{2,1,0:T(8,128)(2,1)S(1)}, bf16[1,64,3584]{2,1,0:T(8,128)(2,1)}, u32[]{:S(2)}) copy-start(bf16[1,64,3584]{2,1,0:T(8,128)(2,1)} %param.10) | copy-start | bytes 1376260
  59.9 17.7 %copy-start.3 = (bf16[3584,96]{0,1:T(8,128)(2,1)S(1)}, bf16[3584,96]{0,1:T(8,128)(2,1)}, u32[]{:S(2)}) copy-start(bf16[3584,96]{0,1:T(8,128)(2,1)} %param.18) | copy-start | bytes 2064388
  59.9 18.1 %collective-permute-start.19 = (bf16[96,3584]{1,0:T(8,128)(2,1)S(1)}, bf16[96,3584]{1,0:T(8,128)(2,1)S(1)}, u32[]{:S(2)}, u32[]{:S(2)}) collective-permute-start(bf16[96,3584]{1,0:T(8,128)(2,1)S(1)} %get-tuple-element.68), channel_id=1, source_target_pairs={{0,1},{1,0},{2,3},{3,2},{4,5},{5,4},{6,7},{7,6},{8,9},{9,8},{10,11... | collective-permute-start | bytes 2064392 | tf_op jit(solution)/shard_map/ppermute | solution.py:62
  63.7 3.1 %collective-permute-start.20 = (bf16[32,3584]{1,0:T(8,128)(2,1)S(1)}, bf16[32,3584]{1,0:T(8,128)(2,1)S(1)}, u32[]{:S(2)}, u32[]{:S(2)}) collective-permute-start(bf16[32,3584]{1,0:T(8,128)(2,1)S(1)} %get-tuple-element.73), channel_id=1, source_target_pairs={{0,1},{1,0},{2,3},{3,2},{4,5},{5,4},{6,7},{7,6},{8,9},{9,8},{10,11... | collective-permute-start | bytes 688136 | tf_op jit(solution)/shard_map/ppermute | solution.py:62
  63.8 9.4 %collective-permute-start.16 = (bf16[32,3584]{1,0:T(8,128)(2,1)S(1)}, bf16[32,3584]{1,0:T(8,128)(2,1)S(1)}, u32[]{:S(2)}, u32[]{:S(2)}) collective-permute-start(bf16[32,3584]{1,0:T(8,128)(2,1)S(1)} %get-tuple-element.60), channel_id=1, source_target_pairs={{4,0},{5,1},{6,4},{7,5},{2,6},{3,7},{0,2},{1,3},{12,8},{13,9},{14,... | collective-permute-start | bytes 688136 | tf_op jit(solution)/shard_map/ppermute | solution.py:447
  64.1 13.5 %collective-permute-start.17 = (bf16[32,3584]{1,0:T(8,128)(2,1)S(1)}, bf16[32,3584]{1,0:T(8,128)(2,1)S(1)}, u32[]{:S(2)}, u32[]{:S(2)}) collective-permute-start(bf16[32,3584]{1,0:T(8,128)(2,1)S(1)} %get-tuple-element.61), channel_id=1, source_target_pairs={{2,0},{3,1},{6,2},{7,3},{4,6},{5,7},{0,4},{1,5},{10,8},{11,9},{14,... | collective-permute-start | bytes 688136 | tf_op jit(solution)/shard_map/ppermute | solution.py:447
  66.8 15.7 %collective-permute-start.21 = (bf16[32,3584]{1,0:T(8,128)(2,1)S(1)}, bf16[32,3584]{1,0:T(8,128)(2,1)S(1)}, u32[]{:S(2)}, u32[]{:S(2)}) collective-permute-start(bf16[32,3584]{1,0:T(8,128)(2,1)S(1)} %shard_map.124), channel_id=1, source_target_pairs={{2,0},{3,1},{0,2},{1,3},{6,4},{7,5},{4,6},{5,7},{10,8},{11,9},{8,1... | collective-permute-start | bytes 688136 | tf_op jit(solution)/shard_map/ppermute | solution.py:428
  77.7 17.6 %copy-start.4 = (bf16[3,96,384]{2,1,0:T(8,128)(2,1)S(1)}, bf16[3,96,384]{2,1,0:T(8,128)(2,1)}, u32[]{:S(2)}) copy-start(bf16[3,96,384]{2,1,0:T(8,128)(2,1)} %weight.1) | copy-start | bytes 663556
  82.7 12.5 %collective-permute-start.23 = (bf16[32,3584]{1,0:T(8,128)(2,1)S(1)}, bf16[32,3584]{1,0:T(8,128)(2,1)S(1)}, u32[]{:S(2)}, u32[]{:S(2)}) collective-permute-start(bf16[32,3584]{1,0:T(8,128)(2,1)S(1)} %get-tuple-element.77), channel_id=1, source_target_pairs={{2,0},{3,1},{6,2},{7,3},{4,6},{5,7},{0,4},{1,5},{10,8},{11,9},{14,... | collective-permute-start | bytes 688136 | tf_op jit(solution)/shard_map/ppermute | solution.py:447
  83.4 11.9 %collective-permute-start.22 = (bf16[32,3584]{1,0:T(8,128)(2,1)S(1)}, bf16[32,3584]{1,0:T(8,128)(2,1)S(1)}, u32[]{:S(2)}, u32[]{:S(2)}) collective-permute-start(bf16[32,3584]{1,0:T(8,128)(2,1)S(1)} %get-tuple-element.75), channel_id=1, source_target_pairs={{4,0},{5,1},{6,4},{7,5},{2,6},{3,7},{0,2},{1,3},{12,8},{13,9},{14,... | collective-permute-start | bytes 688136 | tf_op jit(solution)/shard_map/ppermute | solution.py:447
  84.8 6.4 %collective-permute-start.18 = (bf16[16,96]{1,0:T(8,128)(2,1)S(1)}, bf16[16,96]{1,0:T(8,128)(2,1)S(1)}, u32[]{:S(2)}, u32[]{:S(2)}) collective-permute-start(bf16[16,96]{1,0:T(8,128)(2,1)S(1)} %slice.7), channel_id=1, source_target_pairs={{0,8},{8,16},{16,24},{1,9},{9,17},{17,25},{2,10},{10,18},{18,26},{... | collective-permute-start | bytes 9224 | tf_op jit(solution)/shard_map/ppermute | solution.py:68

commit v6 on v5

--- a/solution.py
+++ b/solution.py
@@ -475,7 +475,7 @@
     packed, origins = from_earlier(lead_part[1:])
 
     last = take(table[-1], body, [after(tile, lead_part) for tile in held], mask[-1])
-    first = [body] + [after(tile, lead_part) for tile in held]
+    first = [body] + held
     across = over_core(jnp.concatenate(first, 0))
     early_part = project([body] + held + [across], qk_gain, weight, False)
     last = after(last, early_part, *packed)

time: 97.1 us -> 97.1 us (level)
  no operation moved by 1% of the time
where the time goes in v6:
time: 97.1 us; the launch traced here: 96.5 us
  waiting for transfers between devices  42.7 us (44%)
  starting transfers between devices  29.8 us (31%)
  Pallas kernels  22.2 us (23%)
  between operations  1.62 us (2%)
    ppermute x4, waiting for transfers between devices, sent_home(): lax.ppermute(term, 'tok', lanes(back(pairs)))  14.5 us
    pallas_call x3, Pallas kernels, project(): pl.pallas_call(functools.partial(project_kernel, len(tiles), load), in_sp...  10.4 us
    ppermute x6, starting transfers between devices, take(): return lax.ppermute(tile, 'tok', lanes(pairs))  9.59 us
    ppermute x2, waiting for transfers between devices, passed_back(): came = lax.ppermute(sums, 'tok', lanes(back(pairs)))  7.83 us
    ppermute x6, waiting for transfers between devices, take(): return lax.ppermute(tile, 'tok', lanes(pairs))  6.43 us
    pallas_call x2, Pallas kernels, attend(): pl.pallas_call(functools.partial(attend_kernel, cuts, len(parts), origins...  5.8 us
    ppermute x4, starting transfers between devices, sent_home(): lax.ppermute(term, 'tok', lanes(back(pairs)))  5.06 us
    ppermute x8, waiting for transfers between devices, over_core(): return lax.ppermute(array, 'tok', [(i, i ^ 1) for i in range(devices)])  4.82 us
  transfers between devices with their start and end apart: 24, of which 15 were waited for; matrix products, arithmetic and copies ran while one was open for 0% of the time, Pallas kernels for 14%

profile of v6, /device:TPU:4, one launch (start us, length us, event | category | flops | bytes accessed | tf_op | source)
XLA Modules:
  0.0 96.5 jit_solution(16775669779804380704)
XLA Ops:
  1.3 1.5 %shard_map.113 = (bf16[16,3584]{1,0:T(8,128)(2,1)S(1)}, bf16[48,3584]{1,0:T(8,128)(2,1)S(1)}) custom-call(s32[1]{0:T(128)S(6)} %copy.12.level, bf16[64,3584]{1,0:T(8,128)(2,1)} %bitcast.14, f32[3,16,3584]{2,1,0:T(8,128)} %bitcast.11), custom_call_target="tpu_custom_call" | custom-call | flops 1 | bytes 1 | tf_op jit(solution)/shard_map/pallas_call | solution.py:138
  2.8 3.7 %collective-permute-start.2 = (bf16[16,3584]{1,0:T(8,128)(2,1)S(1)}, bf16[16,3584]{1,0:T(8,128)(2,1)S(1)}, u32[]{:S(2)}, u32[]{:S(2)}) collective-permute-start(bf16[16,3584]{1,0:T(8,128)(2,1)S(1)} %get-tuple-element.44.refs_0_), channel_id=1, source_target_pairs={{4,2},{5,3},{6,0},{7,1},{0,6},{1,7},{2,4},{3,5},{12,10},{13,11},{1... | collective-permute-start | bytes 344072 | tf_op jit(solution)/shard_map/ppermute | solution.py:385
  6.5 0.0 collective-permute-start.1
  6.5 2.9 %collective-permute-start = (bf16[16,3584]{1,0:T(8,128)(2,1)S(1)}, bf16[16,3584]{1,0:T(8,128)(2,1)S(1)}, u32[]{:S(2)}, u32[]{:S(2)}) collective-permute-start(bf16[16,3584]{1,0:T(8,128)(2,1)S(1)} %get-tuple-element.44.refs_0_), channel_id=1, source_target_pairs={{0,4},{1,5},{4,6},{5,7},{6,2},{7,3},{2,0},{3,1},{8,12},{9,13},{12,... | collective-permute-start | bytes 344072 | tf_op jit(solution)/shard_map/ppermute | solution.py:385
  9.4 2.9 %collective-permute-start.5 = (bf16[48,3584]{1,0:T(8,128)(2,1)S(1)}, bf16[48,3584]{1,0:T(8,128)(2,1)S(1)}, u32[]{:S(2)}, u32[]{:S(2)}) collective-permute-start(bf16[48,3584]{1,0:T(8,128)(2,1)S(1)} %get-tuple-element.45.refs_0_), channel_id=1, source_target_pairs={{0,4},{1,5},{4,6},{5,7},{6,2},{7,3},{2,0},{3,1},{8,12},{9,13},{12,... | collective-permute-start | bytes 1032200 | tf_op jit(solution)/shard_map/ppermute | solution.py:385
  12.4 0.0 collective-permute-done.2.refs_3_
  12.4 4.8 %collective-permute-done.1.refs_2_ = bf16[16,3584]{1,0:T(8,128)(2,1)S(1)} collective-permute-done((bf16[16,3584]{1,0:T(8,128)(2,1)S(1)}, bf16[16,3584]{1,0:T(8,128)(2,1)S(1)}, u32[]{:S(2)}, u32[]{:S(2)}) %collective-permute-start.1) | collective-permute-done | bytes 114720 | tf_op jit(solution)/shard_map/ppermute | solution.py:385
  17.2 0.1 collective-permute-start.4
  17.3 0.0 collective-permute-done.refs_1_
  17.3 0.6 collective-permute-start.3
  17.9 0.9 collective-permute-done.4
  18.8 0.3 collective-permute-done.3
  19.1 0.0 copy-start
  19.1 5.2 %shard_map.114.refs_0_ = bf16[3,128,512]{2,1,0:T(8,128)(2,1)S(1)} custom-call(bf16[16,3584]{1,0:T(8,128)(2,1)S(1)} %get-tuple-element.44.refs_0_, bf16[16,3584]{1,0:T(8,128)(2,1)S(1)} %collective-permute-done.refs_1_, bf16[16,3584]{1,0:T(8,128)(2,1)S(1)} %collective-permute-done.1.refs_2_, bf16[16,3584]{1,0:T(8,128)(2,1)S(1)} %collective-permute-done.2.refs_3_, ...), custom_call_target="tpu_custom_call" | custom-call | flops 1 | bytes 1 | tf_op jit(solution)/shard_map/pallas_call | solution.py:193
  24.3 1.6 %collective-permute-start.10 = (bf16[2,128,512]{2,1,0:T(8,128)(2,1)S(1)}, bf16[2,128,512]{2,1,0:T(8,128)(2,1)S(1)}, u32[]{:S(2)}, u32[]{:S(2)}) collective-permute-start(bf16[2,128,512]{2,1,0:T(8,128)(2,1)S(1)} %slice.8), channel_id=1, source_target_pairs={{0,16},{8,24},{1,17},{9,25},{2,18},{10,26},{3,19},{11,27},{4,20},{... | collective-permute-start | bytes 786440 | tf_op jit(solution)/shard_map/ppermute | solution.py:78
  25.9 3.4 %collective-permute-start.9 = (bf16[2,128,512]{2,1,0:T(8,128)(2,1)S(1)}, bf16[2,128,512]{2,1,0:T(8,128)(2,1)S(1)}, u32[]{:S(2)}, u32[]{:S(2)}) collective-permute-start(bf16[2,128,512]{2,1,0:T(8,128)(2,1)S(1)} %slice.8), channel_id=1, source_target_pairs={{0,8},{16,24},{1,9},{17,25},{2,10},{18,26},{3,11},{19,27},{4,12},{... | collective-permute-start | bytes 786440 | tf_op jit(solution)/shard_map/ppermute | solution.py:77
  29.3 1.6 %collective-permute-done.6.refs_2_ = bf16[48,3584]{1,0:T(8,128)(2,1)S(1)} collective-permute-done((bf16[48,3584]{1,0:T(8,128)(2,1)S(1)}, bf16[48,3584]{1,0:T(8,128)(2,1)S(1)}, u32[]{:S(2)}, u32[]{:S(2)}) %collective-permute-start.6) | collective-permute-done | bytes 344096 | tf_op jit(solution)/shard_map/ppermute | solution.py:385
  30.9 0.0 collective-permute-done.5.refs_1_
  30.9 0.1 pad_maximum_fusion
  31.0 0.1 collective-permute-start.7
  31.1 0.1 collective-permute-start.8
  31.2 3.8 %collective-permute-done.10.refs_4_ = bf16[2,128,512]{2,1,0:T(8,128)(2,1)S(1)} collective-permute-done((bf16[2,128,512]{2,1,0:T(8,128)(2,1)S(1)}, bf16[2,128,512]{2,1,0:T(8,128)(2,1)S(1)}, u32[]{:S(2)}, u32[]{:S(2)}) %collective-permute-start.10) | collective-permute-done | bytes 262176 | tf_op jit(solution)/shard_map/ppermute | solution.py:78
  35.0 0.3 collective-permute-done.9.refs_3_
  35.3 4.6 %collective-permute-start.11 = (bf16[2,128,512]{2,1,0:T(8,128)(2,1)S(1)}, bf16[2,128,512]{2,1,0:T(8,128)(2,1)S(1)}, u32[]{:S(2)}, u32[]{:S(2)}) collective-permute-start(bf16[2,128,512]{2,1,0:T(8,128)(2,1)S(1)} %collective-permute-done.10.refs_4_), channel_id=1, source_target_pairs={{24,16},{16,24},{25,17},{17,25},{26,18},{18,26},{27,19},{19,27},{2... | collective-permute-start | bytes 786440 | tf_op jit(solution)/shard_map/ppermute | solution.py:79
  39.9 0.0 collective-permute-done.7.refs_3_
  39.9 3.4 %shard_map.115.refs_1_ = bf16[3,288,512]{2,1,0:T(8,128)(2,1)S(1)} custom-call(bf16[48,3584]{1,0:T(8,128)(2,1)S(1)} %get-tuple-element.45.refs_0_, bf16[48,3584]{1,0:T(8,128)(2,1)S(1)} %collective-permute-done.5.refs_1_, bf16[48,3584]{1,0:T(8,128)(2,1)S(1)} %collective-permute-done.6.refs_2_, bf16[144,3584]{1,0:T(8,128)(2,1)S(1)} %collective-permute-done.7.refs_3_, ...), custom_call_target="tpu_custom_call" | custom-call | flops 1 | bytes 1 | tf_op jit(solution)/shard_map/pallas_call | solution.py:193
  43.3 0.0 copy-start.6
  43.3 0.0 copy-start.7
  43.3 2.3 %collective-permute-done.11.refs_5_ = bf16[2,128,512]{2,1,0:T(8,128)(2,1)S(1)} collective-permute-done((bf16[2,128,512]{2,1,0:T(8,128)(2,1)S(1)}, bf16[2,128,512]{2,1,0:T(8,128)(2,1)S(1)}, u32[]{:S(2)}, u32[]{:S(2)}) %collective-permute-start.11) | collective-permute-done | bytes 262176 | tf_op jit(solution)/shard_map/ppermute | solution.py:79
  45.6 0.0 collective-permute-start.12
  45.6 1.6 %collective-permute-done.12.refs_1_ = bf16[48,3584]{1,0:T(8,128)(2,1)S(1)} collective-permute-done((bf16[48,3584]{1,0:T(8,128)(2,1)S(1)}, bf16[48,3584]{1,0:T(8,128)(2,1)S(1)}, u32[]{:S(2)}, u32[]{:S(2)}) %collective-permute-start.12) | collective-permute-done | bytes 344096 | tf_op jit(solution)/shard_map/ppermute | solution.py:62
  47.2 1.9 %shard_map.116.refs_2_ = bf16[3,96,512]{2,1,0:T(8,128)(2,1)S(1)} custom-call(bf16[48,3584]{1,0:T(8,128)(2,1)S(1)} %collective-permute-done.8.refs_0_, bf16[48,3584]{1,0:T(8,128)(2,1)S(1)} %collective-permute-done.12.refs_1_, f32[2,512]{1,0:T(2,128)S(1)} %copy-done.5, bf16[3,3584,512]{2,1,0:T(8,128)(2,1)S(1)} %bitcast.10), custom_call_target="tpu_custom_call" | custom-call | flops 1 | bytes 1 | tf_op jit(solution)/shard_map/pallas_call | solution.py:193
  49.1 2.9 %shard_map.117 = (bf16[256,512]{1,0:T(8,128)(2,1)S(1)}, bf16[512,3584]{1,0:T(8,128)(2,1)S(1)}) custom-call(s32[1]{0:T(128)} %bitcast.3.clip, s32[4,4]{1,0:T(4,128)S(1)} %copy-done.6, s32[4]{0:T(128)S(1)} %copy-done.7, bf16[3,128,512]{2,1,0:T(8,128)(2,1)S(1)} %shard_map.114.refs_0_, bf16[3,288,512]{2,1,0:T(8,128)(2,1)S(1)} %shard_map.115.refs_1_, ...), custom_call_target="tpu_custom_call" | custom-call | flops 1 | bytes 1 | tf_op jit(solution)/shard_map/pallas_call | solution.py:257
  52.0 1.1 %shard_map.118 = (bf16[32,3584]{1,0:T(8,128)(2,1)S(1)}, bf16[32,3584]{1,0:T(8,128)(2,1)S(1)}, bf16[32,3584]{1,0:T(8,128)(2,1)S(1)}, bf16[32,3584]{1,0:T(8,128)(2...) custom-call(bf16[256,512]{1,0:T(8,128)(2,1)S(1)} %get-tuple-element.51.attended, ...), custom_call_target="tpu_custom_call" | custom-call | flops 1 | bytes 1 | tf_op jit(solution)/shard_map/pallas_call | solution.py:288
  53.2 0.2 collective-permute-start.13
  53.4 0.4 collective-permute-start.14
  53.8 2.0 %collective-permute-done.14.refs_1_.refs_4_ = bf16[32,3584]{1,0:T(8,128)(2,1)S(1)} collective-permute-done((bf16[32,3584]{1,0:T(8,128)(2,1)S(1)}, bf16[32,3584]{1,0:T(8,128)(2,1)S(1)}, u32[]{:S(2)}, u32[]{:S(2)}) %collective-permute-start.14) | collective-permute-done | bytes 229408 | tf_op jit(solution)/shard_map/ppermute | solution.py:62
  55.7 0.1 shard_map.119
  55.8 0.1 collective-permute-start.15
  55.8 2.9 %shard_map.122 = (bf16[256,512]{1,0:T(8,128)(2,1)S(1)}, bf16[512,3584]{1,0:T(8,128)(2,1)S(1)}) custom-call(s32[1]{0:T(128)} %bitcast.3.clip, s32[4,4]{1,0:T(4,128)S(1)} %copy-done.6, s32[4]{0:T(128)S(1)} %copy-done.7, bf16[3,128,512]{2,1,0:T(8,128)(2,1)S(1)} %shard_map.114.refs_0_, bf16[3,288,512]{2,1,0:T(8,128)(2,1)S(1)} %shard_map.115.refs_1_, ...), custom_call_target="tpu_custom_call" | custom-call | flops 1 | bytes 1 | tf_op jit(solution)/shard_map/pallas_call | solution.py:257
  58.8 1.1 %shard_map.123 = (bf16[32,3584]{1,0:T(8,128)(2,1)S(1)}, bf16[32,3584]{1,0:T(8,128)(2,1)S(1)}, bf16[32,3584]{1,0:T(8,128)(2,1)S(1)}, bf16[32,3584]{1,0:T(8,128)(2...) custom-call(bf16[256,512]{1,0:T(8,128)(2,1)S(1)} %get-tuple-element.65.attended, ...), custom_call_target="tpu_custom_call" | custom-call | flops 1 | bytes 1 | tf_op jit(solution)/shard_map/pallas_call | solution.py:288
  59.9 0.0 copy-start.1
  59.9 0.0 copy-start.2
  59.9 0.0 copy-start.3
  59.9 0.2 collective-permute-start.19
  60.1 3.4 %collective-permute-done.15.refs_5_ = bf16[32,3584]{1,0:T(8,128)(2,1)S(1)} collective-permute-done((bf16[32,3584]{1,0:T(8,128)(2,1)S(1)}, bf16[32,3584]{1,0:T(8,128)(2,1)S(1)}, u32[]{:S(2)}, u32[]{:S(2)}) %collective-permute-start.15) | collective-permute-done | bytes 229408 | tf_op jit(solution)/shard_map/ppermute | solution.py:428
  63.5 0.2 shard_map.120
  63.7 0.1 collective-permute-start.20
  63.8 0.3 collective-permute-start.16
  64.1 2.6 %collective-permute-start.17 = (bf16[32,3584]{1,0:T(8,128)(2,1)S(1)}, bf16[32,3584]{1,0:T(8,128)(2,1)S(1)}, u32[]{:S(2)}, u32[]{:S(2)}) collective-permute-start(bf16[32,3584]{1,0:T(8,128)(2,1)S(1)} %get-tuple-element.61), channel_id=1, source_target_pairs={{2,0},{3,1},{6,2},{7,3},{4,6},{5,7},{0,4},{1,5},{10,8},{11,9},{14,... | collective-permute-start | bytes 688136 | tf_op jit(solution)/shard_map/ppermute | solution.py:447
  66.8 0.1 shard_map.124
  66.8 0.4 collective-permute-start.21
  67.2 6.0 %collective-permute-done.16.refs_2_ = bf16[32,3584]{1,0:T(8,128)(2,1)S(1)} collective-permute-done((bf16[32,3584]{1,0:T(8,128)(2,1)S(1)}, bf16[32,3584]{1,0:T(8,128)(2,1)S(1)}, u32[]{:S(2)}, u32[]{:S(2)}) %collective-permute-start.16) | collective-permute-done | bytes 229408 | tf_op jit(solution)/shard_map/ppermute | solution.py:447
  73.2 4.5 %collective-permute-done.17.refs_3_ = bf16[32,3584]{1,0:T(8,128)(2,1)S(1)} collective-permute-done((bf16[32,3584]{1,0:T(8,128)(2,1)S(1)}, bf16[32,3584]{1,0:T(8,128)(2,1)S(1)}, u32[]{:S(2)}, u32[]{:S(2)}) %collective-permute-start.17) | collective-permute-done | bytes 229408 | tf_op jit(solution)/shard_map/ppermute | solution.py:447
  77.7 0.0 copy-start.4
  77.7 0.4 shard_map.121
  78.0 4.5 %collective-permute-done.21.refs_5_ = bf16[32,3584]{1,0:T(8,128)(2,1)S(1)} collective-permute-done((bf16[32,3584]{1,0:T(8,128)(2,1)S(1)}, bf16[32,3584]{1,0:T(8,128)(2,1)S(1)}, u32[]{:S(2)}, u32[]{:S(2)}) %collective-permute-start.21) | collective-permute-done | bytes 229408 | tf_op jit(solution)/shard_map/ppermute | solution.py:428
  82.5 0.2 shard_map.125
  82.7 0.6 collective-permute-start.23
  83.4 1.4 %collective-permute-start.22 = (bf16[32,3584]{1,0:T(8,128)(2,1)S(1)}, bf16[32,3584]{1,0:T(8,128)(2,1)S(1)}, u32[]{:S(2)}, u32[]{:S(2)}) collective-permute-start(bf16[32,3584]{1,0:T(8,128)(2,1)S(1)} %get-tuple-element.75), channel_id=1, source_target_pairs={{4,0},{5,1},{6,4},{7,5},{2,6},{3,7},{0,2},{1,3},{12,8},{13,9},{14,... | collective-permute-start | bytes 688136 | tf_op jit(solution)/shard_map/ppermute | solution.py:447
  84.8 3.6 %collective-permute-start.18 = (bf16[16,96]{1,0:T(8,128)(2,1)S(1)}, bf16[16,96]{1,0:T(8,128)(2,1)S(1)}, u32[]{:S(2)}, u32[]{:S(2)}) collective-permute-start(bf16[16,96]{1,0:T(8,128)(2,1)S(1)} %slice.7), channel_id=1, source_target_pairs={{0,8},{8,16},{16,24},{1,9},{9,17},{17,25},{2,10},{10,18},{18,26},{... | collective-permute-start | bytes 9224 | tf_op jit(solution)/shard_map/ppermute | solution.py:68
  88.4 2.8 %collective-permute-done.18.earlier = bf16[16,96]{1,0:T(8,128)(2,1)S(1)} collective-permute-done((bf16[16,96]{1,0:T(8,128)(2,1)S(1)}, bf16[16,96]{1,0:T(8,128)(2,1)S(1)}, u32[]{:S(2)}, u32[]{:S(2)}) %collective-permute-start.18) | collective-permute-done | bytes 3104 | tf_op jit(solution)/shard_map/ppermute | solution.py:68
  91.2 4.1 %collective-permute-done.23.refs_3_ = bf16[32,3584]{1,0:T(8,128)(2,1)S(1)} collective-permute-done((bf16[32,3584]{1,0:T(8,128)(2,1)S(1)}, bf16[32,3584]{1,0:T(8,128)(2,1)S(1)}, u32[]{:S(2)}, u32[]{:S(2)}) %collective-permute-start.23) | collective-permute-done | bytes 229408 | tf_op jit(solution)/shard_map/ppermute | solution.py:447
  95.3 1.3 %shard_map.126 = (bf16[64,3584]{1,0:T(8,128)(2,1)}, bf16[64,384]{1,0:T(8,128)(2,1)}) custom-call(s32[1]{0:T(128)S(6)} %copy.12.level, bf16[64,3584]{1,0:T(8,128)(2,1)S(1)} %bitcast.16, f32[3,16,3584]{2,1,0:T(8,128)S(1)} %bitcast.13, bf16[96,3584]{1,0:T(8,128)(2,1)S(1)} %bitcast.18, bf16[3,96,384]{2,1,0:T(8,128)(2,1)S(1)} %copy-done.4, ...), custom_call_target="tpu_custom_call" | custom-call | flops 1 | bytes 1 | tf_op jit(solution)/shard_map/pallas_call | solution.py:352
  (22 shorter events, 0.2 us)
Async XLA Ops:
  0.6 18.5 %copy-start.5 = (f32[2,512]{1,0:T(2,128)S(1)}, f32[2,512]{1,0:T(2,128)}, u32[]{:S(2)}) copy-start(f32[2,512]{1,0:T(2,128)} %refs_2_.1) | copy-start | bytes 12292
  2.8 9.5 %collective-permute-start.2 = (bf16[16,3584]{1,0:T(8,128)(2,1)S(1)}, bf16[16,3584]{1,0:T(8,128)(2,1)S(1)}, u32[]{:S(2)}, u32[]{:S(2)}) collective-permute-start(bf16[16,3584]{1,0:T(8,128)(2,1)S(1)} %get-tuple-element.44.refs_0_), channel_id=1, source_target_pairs={{4,2},{5,3},{6,0},{7,1},{0,6},{1,7},{2,4},{3,5},{12,10},{13,11},{1... | collective-permute-start | bytes 344072 | tf_op jit(solution)/shard_map/ppermute | solution.py:385
  6.5 10.7 %collective-permute-start.1 = (bf16[16,3584]{1,0:T(8,128)(2,1)S(1)}, bf16[16,3584]{1,0:T(8,128)(2,1)S(1)}, u32[]{:S(2)}, u32[]{:S(2)}) collective-permute-start(bf16[16,3584]{1,0:T(8,128)(2,1)S(1)} %get-tuple-element.44.refs_0_), channel_id=1, source_target_pairs={{0,2},{1,3},{2,6},{3,7},{6,4},{7,5},{4,0},{5,1},{8,10},{9,11},{10,... | collective-permute-start | bytes 344072 | tf_op jit(solution)/shard_map/ppermute | solution.py:385
  6.5 10.8 %collective-permute-start = (bf16[16,3584]{1,0:T(8,128)(2,1)S(1)}, bf16[16,3584]{1,0:T(8,128)(2,1)S(1)}, u32[]{:S(2)}, u32[]{:S(2)}) collective-permute-start(bf16[16,3584]{1,0:T(8,128)(2,1)S(1)} %get-tuple-element.44.refs_0_), channel_id=1, source_target_pairs={{0,4},{1,5},{4,6},{5,7},{6,2},{7,3},{2,0},{3,1},{8,12},{9,13},{12,... | collective-permute-start | bytes 344072 | tf_op jit(solution)/shard_map/ppermute | solution.py:385
  9.4 21.5 %collective-permute-start.6 = (bf16[48,3584]{1,0:T(8,128)(2,1)S(1)}, bf16[48,3584]{1,0:T(8,128)(2,1)S(1)}, u32[]{:S(2)}, u32[]{:S(2)}) collective-permute-start(bf16[48,3584]{1,0:T(8,128)(2,1)S(1)} %get-tuple-element.45.refs_0_), channel_id=1, source_target_pairs={{0,2},{1,3},{2,6},{3,7},{6,4},{7,5},{4,0},{5,1},{8,10},{9,11},{10,... | collective-permute-start | bytes 1032200 | tf_op jit(solution)/shard_map/ppermute | solution.py:385
  9.4 21.5 %collective-permute-start.5 = (bf16[48,3584]{1,0:T(8,128)(2,1)S(1)}, bf16[48,3584]{1,0:T(8,128)(2,1)S(1)}, u32[]{:S(2)}, u32[]{:S(2)}) collective-permute-start(bf16[48,3584]{1,0:T(8,128)(2,1)S(1)} %get-tuple-element.45.refs_0_), channel_id=1, source_target_pairs={{0,4},{1,5},{4,6},{5,7},{6,2},{7,3},{2,0},{3,1},{8,12},{9,13},{12,... | collective-permute-start | bytes 1032200 | tf_op jit(solution)/shard_map/ppermute | solution.py:385
  17.2 1.6 %collective-permute-start.4 = (bf16[32,3584]{1,0:T(8,128)(2,1)S(1)}, bf16[32,3584]{1,0:T(8,128)(2,1)S(1)}, u32[]{:S(2)}, u32[]{:S(2)}) collective-permute-start(bf16[32,3584]{1,0:T(8,128)(2,1)S(1)} %pad_maximum_fusion.2), channel_id=1, source_target_pairs={{0,1},{1,0},{2,3},{3,2},{4,5},{5,4},{6,7},{7,6},{8,9},{9,8},{10,11... | collective-permute-start | bytes 688136 | tf_op jit(solution)/shard_map/ppermute | solution.py:62
  17.3 1.8 %collective-permute-start.3 = (bf16[32,3584]{1,0:T(8,128)(2,1)S(1)}, bf16[32,3584]{1,0:T(8,128)(2,1)S(1)}, u32[]{:S(2)}, u32[]{:S(2)}) collective-permute-start(bf16[32,3584]{1,0:T(8,128)(2,1)S(1)} %pad_maximum_fusion.1), channel_id=1, source_target_pairs={{0,1},{1,0},{2,3},{3,2},{4,5},{5,4},{6,7},{7,6},{8,9},{9,8},{10,11... | collective-permute-start | bytes 688136 | tf_op jit(solution)/shard_map/ppermute | solution.py:62
  19.1 20.8 %copy-start = (bf16[3584,3,512]{2,0,1:T(8,128)(2,1)S(1)}, bf16[3584,3,512]{2,0,1:T(8,128)(2,1)}, u32[]{:S(2)}) copy-start(bf16[3584,3,512]{2,0,1:T(8,128)(2,1)} %param.15) | copy-start | bytes 33030148
  24.3 10.7 %collective-permute-start.10 = (bf16[2,128,512]{2,1,0:T(8,128)(2,1)S(1)}, bf16[2,128,512]{2,1,0:T(8,128)(2,1)S(1)}, u32[]{:S(2)}, u32[]{:S(2)}) collective-permute-start(bf16[2,128,512]{2,1,0:T(8,128)(2,1)S(1)} %slice.8), channel_id=1, source_target_pairs={{0,16},{8,24},{1,17},{9,25},{2,18},{10,26},{3,19},{11,27},{4,20},{... | collective-permute-start | bytes 786440 | tf_op jit(solution)/shard_map/ppermute | solution.py:78
  25.9 9.4 %collective-permute-start.9 = (bf16[2,128,512]{2,1,0:T(8,128)(2,1)S(1)}, bf16[2,128,512]{2,1,0:T(8,128)(2,1)S(1)}, u32[]{:S(2)}, u32[]{:S(2)}) collective-permute-start(bf16[2,128,512]{2,1,0:T(8,128)(2,1)S(1)} %slice.8), channel_id=1, source_target_pairs={{0,8},{16,24},{1,9},{17,25},{2,10},{18,26},{3,11},{19,27},{4,12},{... | collective-permute-start | bytes 786440 | tf_op jit(solution)/shard_map/ppermute | solution.py:77
  31.0 8.9 %collective-permute-start.7 = (bf16[144,3584]{1,0:T(8,128)(2,1)S(1)}, bf16[144,3584]{1,0:T(8,128)(2,1)S(1)}, u32[]{:S(2)}, u32[]{:S(2)}) collective-permute-start(bf16[144,3584]{1,0:T(8,128)(2,1)S(1)} %pad_maximum_fusion), channel_id=1, source_target_pairs={{0,1},{1,0},{2,3},{3,2},{4,5},{5,4},{6,7},{7,6},{8,9},{9,8},{10,11... | collective-permute-start | bytes 3096584 | tf_op jit(solution)/shard_map/ppermute | solution.py:62
  31.1 12.2 %collective-permute-start.8 = (bf16[48,3584]{1,0:T(8,128)(2,1)S(1)}, bf16[48,3584]{1,0:T(8,128)(2,1)S(1)}, u32[]{:S(2)}, u32[]{:S(2)}) collective-permute-start(bf16[48,3584]{1,0:T(8,128)(2,1)S(1)} %broadcast_select_fusion), channel_id=1, source_target_pairs={{0,2},{1,3},{2,0},{3,1},{4,6},{5,7},{6,4},{7,5},{8,10},{9,11},{10,... | collective-permute-start | bytes 1032200 | tf_op jit(solution)/shard_map/ppermute | solution.py:385
  35.3 10.3 %collective-permute-start.11 = (bf16[2,128,512]{2,1,0:T(8,128)(2,1)S(1)}, bf16[2,128,512]{2,1,0:T(8,128)(2,1)S(1)}, u32[]{:S(2)}, u32[]{:S(2)}) collective-permute-start(bf16[2,128,512]{2,1,0:T(8,128)(2,1)S(1)} %collective-permute-done.10.refs_4_), channel_id=1, source_target_pairs={{24,16},{16,24},{25,17},{17,25},{26,18},{18,26},{27,19},{19,27},{2... | collective-permute-start | bytes 786440 | tf_op jit(solution)/shard_map/ppermute | solution.py:79
  43.3 5.8 %copy-start.6 = (s32[4,4]{1,0:T(4,128)S(1)}, s32[4,4]{1,0:T(4,128)}, u32[]{:S(2)}) copy-start(s32[4,4]{1,0:T(4,128)} %visible.3) | copy-start | bytes 196
  43.3 5.8 %copy-start.7 = (s32[4]{0:T(128)S(1)}, s32[4]{0:T(128)}, u32[]{:S(2)}) copy-start(s32[4]{0:T(128)} %counts.3) | copy-start | bytes 52
  45.6 1.7 %collective-permute-start.12 = (bf16[48,3584]{1,0:T(8,128)(2,1)S(1)}, bf16[48,3584]{1,0:T(8,128)(2,1)S(1)}, u32[]{:S(2)}, u32[]{:S(2)}) collective-permute-start(bf16[48,3584]{1,0:T(8,128)(2,1)S(1)} %collective-permute-done.8.refs_0_), channel_id=1, source_target_pairs={{0,1},{1,0},{2,3},{3,2},{4,5},{5,4},{6,7},{7,6},{8,9},{9,8},{10,11... | collective-permute-start | bytes 1032200 | tf_op jit(solution)/shard_map/ppermute | solution.py:62
  53.2 10.3 %collective-permute-start.13 = (bf16[96,3584]{1,0:T(8,128)(2,1)S(1)}, bf16[96,3584]{1,0:T(8,128)(2,1)S(1)}, u32[]{:S(2)}, u32[]{:S(2)}) collective-permute-start(bf16[96,3584]{1,0:T(8,128)(2,1)S(1)} %get-tuple-element.54), channel_id=1, source_target_pairs={{0,1},{1,0},{2,3},{3,2},{4,5},{5,4},{6,7},{7,6},{8,9},{9,8},{10,11... | collective-permute-start | bytes 2064392 | tf_op jit(solution)/shard_map/ppermute | solution.py:62
  53.4 2.3 %collective-permute-start.14 = (bf16[32,3584]{1,0:T(8,128)(2,1)S(1)}, bf16[32,3584]{1,0:T(8,128)(2,1)S(1)}, u32[]{:S(2)}, u32[]{:S(2)}) collective-permute-start(bf16[32,3584]{1,0:T(8,128)(2,1)S(1)} %get-tuple-element.59), channel_id=1, source_target_pairs={{0,1},{1,0},{2,3},{3,2},{4,5},{5,4},{6,7},{7,6},{8,9},{9,8},{10,11... | collective-permute-start | bytes 688136 | tf_op jit(solution)/shard_map/ppermute | solution.py:62
  55.8 7.7 %collective-permute-start.15 = (bf16[32,3584]{1,0:T(8,128)(2,1)S(1)}, bf16[32,3584]{1,0:T(8,128)(2,1)S(1)}, u32[]{:S(2)}, u32[]{:S(2)}) collective-permute-start(bf16[32,3584]{1,0:T(8,128)(2,1)S(1)} %shard_map.119), channel_id=1, source_target_pairs={{2,0},{3,1},{0,2},{1,3},{6,4},{7,5},{4,6},{5,7},{10,8},{11,9},{8,1... | collective-permute-start | bytes 688136 | tf_op jit(solution)/shard_map/ppermute | solution.py:428
  59.9 17.8 %copy-start.1 = (f32[16,3,3584]{2,0,1:T(8,128)S(1)}, f32[16,3,3584]{2,0,1:T(8,128)}, u32[]{:S(2)}) copy-start(f32[16,3,3584]{2,0,1:T(8,128)} %param.14) | copy-start | bytes 2064388
  59.9 17.7 %copy-start.2 = (bf16[1,64,3584]{2,1,0:T(8,128)(2,1)S(1)}, bf16[1,64,3584]{2,1,0:T(8,128)(2,1)}, u32[]{:S(2)}) copy-start(bf16[1,64,3584]{2,1,0:T(8,128)(2,1)} %param.10) | copy-start | bytes 1376260
  59.9 17.7 %copy-start.3 = (bf16[3584,96]{0,1:T(8,128)(2,1)S(1)}, bf16[3584,96]{0,1:T(8,128)(2,1)}, u32[]{:S(2)}) copy-start(bf16[3584,96]{0,1:T(8,128)(2,1)} %param.18) | copy-start | bytes 2064388
  59.9 18.1 %collective-permute-start.19 = (bf16[96,3584]{1,0:T(8,128)(2,1)S(1)}, bf16[96,3584]{1,0:T(8,128)(2,1)S(1)}, u32[]{:S(2)}, u32[]{:S(2)}) collective-permute-start(bf16[96,3584]{1,0:T(8,128)(2,1)S(1)} %get-tuple-element.68), channel_id=1, source_target_pairs={{0,1},{1,0},{2,3},{3,2},{4,5},{5,4},{6,7},{7,6},{8,9},{9,8},{10,11... | collective-permute-start | bytes 2064392 | tf_op jit(solution)/shard_map/ppermute | solution.py:62
  63.7 3.1 %collective-permute-start.20 = (bf16[32,3584]{1,0:T(8,128)(2,1)S(1)}, bf16[32,3584]{1,0:T(8,128)(2,1)S(1)}, u32[]{:S(2)}, u32[]{:S(2)}) collective-permute-start(bf16[32,3584]{1,0:T(8,128)(2,1)S(1)} %get-tuple-element.73), channel_id=1, source_target_pairs={{0,1},{1,0},{2,3},{3,2},{4,5},{5,4},{6,7},{7,6},{8,9},{9,8},{10,11... | collective-permute-start | bytes 688136 | tf_op jit(solution)/shard_map/ppermute | solution.py:62
  63.8 9.4 %collective-permute-start.16 = (bf16[32,3584]{1,0:T(8,128)(2,1)S(1)}, bf16[32,3584]{1,0:T(8,128)(2,1)S(1)}, u32[]{:S(2)}, u32[]{:S(2)}) collective-permute-start(bf16[32,3584]{1,0:T(8,128)(2,1)S(1)} %get-tuple-element.60), channel_id=1, source_target_pairs={{4,0},{5,1},{6,4},{7,5},{2,6},{3,7},{0,2},{1,3},{12,8},{13,9},{14,... | collective-permute-start | bytes 688136 | tf_op jit(solution)/shard_map/ppermute | solution.py:447
  64.1 13.5 %collective-permute-start.17 = (bf16[32,3584]{1,0:T(8,128)(2,1)S(1)}, bf16[32,3584]{1,0:T(8,128)(2,1)S(1)}, u32[]{:S(2)}, u32[]{:S(2)}) collective-permute-start(bf16[32,3584]{1,0:T(8,128)(2,1)S(1)} %get-tuple-element.61), channel_id=1, source_target_pairs={{2,0},{3,1},{6,2},{7,3},{4,6},{5,7},{0,4},{1,5},{10,8},{11,9},{14,... | collective-permute-start | bytes 688136 | tf_op jit(solution)/shard_map/ppermute | solution.py:447
  66.8 15.7 %collective-permute-start.21 = (bf16[32,3584]{1,0:T(8,128)(2,1)S(1)}, bf16[32,3584]{1,0:T(8,128)(2,1)S(1)}, u32[]{:S(2)}, u32[]{:S(2)}) collective-permute-start(bf16[32,3584]{1,0:T(8,128)(2,1)S(1)} %shard_map.124), channel_id=1, source_target_pairs={{2,0},{3,1},{0,2},{1,3},{6,4},{7,5},{4,6},{5,7},{10,8},{11,9},{8,1... | collective-permute-start | bytes 688136 | tf_op jit(solution)/shard_map/ppermute | solution.py:428
  77.7 17.6 %copy-start.4 = (bf16[3,96,384]{2,1,0:T(8,128)(2,1)S(1)}, bf16[3,96,384]{2,1,0:T(8,128)(2,1)}, u32[]{:S(2)}) copy-start(bf16[3,96,384]{2,1,0:T(8,128)(2,1)} %weight.1) | copy-start | bytes 663556
  82.7 12.5 %collective-permute-start.23 = (bf16[32,3584]{1,0:T(8,128)(2,1)S(1)}, bf16[32,3584]{1,0:T(8,128)(2,1)S(1)}, u32[]{:S(2)}, u32[]{:S(2)}) collective-permute-start(bf16[32,3584]{1,0:T(8,128)(2,1)S(1)} %get-tuple-element.77), channel_id=1, source_target_pairs={{2,0},{3,1},{6,2},{7,3},{4,6},{5,7},{0,4},{1,5},{10,8},{11,9},{14,... | collective-permute-start | bytes 688136 | tf_op jit(solution)/shard_map/ppermute | solution.py:447
  83.4 11.9 %collective-permute-start.22 = (bf16[32,3584]{1,0:T(8,128)(2,1)S(1)}, bf16[32,3584]{1,0:T(8,128)(2,1)S(1)}, u32[]{:S(2)}, u32[]{:S(2)}) collective-permute-start(bf16[32,3584]{1,0:T(8,128)(2,1)S(1)} %get-tuple-element.75), channel_id=1, source_target_pairs={{4,0},{5,1},{6,4},{7,5},{2,6},{3,7},{0,2},{1,3},{12,8},{13,9},{14,... | collective-permute-start | bytes 688136 | tf_op jit(solution)/shard_map/ppermute | solution.py:447
  84.8 6.4 %collective-permute-start.18 = (bf16[16,96]{1,0:T(8,128)(2,1)S(1)}, bf16[16,96]{1,0:T(8,128)(2,1)S(1)}, u32[]{:S(2)}, u32[]{:S(2)}) collective-permute-start(bf16[16,96]{1,0:T(8,128)(2,1)S(1)} %slice.7), channel_id=1, source_target_pairs={{0,8},{8,16},{16,24},{1,9},{9,17},{17,25},{2,10},{10,18},{18,26},{... | collective-permute-start | bytes 9224 | tf_op jit(solution)/shard_map/ppermute | solution.py:68
